TPU v7x, 512 devices: a whole 4x8x8 slice. The times are simulated.
512 devices in a mesh: blk: 16 (over y, z_hi), grp: 32 (over z_lo, x, core).
Axes of the slice: x: 4, y: 8, z: 8 (z_hi: 2, z_lo: 4; z = z_hi * 4 + z_lo), core: 2. Of those that a mesh axis runs over, the one named last changes fastest.
Arguments:
- images: bfloat16 [12288, 1152], P(('blk', 'grp')), may hold values from -0.19921875 to 0.19921875
- texts: bfloat16 [16384, 1152], P(('blk', 'grp')), may hold values from -0.19921875 to 0.19921875
- image_ids: int32 [12288], replicated, may hold values from 0 to 12287, each once
- text_ids: int32 [16384], replicated, may hold values from 0 to 12287
- log_scale: float32 [1], replicated, may hold values from 1.6 to 2.4
- bias: float32 [1], replicated, may hold values from -8 to -4
Outputs:
- image_grad: float32 [12288, 1152], P(('blk', 'grp'))
- text_grad: float32 [16384, 1152], P(('blk', 'grp'))
- loss: float32 [1], replicated
- scale_grad: float32 [1], replicated
- bias_grad: float32 [1], replicated
Inputs may be any that keep to these rules, and one draw needn't show every extreme that they name: `image_ids`: each pair id appears on exactly one image.
All inputs are finite; a program needn't handle non-finite values.
Results may differ from a plain program's by a relative error of at most 0.00075.
The roundings to bfloat16 on the way count: a program that leaves them out, or rounds other values in their place, can miss the bound.
Values may be sent and summed in bfloat16 or wider, within the bound.
No kernel may reach another device: no remote copies, remote signals or barrier semaphores. Data moves between devices by JAX's collectives and lax.ppermute only.
A program may use at most 64 MiB of HBM per device.

v0:
```python
import jax
import jax.numpy as jnp
from jax import lax
from jax.sharding import PartitionSpec as P


def from_behind(value, axis, steps):
    count = lax.axis_size(axis)
    pairs = [(source, (source + steps) % count) for source in range(count)]
    return lax.ppermute(value, axis, pairs)


def normalize(rows):
    values = rows.astype(jnp.float32)
    radius = jnp.sqrt(jnp.sum(values * values, -1, keepdims=True) + 1e-06)
    unit = values / radius
    return (unit, radius, unit.astype(jnp.bfloat16))


def unnormalize(unit, radius, grad):
    return (grad - unit * jnp.sum(unit * grad, -1, keepdims=True)) / radius


def pair_terms(left, left_ids, right, right_ids, scale, shift):
    dots = jnp.dot(left, right.T, preferred_element_type=jnp.float32)
    logits = scale * dots + shift
    sign = jnp.where(left_ids[:, None] == right_ids[None, :], 1.0, -1.0).astype(jnp.float32)
    margin = sign * logits
    objective = jnp.sum(jax.nn.softplus(-margin))
    slope = -sign * jax.nn.sigmoid(-margin)
    return (slope, objective, jnp.sum(slope * dots), jnp.sum(slope))


def body(images, texts, image_ids, text_ids, log_scale, bias):
    groups = lax.axis_size("blk")
    members = lax.axis_size("grp")
    group_at = lax.axis_index("blk")
    member_at = lax.axis_index("grp")
    img_rows = images.shape[0]
    txt_rows = texts.shape[0]
    width = images.shape[1]
    scale = jnp.exp(log_scale[0])
    shift = bias[0]
    ux, rx, uxb = normalize(images)
    uy, ry, uyb = normalize(texts)
    group = lax.all_gather(uxb, "grp", axis=0, tiled=True)
    group_rows = img_rows * members
    group_ids = lax.dynamic_slice_in_dim(image_ids, group_at * group_rows, group_rows)

    def visit_block(block, owner):
        count = block.shape[0]
        start = (owner * members + member_at) * txt_rows
        ids = lax.dynamic_slice_in_dim(text_ids, start, count)
        slope, obj, s_dot, s_slope = pair_terms(group, group_ids, block, ids, scale, shift)
        slopeb = slope.astype(jnp.bfloat16)
        tgrad = scale * jnp.dot(slopeb.T, group, preferred_element_type=jnp.float32)
        return (slopeb, tgrad, jnp.stack([obj, s_dot, s_slope]))

    slopes_init = jnp.zeros((group_rows, groups * txt_rows), jnp.bfloat16)
    seen_init = jnp.zeros((groups * txt_rows, width), jnp.bfloat16)
    stats_init = jnp.zeros((3,), jnp.float32)

    def step(turn, carry):
        block, accum, slopes, seen, stats = carry
        owner = (group_at - turn) % groups
        slopeb, tgrad, terms = visit_block(block, owner)
        slopes = lax.dynamic_update_slice_in_dim(slopes, slopeb, turn * txt_rows, 1)
        seen = lax.dynamic_update_slice_in_dim(seen, block, turn * txt_rows, 0)
        accum = from_behind(accum + tgrad, "blk", 1)
        block = from_behind(block, "blk", 1)
        return (block, accum, slopes, seen, stats + terms)

    init = (uyb, jnp.zeros((txt_rows, width), jnp.float32), slopes_init, seen_init, stats_init)
    _, text_accum, slopes, seen, stats = lax.fori_loop(0, groups, step, init)
    group_grad = scale * jnp.dot(slopes, seen, preferred_element_type=jnp.float32)
    image_part = lax.psum_scatter(group_grad, "grp", scatter_dimension=0, tiled=True)
    totals = lax.psum(stats, ("blk", "grp"))
    total_texts = txt_rows * groups * members
    image_grad = unnormalize(ux, rx, image_part)
    text_grad = unnormalize(uy, ry, text_accum)
    loss = (totals[0] / total_texts).reshape(1)
    scale_grad = (scale * totals[1] / total_texts).reshape(1)
    bias_grad = (totals[2] / total_texts).reshape(1)
    return (image_grad, text_grad, loss, scale_grad, bias_grad)


def solution(mesh):
    return jax.shard_map(
        body,
        mesh=mesh,
        in_specs=(P(("blk", "grp"), None), P(("blk", "grp"), None), P(), P(), P(), P()),
        out_specs=(P(("blk", "grp"), None), P(("blk", "grp"), None), P(), P(), P()),
        check_vma=False,
    )
```

profile of v0, /device:TPU:1, one launch (start us, length us, event | category | flops | bytes accessed | tf_op | source)
XLA Modules:
  0.0 598.9 jit_solution(1003122583829892207)
XLA Ops:
  13.2 66.3 %all-gather.2.cloned.1.call-done = bf16[768,1152]{1,0:T(8,128)(2,1)} async-done(((bf16[24,1152]{1,0:T(8,128)(2,1)}), bf16[768,1152]{1,0:T(8,128)(2,1)}) %all-gather.2.cloned.1.call-update) | async-done | bytes 1769488 | tf_op jit(solution)/shard_map/all_gather | solution.py:46
  81.3 329.9 %while.24 = (s32[]{:T(128)}, bf16[32,1152]{1,0:T(8,128)(2,1)S(1)}, f32[32,1152]{1,0:T(8,128)S(1)}, bf16[768,512]{0,1:T(8,128)(2,1)}, bf16[512,1152]{1,0:T(8,128)...) while((s32[]{:T(128)}, bf16[32,1152]{1,0:T(8,128)(2,1)S(1)}, ...), condition=%wide.region_6.7_spmd.clone, body=%wide.region_2.6_spmd.clone.sunk | while | flops 114303008 | bytes 5442760 | solution.py:74
  81.3 6.1 %collective-permute-start = (bf16[32,1152]{1,0:T(8,128)(2,1)S(1)}, bf16[32,1152]{1,0:T(8,128)(2,1)S(1)}, u32[]{:S(2)}, u32[]{:S(2)}) collective-permute-start(bf16[32,1152]{1,0:T(8,128)(2,1)S(1)} %copy.20), channel_id=1, source_target_pairs={{0,32},{32,64},{64,96},{96,128},{128,160},{160,192},{192,224},{224... | collective-permute-start | bytes 221192 | tf_op jit(solution)/shard_map/while/body/eval_jaxpr/ppermute | solution.py:10
  98.7 7.1 %collective-permute-done.1 = f32[32,1152]{1,0:T(8,128)S(1)} collective-permute-done((f32[32,1152]{1,0:T(8,128)S(1)}, f32[32,1152]{1,0:T(8,128)S(1)}, u32[]{:S(2)}, u32[]{:S(2)}) %collective-permute-start.1) | collective-permute-done | bytes 147488 | tf_op jit(solution)/shard_map/while/body/eval_jaxpr/ppermute | solution.py:10
  111.6 7.0 %collective-permute-start.1 = (f32[32,1152]{1,0:T(8,128)S(1)}, f32[32,1152]{1,0:T(8,128)S(1)}, u32[]{:S(2)}, u32[]{:S(2)}) collective-permute-start(f32[32,1152]{1,0:T(8,128)S(1)} %fusion.28), channel_id=1, source_target_pairs={{0,32},{32,64},{64,96},{96,128},{128,160},{160,192},{192,224},{224... | collective-permute-start | bytes 442376 | tf_op jit(solution)/shard_map/while/body/eval_jaxpr/ppermute | solution.py:10
  139.5 5.3 collective-permute-done.1
  150.6 6.8 %collective-permute-start.1 = (f32[32,1152]{1,0:T(8,128)S(1)}, f32[32,1152]{1,0:T(8,128)S(1)}, u32[]{:S(2)}, u32[]{:S(2)}) collective-permute-start(f32[32,1152]{1,0:T(8,128)S(1)} %fusion.28), channel_id=1, source_target_pairs={{0,32},{32,64},{64,96},{96,128},{128,160},{160,192},{192,224},{224... | collective-permute-start | bytes 442376 | tf_op jit(solution)/shard_map/while/body/eval_jaxpr/ppermute | solution.py:10
  161.0 4.9 collective-permute-done.1
  179.6 7.1 %collective-permute-done.1 = f32[32,1152]{1,0:T(8,128)S(1)} collective-permute-done((f32[32,1152]{1,0:T(8,128)S(1)}, f32[32,1152]{1,0:T(8,128)S(1)}, u32[]{:S(2)}, u32[]{:S(2)}) %collective-permute-start.1) | collective-permute-done | bytes 147488 | tf_op jit(solution)/shard_map/while/body/eval_jaxpr/ppermute | solution.py:10
  200.5 6.2 %collective-permute-done.1 = f32[32,1152]{1,0:T(8,128)S(1)} collective-permute-done((f32[32,1152]{1,0:T(8,128)S(1)}, f32[32,1152]{1,0:T(8,128)S(1)}, u32[]{:S(2)}, u32[]{:S(2)}) %collective-permute-start.1) | collective-permute-done | bytes 147488 | tf_op jit(solution)/shard_map/while/body/eval_jaxpr/ppermute | solution.py:10
  212.4 8.0 %collective-permute-start.1 = (f32[32,1152]{1,0:T(8,128)S(1)}, f32[32,1152]{1,0:T(8,128)S(1)}, u32[]{:S(2)}, u32[]{:S(2)}) collective-permute-start(f32[32,1152]{1,0:T(8,128)S(1)} %fusion.28), channel_id=1, source_target_pairs={{0,32},{32,64},{64,96},{96,128},{128,160},{160,192},{192,224},{224... | collective-permute-start | bytes 442376 | tf_op jit(solution)/shard_map/while/body/eval_jaxpr/ppermute | solution.py:10
  234.1 8.7 %collective-permute-start.1 = (f32[32,1152]{1,0:T(8,128)S(1)}, f32[32,1152]{1,0:T(8,128)S(1)}, u32[]{:S(2)}, u32[]{:S(2)}) collective-permute-start(f32[32,1152]{1,0:T(8,128)S(1)} %fusion.28), channel_id=1, source_target_pairs={{0,32},{32,64},{64,96},{96,128},{128,160},{160,192},{192,224},{224... | collective-permute-start | bytes 442376 | tf_op jit(solution)/shard_map/while/body/eval_jaxpr/ppermute | solution.py:10
  247.5 5.2 collective-permute-start
  256.5 6.3 %collective-permute-start.1 = (f32[32,1152]{1,0:T(8,128)S(1)}, f32[32,1152]{1,0:T(8,128)S(1)}, u32[]{:S(2)}, u32[]{:S(2)}) collective-permute-start(f32[32,1152]{1,0:T(8,128)S(1)} %fusion.28), channel_id=1, source_target_pairs={{0,32},{32,64},{64,96},{96,128},{128,160},{160,192},{192,224},{224... | collective-permute-start | bytes 442376 | tf_op jit(solution)/shard_map/while/body/eval_jaxpr/ppermute | solution.py:10
  276.5 8.4 %collective-permute-start.1 = (f32[32,1152]{1,0:T(8,128)S(1)}, f32[32,1152]{1,0:T(8,128)S(1)}, u32[]{:S(2)}, u32[]{:S(2)}) collective-permute-start(f32[32,1152]{1,0:T(8,128)S(1)} %fusion.28), channel_id=1, source_target_pairs={{0,32},{32,64},{64,96},{96,128},{128,160},{160,192},{192,224},{224... | collective-permute-start | bytes 442376 | tf_op jit(solution)/shard_map/while/body/eval_jaxpr/ppermute | solution.py:10
  289.8 4.8 collective-permute-start
  323.8 5.0 collective-permute-done.1
  341.8 6.3 %collective-permute-done.1 = f32[32,1152]{1,0:T(8,128)S(1)} collective-permute-done((f32[32,1152]{1,0:T(8,128)S(1)}, f32[32,1152]{1,0:T(8,128)S(1)}, u32[]{:S(2)}, u32[]{:S(2)}) %collective-permute-start.1) | collective-permute-done | bytes 147488 | tf_op jit(solution)/shard_map/while/body/eval_jaxpr/ppermute | solution.py:10
  361.2 7.4 %collective-permute-done.1 = f32[32,1152]{1,0:T(8,128)S(1)} collective-permute-done((f32[32,1152]{1,0:T(8,128)S(1)}, f32[32,1152]{1,0:T(8,128)S(1)}, u32[]{:S(2)}, u32[]{:S(2)}) %collective-permute-start.1) | collective-permute-done | bytes 147488 | tf_op jit(solution)/shard_map/while/body/eval_jaxpr/ppermute | solution.py:10
  374.3 4.7 collective-permute-start.1
  382.5 8.0 %collective-permute-done.1 = f32[32,1152]{1,0:T(8,128)S(1)} collective-permute-done((f32[32,1152]{1,0:T(8,128)S(1)}, f32[32,1152]{1,0:T(8,128)S(1)}, u32[]{:S(2)}, u32[]{:S(2)}) %collective-permute-start.1) | collective-permute-done | bytes 147488 | tf_op jit(solution)/shard_map/while/body/eval_jaxpr/ppermute | solution.py:10
  402.3 8.9 %collective-permute-done.1 = f32[32,1152]{1,0:T(8,128)S(1)} collective-permute-done((f32[32,1152]{1,0:T(8,128)S(1)}, f32[32,1152]{1,0:T(8,128)S(1)}, u32[]{:S(2)}, u32[]{:S(2)}) %collective-permute-start.1) | collective-permute-done | bytes 147488 | tf_op jit(solution)/shard_map/while/body/eval_jaxpr/ppermute | solution.py:10
  415.3 120.7 %psum.7 = f32[3]{0:T(128)S(1)} all-reduce(f32[3]{0:T(128)S(1)} %get-tuple-element.320), channel_id=1, replica_groups=mesh['blk'=16,'grp'=32] {'blk','grp'}, use_global_device_ids=true, to_apply=%region_10.11 | all-reduce | flops 3 | bytes 24 | tf_op jit(solution)/shard_map/psum | solution.py:77
  539.6 46.4 %reduce-scatter.5.cloned.1.call-done = f32[24,1152]{1,0:T(8,128)} async-done(((f32[768,1152]{1,0:T(8,128)}), f32[24,1152]{1,0:T(8,128)}) %reduce-scatter.5.cloned.1.call-update) | async-done | bytes 110608
  (183 shorter events, 212.3 us)
Async XLA Ops:
  7.2 72.3 %all-gather.2.cloned.1.call-start = ((), (), s32[]{:S(2)}) async-start(), calls=%async_computation.1 | async-start | bytes 1824768 | tf_op jit(solution)/shard_map/all_gather | solution.py:46
  9.7 576.2 %reduce-scatter.5.cloned.1.call-start = ((), (), s32[]{:S(2)}) async-start(), calls=%async_computation.2 | async-start | bytes 3649536
  81.3 17.5 %collective-permute-start = (bf16[32,1152]{1,0:T(8,128)(2,1)S(1)}, bf16[32,1152]{1,0:T(8,128)(2,1)S(1)}, u32[]{:S(2)}, u32[]{:S(2)}) collective-permute-start(bf16[32,1152]{1,0:T(8,128)(2,1)S(1)} %copy.20), channel_id=1, source_target_pairs={{0,32},{32,64},{64,96},{96,128},{128,160},{160,192},{192,224},{224... | collective-permute-start | bytes 221192 | tf_op jit(solution)/shard_map/while/body/eval_jaxpr/ppermute | solution.py:10
  91.1 14.7 %collective-permute-start.1 = (f32[32,1152]{1,0:T(8,128)S(1)}, f32[32,1152]{1,0:T(8,128)S(1)}, u32[]{:S(2)}, u32[]{:S(2)}) collective-permute-start(f32[32,1152]{1,0:T(8,128)S(1)} %fusion.28), channel_id=1, source_target_pairs={{0,32},{32,64},{64,96},{96,128},{128,160},{160,192},{192,224},{224... | collective-permute-start | bytes 442376 | tf_op jit(solution)/shard_map/while/body/eval_jaxpr/ppermute | solution.py:10
  105.9 16.2 %collective-permute-start = (bf16[32,1152]{1,0:T(8,128)(2,1)S(1)}, bf16[32,1152]{1,0:T(8,128)(2,1)S(1)}, u32[]{:S(2)}, u32[]{:S(2)}) collective-permute-start(bf16[32,1152]{1,0:T(8,128)(2,1)S(1)} %copy.20), channel_id=1, source_target_pairs={{0,32},{32,64},{64,96},{96,128},{128,160},{160,192},{192,224},{224... | collective-permute-start | bytes 221192 | tf_op jit(solution)/shard_map/while/body/eval_jaxpr/ppermute | solution.py:10
  124.8 14.8 %collective-permute-start = (bf16[32,1152]{1,0:T(8,128)(2,1)S(1)}, bf16[32,1152]{1,0:T(8,128)(2,1)S(1)}, u32[]{:S(2)}, u32[]{:S(2)}) collective-permute-start(bf16[32,1152]{1,0:T(8,128)(2,1)S(1)} %copy.20), channel_id=1, source_target_pairs={{0,32},{32,64},{64,96},{96,128},{128,160},{160,192},{192,224},{224... | collective-permute-start | bytes 221192 | tf_op jit(solution)/shard_map/while/body/eval_jaxpr/ppermute | solution.py:10
  144.9 16.1 %collective-permute-start = (bf16[32,1152]{1,0:T(8,128)(2,1)S(1)}, bf16[32,1152]{1,0:T(8,128)(2,1)S(1)}, u32[]{:S(2)}, u32[]{:S(2)}) collective-permute-start(bf16[32,1152]{1,0:T(8,128)(2,1)S(1)} %copy.20), channel_id=1, source_target_pairs={{0,32},{32,64},{64,96},{96,128},{128,160},{160,192},{192,224},{224... | collective-permute-start | bytes 221192 | tf_op jit(solution)/shard_map/while/body/eval_jaxpr/ppermute | solution.py:10
  150.6 15.3 %collective-permute-start.1 = (f32[32,1152]{1,0:T(8,128)S(1)}, f32[32,1152]{1,0:T(8,128)S(1)}, u32[]{:S(2)}, u32[]{:S(2)}) collective-permute-start(f32[32,1152]{1,0:T(8,128)S(1)} %fusion.28), channel_id=1, source_target_pairs={{0,32},{32,64},{64,96},{96,128},{128,160},{160,192},{192,224},{224... | collective-permute-start | bytes 442376 | tf_op jit(solution)/shard_map/while/body/eval_jaxpr/ppermute | solution.py:10
  165.9 13.7 %collective-permute-start = (bf16[32,1152]{1,0:T(8,128)(2,1)S(1)}, bf16[32,1152]{1,0:T(8,128)(2,1)S(1)}, u32[]{:S(2)}, u32[]{:S(2)}) collective-permute-start(bf16[32,1152]{1,0:T(8,128)(2,1)S(1)} %copy.20), channel_id=1, source_target_pairs={{0,32},{32,64},{64,96},{96,128},{128,160},{160,192},{192,224},{224... | collective-permute-start | bytes 221192 | tf_op jit(solution)/shard_map/while/body/eval_jaxpr/ppermute | solution.py:10
  171.6 15.1 %collective-permute-start.1 = (f32[32,1152]{1,0:T(8,128)S(1)}, f32[32,1152]{1,0:T(8,128)S(1)}, u32[]{:S(2)}, u32[]{:S(2)}) collective-permute-start(f32[32,1152]{1,0:T(8,128)S(1)} %fusion.28), channel_id=1, source_target_pairs={{0,32},{32,64},{64,96},{96,128},{128,160},{160,192},{192,224},{224... | collective-permute-start | bytes 442376 | tf_op jit(solution)/shard_map/while/body/eval_jaxpr/ppermute | solution.py:10
  186.7 13.8 %collective-permute-start = (bf16[32,1152]{1,0:T(8,128)(2,1)S(1)}, bf16[32,1152]{1,0:T(8,128)(2,1)S(1)}, u32[]{:S(2)}, u32[]{:S(2)}) collective-permute-start(bf16[32,1152]{1,0:T(8,128)(2,1)S(1)} %copy.20), channel_id=1, source_target_pairs={{0,32},{32,64},{64,96},{96,128},{128,160},{160,192},{192,224},{224... | collective-permute-start | bytes 221192 | tf_op jit(solution)/shard_map/while/body/eval_jaxpr/ppermute | solution.py:10
  192.4 14.3 %collective-permute-start.1 = (f32[32,1152]{1,0:T(8,128)S(1)}, f32[32,1152]{1,0:T(8,128)S(1)}, u32[]{:S(2)}, u32[]{:S(2)}) collective-permute-start(f32[32,1152]{1,0:T(8,128)S(1)} %fusion.28), channel_id=1, source_target_pairs={{0,32},{32,64},{64,96},{96,128},{128,160},{160,192},{192,224},{224... | collective-permute-start | bytes 442376 | tf_op jit(solution)/shard_map/while/body/eval_jaxpr/ppermute | solution.py:10
  206.7 17.2 %collective-permute-start = (bf16[32,1152]{1,0:T(8,128)(2,1)S(1)}, bf16[32,1152]{1,0:T(8,128)(2,1)S(1)}, u32[]{:S(2)}, u32[]{:S(2)}) collective-permute-start(bf16[32,1152]{1,0:T(8,128)(2,1)S(1)} %copy.20), channel_id=1, source_target_pairs={{0,32},{32,64},{64,96},{96,128},{128,160},{160,192},{192,224},{224... | collective-permute-start | bytes 221192 | tf_op jit(solution)/shard_map/while/body/eval_jaxpr/ppermute | solution.py:10
  212.4 13.7 %collective-permute-start.1 = (f32[32,1152]{1,0:T(8,128)S(1)}, f32[32,1152]{1,0:T(8,128)S(1)}, u32[]{:S(2)}, u32[]{:S(2)}) collective-permute-start(f32[32,1152]{1,0:T(8,128)S(1)} %fusion.28), channel_id=1, source_target_pairs={{0,32},{32,64},{64,96},{96,128},{128,160},{160,192},{192,224},{224... | collective-permute-start | bytes 442376 | tf_op jit(solution)/shard_map/while/body/eval_jaxpr/ppermute | solution.py:10
  226.1 20.2 %collective-permute-start = (bf16[32,1152]{1,0:T(8,128)(2,1)S(1)}, bf16[32,1152]{1,0:T(8,128)(2,1)S(1)}, u32[]{:S(2)}, u32[]{:S(2)}) collective-permute-start(bf16[32,1152]{1,0:T(8,128)(2,1)S(1)} %copy.20), channel_id=1, source_target_pairs={{0,32},{32,64},{64,96},{96,128},{128,160},{160,192},{192,224},{224... | collective-permute-start | bytes 221192 | tf_op jit(solution)/shard_map/while/body/eval_jaxpr/ppermute | solution.py:10
  234.1 13.4 %collective-permute-start.1 = (f32[32,1152]{1,0:T(8,128)S(1)}, f32[32,1152]{1,0:T(8,128)S(1)}, u32[]{:S(2)}, u32[]{:S(2)}) collective-permute-start(f32[32,1152]{1,0:T(8,128)S(1)} %fusion.28), channel_id=1, source_target_pairs={{0,32},{32,64},{64,96},{96,128},{128,160},{160,192},{192,224},{224... | collective-permute-start | bytes 442376 | tf_op jit(solution)/shard_map/while/body/eval_jaxpr/ppermute | solution.py:10
  247.5 18.8 %collective-permute-start = (bf16[32,1152]{1,0:T(8,128)(2,1)S(1)}, bf16[32,1152]{1,0:T(8,128)(2,1)S(1)}, u32[]{:S(2)}, u32[]{:S(2)}) collective-permute-start(bf16[32,1152]{1,0:T(8,128)(2,1)S(1)} %copy.20), channel_id=1, source_target_pairs={{0,32},{32,64},{64,96},{96,128},{128,160},{160,192},{192,224},{224... | collective-permute-start | bytes 221192 | tf_op jit(solution)/shard_map/while/body/eval_jaxpr/ppermute | solution.py:10
  269.0 19.4 %collective-permute-start = (bf16[32,1152]{1,0:T(8,128)(2,1)S(1)}, bf16[32,1152]{1,0:T(8,128)(2,1)S(1)}, u32[]{:S(2)}, u32[]{:S(2)}) collective-permute-start(bf16[32,1152]{1,0:T(8,128)(2,1)S(1)} %copy.20), channel_id=1, source_target_pairs={{0,32},{32,64},{64,96},{96,128},{128,160},{160,192},{192,224},{224... | collective-permute-start | bytes 221192 | tf_op jit(solution)/shard_map/while/body/eval_jaxpr/ppermute | solution.py:10
  289.8 16.3 %collective-permute-start = (bf16[32,1152]{1,0:T(8,128)(2,1)S(1)}, bf16[32,1152]{1,0:T(8,128)(2,1)S(1)}, u32[]{:S(2)}, u32[]{:S(2)}) collective-permute-start(bf16[32,1152]{1,0:T(8,128)(2,1)S(1)} %copy.20), channel_id=1, source_target_pairs={{0,32},{32,64},{64,96},{96,128},{128,160},{160,192},{192,224},{224... | collective-permute-start | bytes 221192 | tf_op jit(solution)/shard_map/while/body/eval_jaxpr/ppermute | solution.py:10
  310.4 13.4 %collective-permute-start = (bf16[32,1152]{1,0:T(8,128)(2,1)S(1)}, bf16[32,1152]{1,0:T(8,128)(2,1)S(1)}, u32[]{:S(2)}, u32[]{:S(2)}) collective-permute-start(bf16[32,1152]{1,0:T(8,128)(2,1)S(1)} %copy.20), channel_id=1, source_target_pairs={{0,32},{32,64},{64,96},{96,128},{128,160},{160,192},{192,224},{224... | collective-permute-start | bytes 221192 | tf_op jit(solution)/shard_map/while/body/eval_jaxpr/ppermute | solution.py:10
  353.8 14.8 %collective-permute-start.1 = (f32[32,1152]{1,0:T(8,128)S(1)}, f32[32,1152]{1,0:T(8,128)S(1)}, u32[]{:S(2)}, u32[]{:S(2)}) collective-permute-start(f32[32,1152]{1,0:T(8,128)S(1)} %fusion.28), channel_id=1, source_target_pairs={{0,32},{32,64},{64,96},{96,128},{128,160},{160,192},{192,224},{224... | collective-permute-start | bytes 442376 | tf_op jit(solution)/shard_map/while/body/eval_jaxpr/ppermute | solution.py:10
  368.6 13.9 %collective-permute-start = (bf16[32,1152]{1,0:T(8,128)(2,1)S(1)}, bf16[32,1152]{1,0:T(8,128)(2,1)S(1)}, u32[]{:S(2)}, u32[]{:S(2)}) collective-permute-start(bf16[32,1152]{1,0:T(8,128)(2,1)S(1)} %copy.20), channel_id=1, source_target_pairs={{0,32},{32,64},{64,96},{96,128},{128,160},{160,192},{192,224},{224... | collective-permute-start | bytes 221192 | tf_op jit(solution)/shard_map/while/body/eval_jaxpr/ppermute | solution.py:10
  374.3 16.2 %collective-permute-start.1 = (f32[32,1152]{1,0:T(8,128)S(1)}, f32[32,1152]{1,0:T(8,128)S(1)}, u32[]{:S(2)}, u32[]{:S(2)}) collective-permute-start(f32[32,1152]{1,0:T(8,128)S(1)} %fusion.28), channel_id=1, source_target_pairs={{0,32},{32,64},{64,96},{96,128},{128,160},{160,192},{192,224},{224... | collective-permute-start | bytes 442376 | tf_op jit(solution)/shard_map/while/body/eval_jaxpr/ppermute | solution.py:10
  396.2 15.0 %collective-permute-start.1 = (f32[32,1152]{1,0:T(8,128)S(1)}, f32[32,1152]{1,0:T(8,128)S(1)}, u32[]{:S(2)}, u32[]{:S(2)}) collective-permute-start(f32[32,1152]{1,0:T(8,128)S(1)} %fusion.28), channel_id=1, source_target_pairs={{0,32},{32,64},{64,96},{96,128},{128,160},{160,192},{192,224},{224... | collective-permute-start | bytes 442376 | tf_op jit(solution)/shard_map/while/body/eval_jaxpr/ppermute | solution.py:10
  (13 other events, 422.5 us)
Sparse Core Ops, SparseCore 0:
  10.7 68.7 all-gather.1
  415.4 170.4 reduce-scatter.4
where the time goes:
time: 606 us; the launch traced here: 599 us
  waiting for transfers between devices  194 us (32%)
  starting transfers between devices  131 us (22%)
  blocking collectives  121 us (20%)
  other arithmetic  63.7 us (11%)
  matrix products  52.1 us (9%)
  between operations  20.1 us (3%)
  local copies, waits for them, and re-layouts  15.7 us (3%)
    ppermute x32, starting transfers between devices, from_behind(): return lax.ppermute(value, axis, pairs)  131 us
    psum x1, blocking collectives, body(): totals = lax.psum(stats, ('blk', 'grp'))  121 us
    ppermute x32, waiting for transfers between devices, from_behind(): return lax.ppermute(value, axis, pairs)  81.5 us
    all_gather x1, waiting for transfers between devices, body(): group = lax.all_gather(uxb, 'grp', axis=0, tiled=True)  66.3 us
    unnamed x3, waiting for transfers between devices  46.4 us
    add x16, other arithmetic, step(): return (block, accum, slopes, seen, stats + terms)  31.6 us
    dot_general x16, matrix products, pair_terms(): dots = jnp.dot(left, right.T, preferred_element_type=jnp.float32)  30.3 us
    reduce_sum x16, other arithmetic, pair_terms(): objective = jnp.sum(jax.nn.softplus(-margin))  23.9 us
  transfers between devices with their start and end apart: 34, of which 19 were waited for; matrix products, arithmetic and copies ran while one was open for 20% of the time, Pallas kernels for 0%

commit v1 on v0

v1 whole, which is shorter than its diff:
```python
import jax
import jax.numpy as jnp
from jax import lax
from jax.sharding import Mesh, PartitionSpec as P

AXES = ("y", "zh", "zl", "x", "core")
SIZES = (8, 2, 4, 4, 2)
Z = ("zh", "zl")


def normalize(rows):
    values = rows.astype(jnp.float32)
    radius = jnp.sqrt(jnp.sum(values * values, -1, keepdims=True) + 1e-06)
    unit = values / radius
    return (unit, radius, unit.astype(jnp.bfloat16))


def unnormalize(unit, radius, grad):
    return (grad - unit * jnp.sum(unit * grad, -1, keepdims=True)) / radius


def swap(value, axis):
    return lax.all_to_all(value, axis, 0, 0, tiled=False)


def spread(block, axis):
    count = lax.axis_size(axis)
    return swap(jnp.broadcast_to(block[None], (count,) + block.shape), axis)


def body(images, texts, image_ids, text_ids, log_scale, bias):
    width = images.shape[1]
    img_rows = images.shape[0]
    txt_rows = texts.shape[0]
    y, x, core = (lax.axis_index(a) for a in ("y", "x", "core"))
    z = lax.axis_index(Z)
    scale = jnp.exp(log_scale[0])
    shift = bias[0]
    uy, ry, uyb = normalize(texts)
    ux, rx, uxb = normalize(images)

    cols = lax.all_gather(uyb, Z + ("core",), axis=0, tiled=True)
    cols = cols.reshape(8, 2, txt_rows, width).transpose(1, 0, 2, 3).reshape(-1, width)
    rows = spread(uxb, "y").reshape(-1, width)
    rows = spread(rows, "x").reshape(-1, width)

    col_ids = text_ids.reshape(8, 8, 4, 2, txt_rows)
    col_ids = lax.dynamic_index_in_dim(col_ids, y, 0, keepdims=False)
    col_ids = lax.dynamic_index_in_dim(col_ids, x, 1, keepdims=False)
    col_ids = col_ids.transpose(1, 0, 2).reshape(-1)
    row_ids = image_ids.reshape(8, 8, 4, 2, img_rows)
    row_ids = lax.dynamic_index_in_dim(row_ids, z, 1, keepdims=False)
    row_ids = lax.dynamic_index_in_dim(row_ids, core, 2, keepdims=False)
    row_ids = row_ids.transpose(1, 0, 2).reshape(-1)

    dots = jnp.dot(rows, cols.T, preferred_element_type=jnp.float32)
    logits = scale * dots + shift
    match = row_ids[:, None] == col_ids[None, :]
    against = jnp.where(match, -logits, logits)
    decay = jnp.exp(-jnp.abs(against))
    objective = jnp.sum(jnp.maximum(against, 0.0) + jnp.log1p(decay))
    weight = jnp.where(against >= 0.0, 1.0, decay) / (1.0 + decay)
    slope = jnp.where(match, -weight, weight)
    stats = jnp.stack([objective, jnp.sum(slope * dots), jnp.sum(slope)])
    slopeb = slope.astype(jnp.bfloat16)

    dcols = jnp.dot(slopeb.T, rows, preferred_element_type=jnp.float32)
    dcols = jnp.sum(swap(dcols.reshape(2, -1, width), "core"), 0)
    text_accum = lax.psum_scatter(dcols, Z, scatter_dimension=0, tiled=True)

    drows = jnp.dot(slopeb, cols, preferred_element_type=jnp.float32)
    drows = (drows * 64.0).astype(jnp.float16).reshape(4, -1, width)
    drows = jnp.sum(swap(drows, "x").astype(jnp.float32), 0)
    drows = (drows * 0.25).astype(jnp.float16).reshape(8, -1, width)
    image_accum = jnp.sum(swap(drows, "y").astype(jnp.float32), 0) * 0.0625

    for axis in ("core", Z, "x", "y"):
        stats = lax.psum(stats, axis)
    total_texts = txt_rows * 512
    image_grad = unnormalize(ux, rx, scale * image_accum)
    text_grad = unnormalize(uy, ry, scale * text_accum)
    loss = (stats[0] / total_texts).reshape(1)
    scale_grad = (scale * stats[1] / total_texts).reshape(1)
    bias_grad = (stats[2] / total_texts).reshape(1)
    return (image_grad, text_grad, loss, scale_grad, bias_grad)


def solution(mesh):
    fine = Mesh(mesh.devices.reshape(SIZES), AXES)
    split = P(AXES, None)
    return jax.shard_map(
        body,
        mesh=fine,
        in_specs=(split, split, P(), P(), P(), P()),
        out_specs=(split, split, P(), P(), P()),
        check_vma=False,
    )
```

time: 606 us -> 182 us (0.30)
  the two profiles are of different devices: /device:TPU:1 before, /device:TPU:2 now
where the time goes in v1:
time: 182 us; the launch traced here: 181 us
  blocking collectives  73.6 us (40%)
  waiting for transfers between devices  36.9 us (20%)
  between operations  20.9 us (11%)
  starting transfers between devices  19.4 us (11%)
  other arithmetic  16.8 us (9%)
  matrix products  9.69 us (5%)
  local copies, waits for them, and re-layouts  4.23 us (2%)
    psum x4, blocking collectives, body(): stats = lax.psum(stats, axis)  50.9 us
    all_to_all x1, blocking collectives, swap(): return lax.all_to_all(value, axis, 0, 0, tiled=False)  22.6 us
    all_to_all x4, waiting for transfers between devices, swap(): return lax.all_to_all(value, axis, 0, 0, tiled=False)  22.3 us
    all_to_all x4, starting transfers between devices, swap(): return lax.all_to_all(value, axis, 0, 0, tiled=False)  19.4 us
    all_gather x1, waiting for transfers between devices, body(): cols = lax.all_gather(uyb, Z + ('core',), axis=0, tiled=True)  14.6 us
    dot_general x1, matrix products, body(): drows = jnp.dot(slopeb, cols, preferred_element_type=jnp.float32)  4.29 us
  transfers between devices with their start and end apart: 6, of which 3 were waited for; matrix products, arithmetic and copies ran while one was open for 11% of the time, Pallas kernels for 0%

profile of v1, /device:TPU:2, one launch (start us, length us, event | category | flops | bytes accessed | tf_op | source)
XLA Modules:
  0.0 181.5 jit_solution(8140245075526525814)
XLA Ops:
  8.2 1.6 fusion.6
  11.8 22.6 %all_to_all.25 = bf16[8,24,1152]{2,1,0:T(8,128)(2,1)S(1)} all-to-all(bf16[8,24,1152]{2,1,0:T(8,128)(2,1)S(1)} %broadcast_in_dim.12), channel_id=1, replica_groups=mesh['y'=8,'zh'=2,'zl'=4,'x'=4,'core'=2] {'y'}, dimensions={0} | all-to-all | bytes 884736 | tf_op jit(solution)/shard_map/all_to_all | solution.py:23
  34.4 1.3 broadcast_in_dim.25
  35.7 5.0 %all-to-all-start.1 = ((bf16[4,192,1152]{2,1,0:T(8,128)(2,1)}), bf16[4,192,1152]{2,1,0:T(8,128)(2,1)S(1)}, u32[]{:S(2)}, u32[]{:S(2)}) async-start(bf16[4,192,1152]{2,1,0:T(8,128)(2,1)} %broadcast_in_dim.25), calls=%async_computation.1 | async-start | bytes 3538944 | tf_op jit(solution)/shard_map/all_to_all | solution.py:23
  43.0 14.6 %all-gather.2.cloned.1.call-done = bf16[512,1152]{1,0:T(8,128)(2,1)} async-done(((bf16[32,1152]{1,0:T(8,128)(2,1)}), bf16[512,1152]{1,0:T(8,128)(2,1)}) %all-gather.2.cloned.1.call-update) | async-done | bytes 1179664 | tf_op jit(solution)/shard_map/all_gather | solution.py:42
  57.6 1.4 copy.17
  58.9 1.2 all-to-all-done.1
  60.2 2.8 %fusion.1 = (bf16[512,768]{1,0:T(8,128)(2,1)S(1)}, f32[768,512]{0,1:T(8,128)}) fusion(s32[768]{0:T(1024)S(1)} %eq.24, f32[]{:T(128)} %bitcast.37, f32[]{:T(128)} %bitcast.4, s32[512]{0:T(512)S(1)} %eq.26, bf16[768,1152]{1,0:T(8,128)(2,1)S(1)} %bitcast.40, bf16[512,1152]{1,0:T(8,128)(2,1)S(1)} %bitcast.45), kind=kOutput, calls=%fused_computation.7 | convolution fusion | flops 911474688 | bytes 5313544 | tf_op jit(solution)/shard_map/dot_general | solution.py:56
  62.9 2.6 %fusion.9 = f32[2,256,1152]{2,1,0:T(8,128)} fusion(bf16[2,256,768]{2,1,0:T(8,128)(2,1)S(1)} %bitcast.49, bf16[768,1152,1]{1,0,2:T(8,128)(2,1)S(1)} %bitcast.41), kind=kOutput, calls=%fused_computation.36 | convolution fusion | flops 905969664 | bytes 4915200 | tf_op jit(solution)/shard_map/dot_general | solution.py:67
  65.5 3.8 %all-to-all-start.4 = ((f32[2,256,1152]{2,1,0:T(8,128)}), f32[2,256,1152]{2,1,0:T(8,128)S(1)}, u32[]{:S(2)}, u32[]{:S(2)}) async-start(f32[2,256,1152]{2,1,0:T(8,128)} %fusion.9), calls=%async_computation.4 | async-start | bytes 4718592 | tf_op jit(solution)/shard_map/all_to_all | solution.py:23
  69.4 4.3 %fusion = f16[768,1152]{1,0:T(8,128)(2,1)} fusion(bf16[512,1152]{1,0:T(8,128)(2,1)S(1)} %bitcast.46, f32[768,512]{0,1:T(8,128)} %get-tuple-element.12, f32[]{:T(128)} %bitcast.38, f32[]{:T(128)} %bitcast.4, s32[768]{0:T(1024)S(1)} %eq.24, s32[512]{0:T(512)S(1)} %eq.26), kind=kOutput, calls=%fused_computation.2 | convolution fusion | flops 913244160 | bytes 4527112 | tf_op jit(solution)/shard_map/dot_general | solution.py:71
  73.7 5.8 %all-to-all-start.2 = ((f16[4,192,1152]{2,1,0:T(8,128)(2,1)}), f16[4,192,1152]{2,1,0:T(8,128)(2,1)}, u32[]{:S(2)}, u32[]{:S(2)}) async-start(f16[4,192,1152]{2,1,0:T(8,128)(2,1)} %bitcast.42), calls=%async_computation.2 | async-start | bytes 3538944 | tf_op jit(solution)/shard_map/all_to_all | solution.py:23
  79.5 1.3 reduce_sum.95
  80.8 21.1 %all-to-all-done.2 = f16[4,192,1152]{2,1,0:T(8,128)(2,1)} async-done(((f16[4,192,1152]{2,1,0:T(8,128)(2,1)}), f16[4,192,1152]{2,1,0:T(8,128)(2,1)}, u32[]{:S(2)}, u32[]{:S(2)}) %all-to-all-start.2) | async-done | bytes 1769504 | tf_op jit(solution)/shard_map/all_to_all | solution.py:23
  101.9 1.8 %convert_reduce_fusion = f32[192,1152]{1,0:T(8,128)S(1)} fusion(f16[4,192,1152]{2,1,0:T(8,128)(2,1)} %all-to-all-done.2), kind=kLoop, calls=%fused_computation.1 | loop fusion | flops 1548288 | bytes 2654208 | tf_op jit(solution)/shard_map/reduce_sum | solution.py:73
  104.6 4.8 %all-to-all-start.3 = ((f16[8,24,1152]{2,1,0:T(8,128)(2,1)}), f16[8,24,1152]{2,1,0:T(8,128)(2,1)S(1)}, u32[]{:S(2)}, u32[]{:S(2)}) async-start(f16[8,24,1152]{2,1,0:T(8,128)(2,1)} %bitcast.12), calls=%async_computation.3 | async-start | bytes 884736 | tf_op jit(solution)/shard_map/all_to_all | solution.py:23
  109.4 2.6 %add_reduce_fusion = (f32[]{:T(128)}, f32[]{:T(128)}, f32[]{:T(128)}) fusion(f32[768,512]{0,1:T(8,128)S(1)} %copy-done, f32[]{:T(128)} %bitcast.39, f32[]{:T(128)} %bitcast.4, s32[768]{0:T(1024)S(1)} %eq.24, s32[512]{0:T(512)S(1)} %eq.26), kind=kLoop, calls=%fused_computation.9 | loop fusion | flops 7471101 | bytes 1578004 | tf_op jit(solution)/shard_map/reduce_sum | solution.py:61
  111.9 2.0 %pad_maximum_fusion = f32[3]{0:T(128)S(1)} fusion(f32[1]{0:T(128)} %bitcast.18, f32[1]{0:T(128)} %bitcast.17, f32[1]{0:T(128)} %bitcast.16), kind=kLoop, calls=%fused_computation.27 | loop fusion | flops 6 | bytes 24 | tf_op jit(solution)/shard_map/stack | solution.py:64
  113.9 2.4 %psum.28 = f32[3]{0:T(128)S(1)} all-reduce(f32[3]{0:T(128)S(1)} %pad_maximum_fusion), channel_id=1, replica_groups=mesh['y'=8,'zh'=2,'zl'=4,'x'=4,'core'=2] {'core'}, use_global_device_ids=true, to_apply=%region_11.12 | all-reduce | flops 3 | bytes 24 | tf_op jit(solution)/shard_map/psum | solution.py:78
  116.4 22.0 %psum.29 = f32[3]{0:T(128)S(1)} all-reduce(f32[3]{0:T(128)S(1)} %psum.28), channel_id=1, replica_groups=mesh['y'=8,'zh'=2,'zl'=4,'x'=4,'core'=2] {'zh','zl'}, use_global_device_ids=true, to_apply=%region_12.13 | all-reduce | flops 3 | bytes 24 | tf_op jit(solution)/shard_map/psum | solution.py:78
  138.4 9.2 %psum.30 = f32[3]{0:T(128)S(1)} all-reduce(f32[3]{0:T(128)S(1)} %psum.29), channel_id=1, replica_groups=mesh['y'=8,'zh'=2,'zl'=4,'x'=4,'core'=2] {'x'}, use_global_device_ids=true, to_apply=%region_13.14 | all-reduce | flops 3 | bytes 24 | tf_op jit(solution)/shard_map/psum | solution.py:78
  147.6 17.3 %psum.31 = f32[3]{0:T(128)S(1)} all-reduce(f32[3]{0:T(128)S(1)} %psum.30), channel_id=1, replica_groups=mesh['y'=8,'zh'=2,'zl'=4,'x'=4,'core'=2] {'y'}, use_global_device_ids=true, to_apply=%region_14.15 | all-reduce | flops 3 | bytes 24 | tf_op jit(solution)/shard_map/psum | solution.py:78
  168.4 1.1 multiply_reduce_fusion.1
  169.6 1.7 subtract_divide_fusion
  (36 shorter events, 6.3 us)
Async XLA Ops:
  7.2 50.4 %all-gather.2.cloned.1.call-start = ((), (), s32[]{:S(2)}) async-start(), calls=%async_computation.6 | async-start | bytes 1253376 | tf_op jit(solution)/shard_map/all_gather | solution.py:42
  35.7 6.3 %copy-start.4 = (s32[12288]{0:T(1024)S(1)}, s32[12288]{0:T(1024)}, u32[]{:S(2)}) copy-start(s32[12288]{0:T(1024)} %param.8) | copy-start | bytes 147460
  35.7 6.9 %copy-start.3 = (s32[16384]{0:T(1024)S(1)}, s32[16384]{0:T(1024)}, u32[]{:S(2)}) copy-start(s32[16384]{0:T(1024)} %param.9) | copy-start | bytes 196612
  35.7 24.4 %all-to-all-start.1 = ((bf16[4,192,1152]{2,1,0:T(8,128)(2,1)}), bf16[4,192,1152]{2,1,0:T(8,128)(2,1)S(1)}, u32[]{:S(2)}, u32[]{:S(2)}) async-start(bf16[4,192,1152]{2,1,0:T(8,128)(2,1)} %broadcast_in_dim.25), calls=%async_computation.1 | async-start | bytes 3538944 | tf_op jit(solution)/shard_map/all_to_all | solution.py:23
  65.5 8.1 %all-to-all-start.4 = ((f32[2,256,1152]{2,1,0:T(8,128)}), f32[2,256,1152]{2,1,0:T(8,128)S(1)}, u32[]{:S(2)}, u32[]{:S(2)}) async-start(f32[2,256,1152]{2,1,0:T(8,128)} %fusion.9), calls=%async_computation.4 | async-start | bytes 4718592 | tf_op jit(solution)/shard_map/all_to_all | solution.py:23
  73.7 28.2 %all-to-all-start.2 = ((f16[4,192,1152]{2,1,0:T(8,128)(2,1)}), f16[4,192,1152]{2,1,0:T(8,128)(2,1)}, u32[]{:S(2)}, u32[]{:S(2)}) async-start(f16[4,192,1152]{2,1,0:T(8,128)(2,1)} %bitcast.42), calls=%async_computation.2 | async-start | bytes 3538944 | tf_op jit(solution)/shard_map/all_to_all | solution.py:23
  79.5 89.0 %reduce-scatter.2.cloned.1.call-start = ((), (), s32[]{:S(2)}) async-start(), calls=%async_computation.7 | async-start | bytes 1327104 | tf_op jit(solution)/shard_map/reduce_scatter | solution.py:69
  103.7 5.7 %copy-start = (f32[768,512]{0,1:T(8,128)S(1)}, f32[768,512]{0,1:T(8,128)}, u32[]{:S(2)}) copy-start(f32[768,512]{0,1:T(8,128)} %get-tuple-element.12) | copy-start | bytes 4718596
  104.6 62.9 %copy-start.2 = (bf16[24,1152]{1,0:T(8,128)(2,1)S(1)}, bf16[24,1152]{1,0:T(8,128)(2,1)}, u32[]{:S(2)}) copy-start(bf16[24,1152]{1,0:T(8,128)(2,1)} %param.6) | copy-start | bytes 165892
  104.6 63.9 %copy-start.1 = (bf16[32,1152]{1,0:T(8,128)(2,1)S(1)}, bf16[32,1152]{1,0:T(8,128)(2,1)}, u32[]{:S(2)}) copy-start(bf16[32,1152]{1,0:T(8,128)(2,1)} %param.7) | copy-start | bytes 221188
  104.6 62.8 %all-to-all-start.3 = ((f16[8,24,1152]{2,1,0:T(8,128)(2,1)}), f16[8,24,1152]{2,1,0:T(8,128)(2,1)S(1)}, u32[]{:S(2)}, u32[]{:S(2)}) async-start(f16[8,24,1152]{2,1,0:T(8,128)(2,1)} %bitcast.12), calls=%async_computation.3 | async-start | bytes 884736 | tf_op jit(solution)/shard_map/all_to_all | solution.py:23
Sparse Core Ops, SparseCore 0:
  10.7 46.8 all-gather.1
  83.1 43.1 reduce-scatter.1

commit v2 on v1

v2 whole, which is shorter than its diff:
```python
import jax
import jax.numpy as jnp
from jax import lax
from jax.sharding import Mesh, PartitionSpec as P

AXES = ("y", "zh", "zl", "x", "core")
SIZES = (8, 2, 4, 4, 2)
Z = ("zh", "zl")
UNIT = 16384.0


def normalize(rows):
    values = rows.astype(jnp.float32)
    radius = jnp.sqrt(jnp.sum(values * values, -1, keepdims=True) + 1e-06)
    unit = values / radius
    return (unit, radius, lax.reduce_precision(unit, 8, 7))


def unnormalize(unit, radius, grad):
    return (grad - unit * jnp.sum(unit * grad, -1, keepdims=True)) / radius


def swap(value, axis):
    return lax.all_to_all(value, axis, 0, 0, tiled=False)


def shifted(value, axis, steps):
    count = lax.axis_size(axis)
    return lax.ppermute(value, axis, [(i, (i + steps) % count) for i in range(count)])


def spread(block, axis):
    count = lax.axis_size(axis)
    return swap(jnp.broadcast_to(block[None], (count,) + block.shape), axis)


def body(images, texts, image_ids, text_ids, log_scale, bias):
    width = images.shape[1]
    img_rows = images.shape[0]
    txt_rows = texts.shape[0]
    y, x, core = (lax.axis_index(a) for a in ("y", "x", "core"))
    z = lax.axis_index(Z)
    scale = jnp.exp(log_scale[0])
    shift = bias[0]
    ux, rx, uxb = normalize(images)
    uy, ry, uyb = normalize(texts)

    own = spread(uxb.astype(jnp.bfloat16), "y").reshape(-1, width)
    cols = (uyb * UNIT).astype(jnp.float16)
    cols = lax.all_gather(cols, Z + ("core",), axis=0, tiled=True)
    cols = (cols.astype(jnp.float32) * (1 / UNIT)).astype(jnp.bfloat16)
    cols = cols.reshape(8, 2, txt_rows, width)
    cols = jnp.concatenate([cols[:, 0], cols[:, 1]], 0).reshape(-1, width)

    col_ids = text_ids.reshape(8, 8, 4, 2, txt_rows)
    col_ids = lax.dynamic_index_in_dim(col_ids, y, 0, keepdims=False)
    col_ids = lax.dynamic_index_in_dim(col_ids, x, 1, keepdims=False)
    col_ids = col_ids.transpose(1, 0, 2).reshape(-1)
    row_ids = image_ids.reshape(8, 8, 4, 2, img_rows)
    row_ids = lax.dynamic_index_in_dim(row_ids, z, 1, keepdims=False)
    row_ids = lax.dynamic_index_in_dim(row_ids, core, 2, keepdims=False)
    row_ids = row_ids.transpose(1, 0, 2).reshape(4, -1)

    order = (0, 1, 3, 2)
    parts = {k: shifted(own, "x", k) if k else own for k in order}
    slopes, back, stats = {}, {}, jnp.zeros((3,), jnp.float32)
    for k in order:
        ids = lax.dynamic_index_in_dim(row_ids, (x - k) % 4, 0, keepdims=False)
        dots = jnp.dot(parts[k], cols.T, preferred_element_type=jnp.float32)
        logits = scale * dots + shift
        match = ids[:, None] == col_ids[None, :]
        against = jnp.where(match, -logits, logits)
        decay = jnp.exp(-jnp.abs(against))
        objective = jnp.sum(jnp.maximum(against, 0.0) + jnp.log1p(decay))
        weight = jnp.where(against >= 0.0, 1.0, decay) / (1.0 + decay)
        slope = jnp.where(match, -weight, weight)
        stats += jnp.stack([objective, jnp.sum(slope * dots), jnp.sum(slope)])
        slopes[k] = slope.astype(jnp.bfloat16)
        drows = jnp.dot(slopes[k], cols, preferred_element_type=jnp.float32)
        back[k] = shifted((drows * 64.0).astype(jnp.float16), "x", -k) if k else drows * 64.0

    rows = jnp.concatenate([parts[k] for k in order], 0)
    weights = jnp.concatenate([slopes[k] for k in order], 0).reshape(-1, 2, 8 * txt_rows)
    theirs = lax.dynamic_index_in_dim(weights, 1 - core, 1, keepdims=False)
    mine = lax.dynamic_index_in_dim(weights, core, 1, keepdims=False)
    theirs = jnp.dot(theirs.T, rows, preferred_element_type=jnp.float32)
    theirs = shifted(theirs, "core", 1)
    dcols = theirs + jnp.dot(mine.T, rows, preferred_element_type=jnp.float32)
    dcols = (dcols * 32.0).astype(jnp.float16).reshape(8, txt_rows, width)
    text_accum = jnp.sum(swap(dcols, Z).astype(jnp.float32), 0) * (1 / 32.0)

    drows = sum(back[k].astype(jnp.float32) for k in order)
    drows = (drows * 0.25).astype(jnp.float16).reshape(8, -1, width)
    image_accum = jnp.sum(swap(drows, "y").astype(jnp.float32), 0) * 0.0625

    for axis in (("x", "core"), Z, "y"):
        stats = lax.psum(stats, axis)
    total_texts = txt_rows * 512
    image_grad = unnormalize(ux, rx, scale * image_accum)
    text_grad = unnormalize(uy, ry, scale * text_accum)
    loss = (stats[0] / total_texts).reshape(1)
    scale_grad = (scale * stats[1] / total_texts).reshape(1)
    bias_grad = (stats[2] / total_texts).reshape(1)
    return (image_grad, text_grad, loss, scale_grad, bias_grad)


def solution(mesh):
    fine = Mesh(mesh.devices.reshape(SIZES), AXES)
    split = P(AXES, None)
    return jax.shard_map(
        body,
        mesh=fine,
        in_specs=(split, split, P(), P(), P(), P()),
        out_specs=(split, split, P(), P(), P()),
        check_vma=False,
    )
```

time: 182 us -> 196 us (1.077)
  the two profiles are of different devices: /device:TPU:2 before, /device:TPU:8 now
where the time goes in v2:
time: 196 us
  blocking collectives  72.6 us (37%)
  starting transfers between devices  43.2 us (22%)
  waiting for transfers between devices  41.4 us (21%)
  other arithmetic  13.1 us (7%)
  matrix products  12.1 us (6%)
  between operations  7.74 us (4%)
  local copies, waits for them, and re-layouts  5.35 us (3%)
    psum x3, blocking collectives, body(): stats = lax.psum(stats, axis)  47.9 us
    ppermute x7, waiting for transfers between devices, shifted(): lax.ppermute(value, axis, [(i, (i + steps) % count) for i in range(count)])  30.3 us
    all_gather x1, blocking collectives, body(): cols = lax.all_gather(cols, Z + ('core',), axis=0, tiled=True)  24.8 us
    ppermute x7, starting transfers between devices, shifted(): lax.ppermute(value, axis, [(i, (i + steps) % count) for i in range(count)])  23.3 us
    all_to_all x3, starting transfers between devices, swap(): return lax.all_to_all(value, axis, 0, 0, tiled=False)  19.9 us
    all_to_all x3, waiting for transfers between devices, swap(): return lax.all_to_all(value, axis, 0, 0, tiled=False)  11.1 us
    add x1, other arithmetic, body(): stats += jnp.stack([objective, jnp.sum(slope * dots), jnp.sum(slope)])  7.6 us
    dot_general x4, matrix products, body(): dots = jnp.dot(parts[k], cols.T, preferred_element_type=jnp.float32)  4.14 us
  transfers between devices with their start and end apart: 10, of which 6 were waited for; matrix products, arithmetic and copies ran while one was open for 9% of the time, Pallas kernels for 0%

profile of v2, /device:TPU:8, one launch (start us, length us, event | category | flops | bytes accessed | tf_op | source)
XLA Modules:
  0.0 195.6 jit_solution(2028064428366789027)
XLA Ops:
  3.4 9.2 %all-to-all-start = ((bf16[8,24,1152]{2,1,0:T(8,128)(2,1)}), bf16[8,24,1152]{2,1,0:T(8,128)(2,1)S(1)}, u32[]{:S(2)}, u32[]{:S(2)}) async-start(bf16[8,24,1152]{2,1,0:T(8,128)(2,1)} %broadcast_in_dim.9), calls=%async_computation | async-start | bytes 884736 | tf_op jit(solution)/shard_map/all_to_all | solution.py:24
  13.5 24.8 %all-gather.1 = f16[512,1152]{1,0:T(8,128)(2,1)S(1)} all-gather(f16[32,1152]{1,0:T(8,128)(2,1)S(1)} %multiply_convert_fusion.3), channel_id=1, replica_groups=mesh['y'=8,'zh'=2,'zl'=4,'x'=4,'core'=2] {'zh','zl','core'}, dimensions={0}, use_global_device_ids=true | all-gather | bytes 1253376 | tf_op jit(solution)/shard_map/all_gather | solution.py:50
  38.8 3.4 %collective-permute-start = (bf16[192,1152]{1,0:T(8,128)(2,1)S(1)}, bf16[192,1152]{1,0:T(8,128)(2,1)S(1)}, u32[]{:S(2)}, u32[]{:S(2)}) collective-permute-start(bf16[192,1152]{1,0:T(8,128)(2,1)S(1)} %bitcast.73), channel_id=1, source_target_pairs={{0,2},{2,4},{4,6},{6,0},{1,3},{3,5},{5,7},{7,1},{8,10},{10,12},{12... | collective-permute-start | bytes 1327112 | tf_op jit(solution)/shard_map/ppermute | solution.py:29
  43.8 3.7 %collective-permute-start.2 = (bf16[192,1152]{1,0:T(8,128)(2,1)S(1)}, bf16[192,1152]{1,0:T(8,128)(2,1)S(1)}, u32[]{:S(2)}, u32[]{:S(2)}) collective-permute-start(bf16[192,1152]{1,0:T(8,128)(2,1)S(1)} %bitcast.74), channel_id=1, source_target_pairs={{0,6},{2,0},{4,2},{6,4},{1,7},{3,1},{5,3},{7,5},{8,14},{10,8},{12,... | collective-permute-start | bytes 1327112 | tf_op jit(solution)/shard_map/ppermute | solution.py:29
  47.5 3.7 %collective-permute-start.4 = (bf16[192,1152]{1,0:T(8,128)(2,1)S(1)}, bf16[192,1152]{1,0:T(8,128)(2,1)S(1)}, u32[]{:S(2)}, u32[]{:S(2)}) collective-permute-start(bf16[192,1152]{1,0:T(8,128)(2,1)S(1)} %bitcast.75), channel_id=1, source_target_pairs={{0,4},{2,6},{4,0},{6,2},{1,5},{3,7},{5,1},{7,3},{8,12},{10,14},{12... | collective-permute-start | bytes 1327112 | tf_op jit(solution)/shard_map/ppermute | solution.py:29
  51.7 2.6 %collective-permute-done = bf16[192,1152]{1,0:T(8,128)(2,1)S(1)} collective-permute-done((bf16[192,1152]{1,0:T(8,128)(2,1)S(1)}, bf16[192,1152]{1,0:T(8,128)(2,1)S(1)}, u32[]{:S(2)}, u32[]{:S(2)}) %collective-permute-start) | collective-permute-done | bytes 442400 | tf_op jit(solution)/shard_map/ppermute | solution.py:29
  54.9 11.8 %collective-permute-done.2 = bf16[192,1152]{1,0:T(8,128)(2,1)S(1)} collective-permute-done((bf16[192,1152]{1,0:T(8,128)(2,1)S(1)}, bf16[192,1152]{1,0:T(8,128)(2,1)S(1)}, u32[]{:S(2)}, u32[]{:S(2)}) %collective-permute-start.2) | collective-permute-done | bytes 442400 | tf_op jit(solution)/shard_map/ppermute | solution.py:29
  67.4 2.5 %add_reduce_fusion = (f32[]{:T(128)}, f32[]{:T(128)}, f32[]{:T(128)}, f32[]{:T(128)}, f32[]{:T(128)}, /*index=5*/f32[]{:T(128)}, f32[]{:T(128)}, f32[]{:T(128)},...) fusion(f32[]{:T(128)} %bitcast.63, f32[]{:T(128)} %bitcast.5, ...), kind=kOutput, calls=%fused_computation.30 | convolution fusion | flops 234356736 | bytes 3593272 | tf_op jit(solution)/shard_map/dot_general | solution.py:69
  72.6 2.6 %constant_dynamic-slice_fusion = (bf16[768,1,256]{2,1,0:T(2,128)(2,1)}, bf16[768,1,256]{2,1,0:T(2,128)(2,1)S(1)}) fusion(bf16[768,2,256]{2,1,0:T(2,128)(2,1)S(1)} %reshape.84, s32[]{:T(128)S(6)} %select_n.101, s32[]{:T(128)S(6)} %select_n.127), kind=kLoop, calls=%fused_computation.55 | loop fusion | bytes 1572872 | tf_op jit(solution)/shard_map/jit(dynamic_index_in_dim)/dynamic_slice | solution.py:85
  75.1 1.7 fusion.4
  76.9 2.0 %collective-permute-start.6 = (f32[256,1152]{1,0:T(8,128)}, f32[256,1152]{1,0:T(8,128)S(1)}, u32[]{:S(2)}, u32[]{:S(2)}) collective-permute-start(f32[256,1152]{1,0:T(8,128)} %fusion.4), channel_id=1, source_target_pairs={{0,1},{1,0},{2,3},{3,2},{4,5},{5,4},{6,7},{7,6},{8,9},{9,8},{10,11... | collective-permute-start | bytes 3538952 | tf_op jit(solution)/shard_map/ppermute | solution.py:29
  79.4 1.9 collective-permute-start.5
  81.3 6.4 %collective-permute-start.3 = (f16[192,1152]{1,0:T(8,128)(2,1)S(1)}, f16[192,1152]{1,0:T(8,128)(2,1)S(1)}, u32[]{:S(2)}, u32[]{:S(2)}) collective-permute-start(f16[192,1152]{1,0:T(8,128)(2,1)S(1)} %copy-done.4), channel_id=1, source_target_pairs={{0,2},{2,4},{4,6},{6,0},{1,3},{3,5},{5,7},{7,1},{8,10},{10,12},{12... | collective-permute-start | bytes 1327112 | tf_op jit(solution)/shard_map/ppermute | solution.py:29
  87.7 2.1 %collective-permute-start.1 = (f16[192,1152]{1,0:T(8,128)(2,1)S(1)}, f16[192,1152]{1,0:T(8,128)(2,1)S(1)}, u32[]{:S(2)}, u32[]{:S(2)}) collective-permute-start(f16[192,1152]{1,0:T(8,128)(2,1)S(1)} %fusion), channel_id=1, source_target_pairs={{0,6},{2,0},{4,2},{6,4},{1,7},{3,1},{5,3},{7,5},{8,14},{10,8},{12,... | collective-permute-start | bytes 1327112 | tf_op jit(solution)/shard_map/ppermute | solution.py:29
  89.9 5.9 %collective-permute-done.5 = f16[192,1152]{1,0:T(8,128)(2,1)S(1)} collective-permute-done((f16[192,1152]{1,0:T(8,128)(2,1)S(1)}, f16[192,1152]{1,0:T(8,128)(2,1)S(1)}, u32[]{:S(2)}, u32[]{:S(2)}) %collective-permute-start.5) | collective-permute-done | bytes 442400 | tf_op jit(solution)/shard_map/ppermute | solution.py:29
  95.8 9.0 %collective-permute-done.3 = f16[192,1152]{1,0:T(8,128)(2,1)S(1)} collective-permute-done((f16[192,1152]{1,0:T(8,128)(2,1)S(1)}, f16[192,1152]{1,0:T(8,128)(2,1)S(1)}, u32[]{:S(2)}, u32[]{:S(2)}) %collective-permute-start.3) | collective-permute-done | bytes 442400 | tf_op jit(solution)/shard_map/ppermute | solution.py:29
  107.2 7.2 %all-to-all-start.1 = ((f16[8,24,1152]{2,1,0:T(8,128)(2,1)}), f16[8,24,1152]{2,1,0:T(8,128)(2,1)S(1)}, u32[]{:S(2)}, u32[]{:S(2)}) async-start(f16[8,24,1152]{2,1,0:T(8,128)(2,1)} %bitcast.15), calls=%async_computation.1 | async-start | bytes 884736 | tf_op jit(solution)/shard_map/all_to_all | solution.py:24
  114.4 2.1 %fusion.3 = f32[256,1152]{1,0:T(8,128)S(1)} fusion(bf16[768,1,256]{2,1,0:T(2,128)(2,1)} %get-tuple-element.32, bf16[192,1152]{1,0:T(8,128)(2,1)} %copy-done.12, bf16[192,1152]{1,0:T(8,128)(2,1)} %copy-done.8, bf16[192,1152]{1,0:T(8,128)(2,1)S(1)} %copy-done.7, bf16[192,1152]{1,0:T(8,128)(2,1)S(1)} %bitcast.78), kind=kOutput, calls=%fused_computation.26 | convolution fusion | flops 460062720 | bytes 3342336 | tf_op jit(solution)/shard_map/dot_general | solution.py:88
  117.4 11.1 %all-to-all-done.1 = f16[8,24,1152]{2,1,0:T(8,128)(2,1)S(1)} async-done(((f16[8,24,1152]{2,1,0:T(8,128)(2,1)}), f16[8,24,1152]{2,1,0:T(8,128)(2,1)S(1)}, u32[]{:S(2)}, u32[]{:S(2)}) %all-to-all-start.1) | async-done | bytes 442400 | tf_op jit(solution)/shard_map/all_to_all | solution.py:24
  128.5 3.5 %all-to-all-start.2 = ((f16[8,32,1152]{2,1,0:T(8,128)(2,1)}), f16[8,32,1152]{2,1,0:T(8,128)(2,1)S(1)}, u32[]{:S(2)}, u32[]{:S(2)}) async-start(f16[8,32,1152]{2,1,0:T(8,128)(2,1)} %bitcast.18), calls=%async_computation.2 | async-start | bytes 1179648 | tf_op jit(solution)/shard_map/all_to_all | solution.py:24
  132.1 7.6 %fusion.8 = f32[3]{0:T(128)S(1)} fusion(f32[1]{0:T(128)} %bitcast.21, f32[1]{0:T(128)} %bitcast.20, f32[1]{0:T(128)} %bitcast.19, f32[1]{0:T(128)} %bitcast.24, f32[1]{0:T(128)} %bitcast.23, f32[1]{0:T(128)} %bitcast.22, f32[1]{0:T(128)} %bitcast.27, f32[1]{0:T(128)} %bitcast.26, f32[1]{0:T(128)} %bitcast.25, f32[1]{0:T(128)} %bitcast.30, f32[1]{0:T(128)} %bitcast.29, ...), kind=kLoop, calls=%fused_computation.65 | loop fusion | flops 33 | bytes 60 | tf_op jit(solution)/shard_map/add | solution.py:77
  139.7 12.9 %psum.21 = f32[3]{0:T(128)S(1)} all-reduce(f32[3]{0:T(128)S(1)} %fusion.8), channel_id=1, replica_groups=mesh['y'=8,'zh'=2,'zl'=4,'x'=4,'core'=2] {'x','core'}, use_global_device_ids=true, to_apply=%region_18.19 | all-reduce | flops 3 | bytes 24 | tf_op jit(solution)/shard_map/psum | solution.py:97
  152.5 17.1 %psum.22 = f32[3]{0:T(128)S(1)} all-reduce(f32[3]{0:T(128)S(1)} %psum.21), channel_id=1, replica_groups=mesh['y'=8,'zh'=2,'zl'=4,'x'=4,'core'=2] {'zh','zl'}, use_global_device_ids=true, to_apply=%region_19.20 | all-reduce | flops 3 | bytes 24 | tf_op jit(solution)/shard_map/psum | solution.py:97
  169.7 17.9 %psum.23 = f32[3]{0:T(128)S(1)} all-reduce(f32[3]{0:T(128)S(1)} %psum.22), channel_id=1, replica_groups=mesh['y'=8,'zh'=2,'zl'=4,'x'=4,'core'=2] {'y'}, use_global_device_ids=true, to_apply=%region_20.21 | all-reduce | flops 3 | bytes 24 | tf_op jit(solution)/shard_map/psum | solution.py:97
  (69 shorter events, 15.1 us)
Async XLA Ops:
  0.6 11.9 %copy-start.10 = (s32[16384]{0:T(1024)S(1)}, s32[16384]{0:T(1024)}, u32[]{:S(2)}) copy-start(s32[16384]{0:T(1024)} %param.9) | copy-start | bytes 196612
  0.6 12.2 %copy-start.11 = (s32[12288]{0:T(1024)S(1)}, s32[12288]{0:T(1024)}, u32[]{:S(2)}) copy-start(s32[12288]{0:T(1024)} %param.8) | copy-start | bytes 147460
  0.7 12.6 %copy-start = (bf16[32,1152]{1,0:T(8,128)(2,1)S(1)}, bf16[32,1152]{1,0:T(8,128)(2,1)}, u32[]{:S(2)}) copy-start(bf16[32,1152]{1,0:T(8,128)(2,1)} %param.7) | copy-start | bytes 221188
  3.4 35.4 %all-to-all-start = ((bf16[8,24,1152]{2,1,0:T(8,128)(2,1)}), bf16[8,24,1152]{2,1,0:T(8,128)(2,1)S(1)}, u32[]{:S(2)}, u32[]{:S(2)}) async-start(bf16[8,24,1152]{2,1,0:T(8,128)(2,1)} %broadcast_in_dim.9), calls=%async_computation | async-start | bytes 884736 | tf_op jit(solution)/shard_map/all_to_all | solution.py:24
  38.8 15.5 %collective-permute-start = (bf16[192,1152]{1,0:T(8,128)(2,1)S(1)}, bf16[192,1152]{1,0:T(8,128)(2,1)S(1)}, u32[]{:S(2)}, u32[]{:S(2)}) collective-permute-start(bf16[192,1152]{1,0:T(8,128)(2,1)S(1)} %bitcast.73), channel_id=1, source_target_pairs={{0,2},{2,4},{4,6},{6,0},{1,3},{3,5},{5,7},{7,1},{8,10},{10,12},{12... | collective-permute-start | bytes 1327112 | tf_op jit(solution)/shard_map/ppermute | solution.py:29
  43.8 22.8 %collective-permute-start.2 = (bf16[192,1152]{1,0:T(8,128)(2,1)S(1)}, bf16[192,1152]{1,0:T(8,128)(2,1)S(1)}, u32[]{:S(2)}, u32[]{:S(2)}) collective-permute-start(bf16[192,1152]{1,0:T(8,128)(2,1)S(1)} %bitcast.74), channel_id=1, source_target_pairs={{0,6},{2,0},{4,2},{6,4},{1,7},{3,1},{5,3},{7,5},{8,14},{10,8},{12,... | collective-permute-start | bytes 1327112 | tf_op jit(solution)/shard_map/ppermute | solution.py:29
  47.5 19.7 %collective-permute-start.4 = (bf16[192,1152]{1,0:T(8,128)(2,1)S(1)}, bf16[192,1152]{1,0:T(8,128)(2,1)S(1)}, u32[]{:S(2)}, u32[]{:S(2)}) collective-permute-start(bf16[192,1152]{1,0:T(8,128)(2,1)S(1)} %bitcast.75), channel_id=1, source_target_pairs={{0,4},{2,6},{4,0},{6,2},{1,5},{3,7},{5,1},{7,3},{8,12},{10,14},{12... | collective-permute-start | bytes 1327112 | tf_op jit(solution)/shard_map/ppermute | solution.py:29
  54.3 12.9 %copy-start.6 = (bf16[192,1152]{1,0:T(8,128)(2,1)}, bf16[192,1152]{1,0:T(8,128)(2,1)S(1)}, u32[]{:S(2)}) copy-start(bf16[192,1152]{1,0:T(8,128)(2,1)S(1)} %collective-permute-done) | copy-start | bytes 1327108
  66.6 0.8 copy-start.8
  67.2 2.7 %copy-start.12 = (bf16[192,1152]{1,0:T(8,128)(2,1)}, bf16[192,1152]{1,0:T(8,128)(2,1)S(1)}, u32[]{:S(2)}) copy-start(bf16[192,1152]{1,0:T(8,128)(2,1)S(1)} %collective-permute-done.4) | copy-start | bytes 1327108
  69.9 2.4 %copy-start.2 = (bf16[192,512]{1,0:T(8,128)(2,1)}, bf16[192,512]{1,0:T(8,128)(2,1)S(1)}, u32[]{:S(2)}) copy-start(bf16[192,512]{1,0:T(8,128)(2,1)S(1)} %get-tuple-element.27) | copy-start | bytes 589828
  72.5 2.6 %copy-start.7 = (bf16[192,1152]{1,0:T(8,128)(2,1)S(1)}, bf16[192,1152]{1,0:T(8,128)(2,1)}, u32[]{:S(2)}) copy-start(bf16[192,1152]{1,0:T(8,128)(2,1)} %copy-done.6) | copy-start | bytes 1327108
  72.5 2.6 %copy-start.9 = (bf16[192,1152]{1,0:T(8,128)(2,1)S(1)}, bf16[192,1152]{1,0:T(8,128)(2,1)}, u32[]{:S(2)}) copy-start(bf16[192,1152]{1,0:T(8,128)(2,1)} %copy-done.8) | copy-start | bytes 1327108
  72.5 2.6 %copy-start.13 = (bf16[192,1152]{1,0:T(8,128)(2,1)S(1)}, bf16[192,1152]{1,0:T(8,128)(2,1)}, u32[]{:S(2)}) copy-start(bf16[192,1152]{1,0:T(8,128)(2,1)} %copy-done.12) | copy-start | bytes 1327108
  75.1 3.8 %copy-start.3 = (bf16[192,512]{1,0:T(8,128)(2,1)S(1)}, bf16[192,512]{1,0:T(8,128)(2,1)}, u32[]{:S(2)}) copy-start(bf16[192,512]{1,0:T(8,128)(2,1)} %copy-done.2) | copy-start | bytes 589828
  76.9 2.5 %copy-start.5 = (f16[192,1152]{1,0:T(8,128)(2,1)S(1)}, f16[192,1152]{1,0:T(8,128)(2,1)}, u32[]{:S(2)}) copy-start(f16[192,1152]{1,0:T(8,128)(2,1)} %fusion.2) | copy-start | bytes 1327108
  76.9 4.4 %copy-start.4 = (f16[192,1152]{1,0:T(8,128)(2,1)S(1)}, f16[192,1152]{1,0:T(8,128)(2,1)}, u32[]{:S(2)}) copy-start(f16[192,1152]{1,0:T(8,128)(2,1)} %fusion.1) | copy-start | bytes 1327108
  76.9 39.6 %collective-permute-start.6 = (f32[256,1152]{1,0:T(8,128)}, f32[256,1152]{1,0:T(8,128)S(1)}, u32[]{:S(2)}, u32[]{:S(2)}) collective-permute-start(f32[256,1152]{1,0:T(8,128)} %fusion.4), channel_id=1, source_target_pairs={{0,1},{1,0},{2,3},{3,2},{4,5},{5,4},{6,7},{7,6},{8,9},{9,8},{10,11... | collective-permute-start | bytes 3538952 | tf_op jit(solution)/shard_map/ppermute | solution.py:29
  79.4 16.4 %collective-permute-start.5 = (f16[192,1152]{1,0:T(8,128)(2,1)S(1)}, f16[192,1152]{1,0:T(8,128)(2,1)S(1)}, u32[]{:S(2)}, u32[]{:S(2)}) collective-permute-start(f16[192,1152]{1,0:T(8,128)(2,1)S(1)} %copy-done.5), channel_id=1, source_target_pairs={{0,4},{2,6},{4,0},{6,2},{1,5},{3,7},{5,1},{7,3},{8,12},{10,14},{12... | collective-permute-start | bytes 1327112 | tf_op jit(solution)/shard_map/ppermute | solution.py:29
  81.3 23.5 %collective-permute-start.3 = (f16[192,1152]{1,0:T(8,128)(2,1)S(1)}, f16[192,1152]{1,0:T(8,128)(2,1)S(1)}, u32[]{:S(2)}, u32[]{:S(2)}) collective-permute-start(f16[192,1152]{1,0:T(8,128)(2,1)S(1)} %copy-done.4), channel_id=1, source_target_pairs={{0,2},{2,4},{4,6},{6,0},{1,3},{3,5},{5,7},{7,1},{8,10},{10,12},{12... | collective-permute-start | bytes 1327112 | tf_op jit(solution)/shard_map/ppermute | solution.py:29
  87.7 18.1 %collective-permute-start.1 = (f16[192,1152]{1,0:T(8,128)(2,1)S(1)}, f16[192,1152]{1,0:T(8,128)(2,1)S(1)}, u32[]{:S(2)}, u32[]{:S(2)}) collective-permute-start(f16[192,1152]{1,0:T(8,128)(2,1)S(1)} %fusion), channel_id=1, source_target_pairs={{0,6},{2,0},{4,2},{6,4},{1,7},{3,1},{5,3},{7,5},{8,14},{10,8},{12,... | collective-permute-start | bytes 1327112 | tf_op jit(solution)/shard_map/ppermute | solution.py:29
  107.2 21.4 %all-to-all-start.1 = ((f16[8,24,1152]{2,1,0:T(8,128)(2,1)}), f16[8,24,1152]{2,1,0:T(8,128)(2,1)S(1)}, u32[]{:S(2)}, u32[]{:S(2)}) async-start(f16[8,24,1152]{2,1,0:T(8,128)(2,1)} %bitcast.15), calls=%async_computation.1 | async-start | bytes 884736 | tf_op jit(solution)/shard_map/all_to_all | solution.py:24
  117.4 72.7 %copy-start.1 = (bf16[24,1152]{1,0:T(8,128)(2,1)S(1)}, bf16[24,1152]{1,0:T(8,128)(2,1)}, u32[]{:S(2)}) copy-start(bf16[24,1152]{1,0:T(8,128)(2,1)} %param.6) | copy-start | bytes 165892
  128.5 62.6 %all-to-all-start.2 = ((f16[8,32,1152]{2,1,0:T(8,128)(2,1)}), f16[8,32,1152]{2,1,0:T(8,128)(2,1)S(1)}, u32[]{:S(2)}, u32[]{:S(2)}) async-start(f16[8,32,1152]{2,1,0:T(8,128)(2,1)} %bitcast.18), calls=%async_computation.2 | async-start | bytes 1179648 | tf_op jit(solution)/shard_map/all_to_all | solution.py:24

commit v3 on v2

v3 whole, which is shorter than its diff:
```python
import jax
import jax.numpy as jnp
from jax import lax
from jax.experimental import pallas as pl
from jax.experimental.pallas import tpu as pltpu
from jax.sharding import Mesh, PartitionSpec as P

AXES = ("y", "zh", "zl", "x", "core")
SIZES = (8, 2, 4, 4, 2)
Z = ("zh", "zl")
UNIT = 16384.0


def normalize(rows):
    values = rows.astype(jnp.float32)
    radius = jnp.sqrt(jnp.sum(values * values, -1, keepdims=True) + 1e-06)
    unit = values / radius
    return (unit, radius, lax.reduce_precision(unit, 8, 7))


def unnormalize(unit, radius, grad):
    return (grad - unit * jnp.sum(unit * grad, -1, keepdims=True)) / radius


def swap(value, axis):
    return lax.all_to_all(value, axis, 0, 0, tiled=False)


def shifted(value, axis, steps):
    count = lax.axis_size(axis)
    return lax.ppermute(value, axis, [(i, (i + steps) % count) for i in range(count)])


def spread(block, axis):
    count = lax.axis_size(axis)
    return swap(jnp.broadcast_to(block[None], (count,) + block.shape), axis)


def forward_kernel(place, scalars, rows, cols, row_ids, col_ids, near, whole, stats, sums):
    step = pl.program_id(0)
    dots = lax.dot_general(
        rows[...], cols[...], (((1,), (1,)), ((), ())), preferred_element_type=jnp.float32
    )
    logits = scalars[0] * dots + scalars[1]
    match = row_ids[...] == col_ids[...]
    against = jnp.where(match, -logits, logits)
    decay = jnp.exp(-jnp.abs(against))
    objective = jnp.maximum(against, 0.0) + jnp.log1p(decay)
    weight = jnp.where(against >= 0.0, 1.0, decay) / (1.0 + decay)
    slope = jnp.where(match, -weight, weight)
    slopeb = slope.astype(jnp.bfloat16)
    near[...] = slopeb
    whole[...] = slopeb

    @pl.when(step == 0)
    def _():
        sums[...] = jnp.zeros_like(sums)

    for i, term in enumerate((objective, slope * dots, slope)):
        sums[i : i + 1, :] += jnp.sum(term, 0, keepdims=True)

    @pl.when(step == pl.num_programs(0) - 1)
    def _():
        stats[...] = jnp.broadcast_to(jnp.sum(sums[...], 1, keepdims=True), stats.shape)


def forward(x, scalars, rows, cols, row_ids, col_ids):
    parts = lax.axis_size("x")
    high, width = rows.shape[0] // parts, rows.shape[1]
    wide = cols.shape[0]
    part = lambda k, place: ((place[0] + k) % parts, 0)
    same = lambda k, place: (0, 0)
    slopes = jax.ShapeDtypeStruct((rows.shape[0], wide), jnp.bfloat16)
    return pl.pallas_call(
        forward_kernel,
        grid_spec=pltpu.PrefetchScalarGridSpec(
            num_scalar_prefetch=1,
            grid=(parts,),
            in_specs=[
                pl.BlockSpec(memory_space=pltpu.SMEM),
                pl.BlockSpec((high, width), part),
                pl.BlockSpec((wide, width), same),
                pl.BlockSpec((high, 1), part),
                pl.BlockSpec((1, wide), same),
            ],
            out_specs=[
                pl.BlockSpec((high, wide), lambda k, place: (k, 0)),
                pl.BlockSpec((high, wide), part),
                pl.BlockSpec((8, 128), same),
            ],
            scratch_shapes=[pltpu.VMEM((8, wide), jnp.float32)],
        ),
        out_shape=(slopes, slopes, jax.ShapeDtypeStruct((8, 128), jnp.float32)),
        compiler_params=pltpu.CompilerParams(vmem_limit_bytes=32 * 2**20),
        cost_estimate=pl.CostEstimate(flops=10**9, bytes_accessed=5 * 10**6, transcendentals=10**6),
        name="forward",
    )(x.reshape(1).astype(jnp.int32), scalars, rows, cols, row_ids, col_ids)


def body(images, texts, image_ids, text_ids, log_scale, bias):
    width = images.shape[1]
    img_rows = images.shape[0]
    txt_rows = texts.shape[0]
    y, x, core = (lax.axis_index(a) for a in ("y", "x", "core"))
    z = lax.axis_index(Z)
    scale = jnp.exp(log_scale[0])
    ux, rx, uxb = normalize(images)
    uy, ry, uyb = normalize(texts)

    own = spread(uxb.astype(jnp.bfloat16), "y").reshape(-1, width)
    cols = (uyb * UNIT).astype(jnp.float16)
    own, cols = lax.optimization_barrier((own, cols))
    rows = spread(own, "x").reshape(-1, width)
    cols = lax.all_gather(cols, Z + ("core",), axis=0, tiled=True)
    cols = (cols.astype(jnp.float32) * (1 / UNIT)).astype(jnp.bfloat16)
    cols = cols.reshape(8, 2, txt_rows, width)
    mine = lax.dynamic_index_in_dim(cols, core, 1, keepdims=False)
    theirs = lax.dynamic_index_in_dim(cols, 1 - core, 1, keepdims=False)
    cols = jnp.concatenate([mine, theirs], 0).reshape(-1, width)

    col_ids = text_ids.reshape(8, 8, 4, 2, txt_rows)
    col_ids = lax.dynamic_index_in_dim(col_ids, y, 0, keepdims=False)
    col_ids = lax.dynamic_index_in_dim(col_ids, x, 1, keepdims=False)
    mine = lax.dynamic_index_in_dim(col_ids, core, 1, keepdims=False)
    theirs = lax.dynamic_index_in_dim(col_ids, 1 - core, 1, keepdims=False)
    col_ids = jnp.concatenate([mine, theirs], 0).reshape(1, -1)
    row_ids = image_ids.reshape(8, 8, 4, 2, img_rows)
    row_ids = lax.dynamic_index_in_dim(row_ids, z, 1, keepdims=False)
    row_ids = lax.dynamic_index_in_dim(row_ids, core, 2, keepdims=False)
    row_ids = row_ids.transpose(1, 0, 2).reshape(-1, 1)

    near, whole, stats = forward(x, jnp.stack([scale, bias[0]]), rows, cols, row_ids, col_ids)
    stats = stats[:3, 0]

    half = cols.shape[0] // 2
    theirs = lax.dot_general(
        whole[:, half:], rows, (((0,), (0,)), ((), ())), preferred_element_type=jnp.float32
    )
    theirs = shifted(theirs, "core", 1)
    dcols = theirs + lax.dot_general(
        whole[:, :half], rows, (((0,), (0,)), ((), ())), preferred_element_type=jnp.float32
    )
    dcols = (dcols * 32.0).astype(jnp.float16).reshape(8, txt_rows, width)
    dcols = swap(dcols, Z)

    high = rows.shape[0] // 4
    back = {}
    for k in (1, 3, 2, 0):
        drows = 64.0 * jnp.dot(near[k * high : (k + 1) * high], cols, preferred_element_type=jnp.float32)
        back[k] = shifted(drows.astype(jnp.float16), "x", k) if k else drows
    drows = sum(part.astype(jnp.float32) for part in back.values())
    drows = (drows * 0.25).astype(jnp.float16).reshape(8, -1, width)
    drows = swap(drows, "y")

    for axis in (("x", "core"), Z, "y"):
        stats = lax.psum(stats, axis)
    total_texts = txt_rows * 512
    image_accum = jnp.sum(drows.astype(jnp.float32), 0) * 0.0625
    text_accum = jnp.sum(dcols.astype(jnp.float32), 0) * (1 / 32.0)
    image_grad = unnormalize(ux, rx, scale * image_accum)
    text_grad = unnormalize(uy, ry, scale * text_accum)
    loss = (stats[0] / total_texts).reshape(1)
    scale_grad = (scale * stats[1] / total_texts).reshape(1)
    bias_grad = (stats[2] / total_texts).reshape(1)
    return (image_grad, text_grad, loss, scale_grad, bias_grad)


def solution(mesh):
    fine = Mesh(mesh.devices.reshape(SIZES), AXES)
    split = P(AXES, None)
    return jax.shard_map(
        body,
        mesh=fine,
        in_specs=(split, split, P(), P(), P(), P()),
        out_specs=(split, split, P(), P(), P()),
        check_vma=False,
    )
```

time: 196 us -> 170 us (0.87)
  waiting for transfers between devices: 41.4 us -> 32.7 us
  other arithmetic: 13.1 us -> 4.59 us
  starting transfers between devices: 43.2 us -> 35.1 us
  matrix products: 12.1 us -> 7.26 us
  Pallas kernels: 0 us -> 4.47 us
    ppermute x7 -> x4, waiting for transfers between devices: 30.3 us -> 11.5 us  [shifted(): lax.ppermute(value, axis, [(i, (i + steps) % count) for i in range(count)])]
    all_to_all x3 -> x4, waiting for transfers between devices: 11.1 us -> 21.3 us  [swap(): return lax.all_to_all(value, axis, 0, 0, tiled=False)]
    ppermute x7 -> x4, starting transfers between devices: 23.3 us -> 13.2 us  [shifted(): lax.ppermute(value, axis, [(i, (i + steps) % count) for i in range(count)])]
    add x1 -> x0, other arithmetic: 7.6 us -> none  [body(): stats += jnp.stack([objective, jnp.sum(slope * dots), jnp.sum(slope)])]
    dot_general x10 -> x6, matrix products: 12.1 us -> 7.26 us  [the longest x1 2.97 us: body(): lax.dot_general(whole[:, :half], rows, (((0,), (0,)), ((), ())), preferre...]
    pallas_call x0 -> x1, Pallas kernels: none -> 4.47 us  [forward(): pl.pallas_call(forward_kernel, grid_spec=pltpu.PrefetchScalarGridSpec(num...]
    dynamic_slice x4 -> x1, local copies, waits for them, and re-layouts: 2.58 us -> 0.02 us  [body(): mine = lax.dynamic_index_in_dim(col_ids, core, 1, keepdims=False)]
    all_to_all x3 -> x4, starting transfers between devices: 19.9 us -> 21.9 us  [swap(): return lax.all_to_all(value, axis, 0, 0, tiled=False)]
  transfers between devices with their start and end apart: 10 -> 8, of which waited for: 6 -> 5; matrix products, arithmetic and copies ran while one was open for 9% -> 6% of each run, Pallas kernels for 0% -> 0%
where the time goes in v3:
time: 170 us; the launch traced here: 169 us
  blocking collectives  73.2 us (43%)
  starting transfers between devices  35.1 us (21%)
  waiting for transfers between devices  32.7 us (19%)
  between operations  7.54 us (4%)
  matrix products  7.26 us (4%)
  other arithmetic  4.59 us (3%)
  Pallas kernels  4.47 us (3%)
  local copies, waits for them, and re-layouts  3.94 us (2%)
    psum x3, blocking collectives, body(): stats = lax.psum(stats, axis)  46.8 us
    all_gather x1, blocking collectives, body(): cols = lax.all_gather(cols, Z + ('core',), axis=0, tiled=True)  26.4 us
    all_to_all x4, starting transfers between devices, swap(): return lax.all_to_all(value, axis, 0, 0, tiled=False)  21.9 us
    all_to_all x4, waiting for transfers between devices, swap(): return lax.all_to_all(value, axis, 0, 0, tiled=False)  21.3 us
    ppermute x4, starting transfers between devices, shifted(): lax.ppermute(value, axis, [(i, (i + steps) % count) for i in range(count)])  13.2 us
    ppermute x4, waiting for transfers between devices, shifted(): lax.ppermute(value, axis, [(i, (i + steps) % count) for i in range(count)])  11.5 us
    pallas_call x1, Pallas kernels, forward(): pl.pallas_call(forward_kernel, grid_spec=pltpu.PrefetchScalarGridSpec(num...  4.47 us
  transfers between devices with their start and end apart: 8, of which 5 were waited for; matrix products, arithmetic and copies ran while one was open for 6% of the time, Pallas kernels for 0%

profile of v3, /device:TPU:8, one launch (start us, length us, event | category | flops | bytes accessed | tf_op | source)
XLA Modules:
  0.0 168.8 jit_solution(9961624376710584693)
XLA Ops:
  0.7 1.0 fusion.13
  1.7 0.9 reduce-precision_convert_fusion
  3.4 9.2 %all-to-all-start = ((bf16[8,24,1152]{2,1,0:T(8,128)(2,1)}), bf16[8,24,1152]{2,1,0:T(8,128)(2,1)S(1)}, u32[]{:S(2)}, u32[]{:S(2)}) async-start(bf16[8,24,1152]{2,1,0:T(8,128)(2,1)} %broadcast_in_dim.4), calls=%async_computation | async-start | bytes 884736 | tf_op jit(solution)/shard_map/all_to_all | solution.py:26
  15.3 9.9 %all-to-all-done = bf16[8,24,1152]{2,1,0:T(8,128)(2,1)S(1)} async-done(((bf16[8,24,1152]{2,1,0:T(8,128)(2,1)}), bf16[8,24,1152]{2,1,0:T(8,128)(2,1)S(1)}, u32[]{:S(2)}, u32[]{:S(2)}) %all-to-all-start) | async-done | bytes 442400 | tf_op jit(solution)/shard_map/all_to_all | solution.py:26
  25.2 1.3 broadcast_in_dim.5
  26.5 4.3 %all-to-all-start.1 = ((bf16[4,192,1152]{2,1,0:T(8,128)(2,1)}), bf16[4,192,1152]{2,1,0:T(8,128)(2,1)S(1)}, u32[]{:S(2)}, u32[]{:S(2)}) async-start(bf16[4,192,1152]{2,1,0:T(8,128)(2,1)} %broadcast_in_dim.5), calls=%async_computation.1 | async-start | bytes 3538944 | tf_op jit(solution)/shard_map/all_to_all | solution.py:26
  30.8 26.4 %all-gather.1 = f16[512,1152]{1,0:T(8,128)(2,1)S(1)} all-gather(f16[32,1152]{1,0:T(8,128)(2,1)S(1)} %multiply_convert_fusion.2), channel_id=1, replica_groups=mesh['y'=8,'zh'=2,'zl'=4,'x'=4,'core'=2] {'zh','zl','core'}, dimensions={0}, use_global_device_ids=true | all-gather | bytes 1253376 | tf_op jit(solution)/shard_map/all_gather | solution.py:114
  57.7 4.5 %forward.1 = (bf16[768,512]{1,0:T(8,128)(2,1)S(1)}, bf16[768,512]{1,0:T(8,128)(2,1)S(1)}, f32[8,128]{1,0:T(8,128)S(1)}) custom-call(s32[1]{0:T(128)} %bitcast.place, f32[2]{0:T(128)S(1)} %pad_maximum_fusion.1.scalars, bf16[768,1152]{1,0:T(8,128)(2,1)S(1)} %bitcast.31, bf16[512,1152]{1,0:T(8,128)(2,1)S(1)} %bitcast.26, s32[768,1]{1,0:T(8,128)S(1)} %reshape.97.row_ids, ...), custom_call_target="tpu_custom_call" | custom-call | flops 1000000000 | bytes 5000000 | tf_op jit(solution)/shard_map/forward/pallas_call | solution.py:74
  63.4 3.9 %collective-permute-start = (f16[192,1152]{1,0:T(8,128)(2,1)S(1)}, f16[192,1152]{1,0:T(8,128)(2,1)S(1)}, u32[]{:S(2)}, u32[]{:S(2)}) collective-permute-start(f16[192,1152]{1,0:T(8,128)(2,1)S(1)} %fusion.2), channel_id=1, source_target_pairs={{0,2},{2,4},{4,6},{6,0},{1,3},{3,5},{5,7},{7,1},{8,10},{10,12},{12... | collective-permute-start | bytes 1327112 | tf_op jit(solution)/shard_map/ppermute | solution.py:31
  67.4 3.1 %collective-permute-start.1 = (f16[192,1152]{1,0:T(8,128)(2,1)S(1)}, f16[192,1152]{1,0:T(8,128)(2,1)S(1)}, u32[]{:S(2)}, u32[]{:S(2)}) collective-permute-start(f16[192,1152]{1,0:T(8,128)(2,1)S(1)} %fusion.3), channel_id=1, source_target_pairs={{0,6},{2,0},{4,2},{6,4},{1,7},{3,1},{5,3},{7,5},{8,14},{10,8},{12,... | collective-permute-start | bytes 1327112 | tf_op jit(solution)/shard_map/ppermute | solution.py:31
  70.5 4.2 %collective-permute-start.2 = (f16[192,1152]{1,0:T(8,128)(2,1)S(1)}, f16[192,1152]{1,0:T(8,128)(2,1)S(1)}, u32[]{:S(2)}, u32[]{:S(2)}) collective-permute-start(f16[192,1152]{1,0:T(8,128)(2,1)S(1)} %fusion.4), channel_id=1, source_target_pairs={{0,4},{2,6},{4,0},{6,2},{1,5},{3,7},{5,1},{7,3},{8,12},{10,14},{12... | collective-permute-start | bytes 1327112 | tf_op jit(solution)/shard_map/ppermute | solution.py:31
  74.7 1.8 %fusion.6 = f32[256,1152]{1,0:T(8,128)} fusion(bf16[768,1152]{1,0:T(8,128)(2,1)S(1)} %bitcast.32, bf16[768,512]{1,0:T(8,128)(2,1)S(1)} %get-tuple-element.13), kind=kOutput, calls=%fused_computation.18 | convolution fusion | flops 452984832 | bytes 3342336 | tf_op jit(solution)/shard_map/dot_general | solution.py:136
  76.5 1.9 %collective-permute-start.3 = (f32[256,1152]{1,0:T(8,128)}, f32[256,1152]{1,0:T(8,128)}, u32[]{:S(2)}, u32[]{:S(2)}) collective-permute-start(f32[256,1152]{1,0:T(8,128)} %fusion.6), channel_id=1, source_target_pairs={{0,1},{1,0},{2,3},{3,2},{4,5},{5,4},{6,7},{7,6},{8,9},{9,8},{10,11... | collective-permute-start | bytes 3538952 | tf_op jit(solution)/shard_map/ppermute | solution.py:31
  78.4 0.8 collective-permute-done
  79.3 3.0 %collective-permute-done.1 = f16[192,1152]{1,0:T(8,128)(2,1)S(1)} collective-permute-done((f16[192,1152]{1,0:T(8,128)(2,1)S(1)}, f16[192,1152]{1,0:T(8,128)(2,1)S(1)}, u32[]{:S(2)}, u32[]{:S(2)}) %collective-permute-start.1) | collective-permute-done | bytes 442400 | tf_op jit(solution)/shard_map/ppermute | solution.py:31
  82.3 7.6 %collective-permute-done.2 = f16[192,1152]{1,0:T(8,128)(2,1)S(1)} collective-permute-done((f16[192,1152]{1,0:T(8,128)(2,1)S(1)}, f16[192,1152]{1,0:T(8,128)(2,1)S(1)}, u32[]{:S(2)}, u32[]{:S(2)}) %collective-permute-start.2) | collective-permute-done | bytes 442400 | tf_op jit(solution)/shard_map/ppermute | solution.py:31
  89.9 1.2 multiply_convert_fusion.1
  91.1 4.8 %all-to-all-start.2 = ((f16[8,24,1152]{2,1,0:T(8,128)(2,1)}), f16[8,24,1152]{2,1,0:T(8,128)(2,1)S(1)}, u32[]{:S(2)}, u32[]{:S(2)}) async-start(f16[8,24,1152]{2,1,0:T(8,128)(2,1)} %bitcast.36), calls=%async_computation.2 | async-start | bytes 884736 | tf_op jit(solution)/shard_map/all_to_all | solution.py:26
  96.0 3.0 %fusion.1 = f16[256,1152]{1,0:T(8,128)(2,1)} fusion(f32[256,1152]{1,0:T(8,128)} %collective-permute-done.3, bf16[768,1152]{1,0:T(8,128)(2,1)S(1)} %bitcast.33, bf16[768,512]{1,0:T(8,128)(2,1)} %copy-done), kind=kOutput, calls=%fused_computation.6 | convolution fusion | flops 453869568 | bytes 3932160 | tf_op jit(solution)/shard_map/dot_general | solution.py:140
  99.0 11.3 %all-to-all-done.2 = f16[8,24,1152]{2,1,0:T(8,128)(2,1)S(1)} async-done(((f16[8,24,1152]{2,1,0:T(8,128)(2,1)}), f16[8,24,1152]{2,1,0:T(8,128)(2,1)S(1)}, u32[]{:S(2)}, u32[]{:S(2)}) %all-to-all-start.2) | async-done | bytes 442400 | tf_op jit(solution)/shard_map/all_to_all | solution.py:26
  110.3 3.5 %all-to-all-start.3 = ((f16[8,32,1152]{2,1,0:T(8,128)(2,1)}), f16[8,32,1152]{2,1,0:T(8,128)(2,1)S(1)}, u32[]{:S(2)}, u32[]{:S(2)}) async-start(f16[8,32,1152]{2,1,0:T(8,128)(2,1)} %bitcast.13), calls=%async_computation.3 | async-start | bytes 1179648 | tf_op jit(solution)/shard_map/all_to_all | solution.py:26
  113.9 12.6 %psum.21 = f32[3]{0:T(128)S(1)} all-reduce(f32[3]{0:T(128)S(1)} %slice_reduce_fusion), channel_id=1, replica_groups=mesh['y'=8,'zh'=2,'zl'=4,'x'=4,'core'=2] {'x','core'}, use_global_device_ids=true, to_apply=%region_6.7 | all-reduce | flops 3 | bytes 24 | tf_op jit(solution)/shard_map/psum | solution.py:156
  126.6 17.5 %psum.22 = f32[3]{0:T(128)S(1)} all-reduce(f32[3]{0:T(128)S(1)} %psum.21), channel_id=1, replica_groups=mesh['y'=8,'zh'=2,'zl'=4,'x'=4,'core'=2] {'zh','zl'}, use_global_device_ids=true, to_apply=%region_7.8 | all-reduce | flops 3 | bytes 24 | tf_op jit(solution)/shard_map/psum | solution.py:156
  144.1 16.7 %psum.23 = f32[3]{0:T(128)S(1)} all-reduce(f32[3]{0:T(128)S(1)} %psum.22), channel_id=1, replica_groups=mesh['y'=8,'zh'=2,'zl'=4,'x'=4,'core'=2] {'y'}, use_global_device_ids=true, to_apply=%region_8.9 | all-reduce | flops 3 | bytes 24 | tf_op jit(solution)/shard_map/psum | solution.py:156
  (41 shorter events, 6.6 us)
Async XLA Ops:
  0.6 13.3 %copy-start.1 = (bf16[32,1152]{1,0:T(8,128)(2,1)S(1)}, bf16[32,1152]{1,0:T(8,128)(2,1)}, u32[]{:S(2)}) copy-start(bf16[32,1152]{1,0:T(8,128)(2,1)} %param.7) | copy-start | bytes 221188
  0.6 13.4 %copy-start.4 = (s32[12288]{0:T(1024)S(1)}, s32[12288]{0:T(1024)}, u32[]{:S(2)}) copy-start(s32[12288]{0:T(1024)} %param.8) | copy-start | bytes 147460
  0.7 13.9 %copy-start.3 = (s32[16384]{0:T(1024)S(1)}, s32[16384]{0:T(1024)}, u32[]{:S(2)}) copy-start(s32[16384]{0:T(1024)} %param.9) | copy-start | bytes 196612
  3.4 21.8 %all-to-all-start = ((bf16[8,24,1152]{2,1,0:T(8,128)(2,1)}), bf16[8,24,1152]{2,1,0:T(8,128)(2,1)S(1)}, u32[]{:S(2)}, u32[]{:S(2)}) async-start(bf16[8,24,1152]{2,1,0:T(8,128)(2,1)} %broadcast_in_dim.4), calls=%async_computation | async-start | bytes 884736 | tf_op jit(solution)/shard_map/all_to_all | solution.py:26
  26.5 31.1 %all-to-all-start.1 = ((bf16[4,192,1152]{2,1,0:T(8,128)(2,1)}), bf16[4,192,1152]{2,1,0:T(8,128)(2,1)S(1)}, u32[]{:S(2)}, u32[]{:S(2)}) async-start(bf16[4,192,1152]{2,1,0:T(8,128)(2,1)} %broadcast_in_dim.5), calls=%async_computation.1 | async-start | bytes 3538944 | tf_op jit(solution)/shard_map/all_to_all | solution.py:26
  62.1 12.6 %copy-start = (bf16[768,512]{1,0:T(8,128)(2,1)}, bf16[768,512]{1,0:T(8,128)(2,1)S(1)}, u32[]{:S(2)}) copy-start(bf16[768,512]{1,0:T(8,128)(2,1)S(1)} %get-tuple-element.13) | copy-start | bytes 2359300
  63.4 15.8 %collective-permute-start = (f16[192,1152]{1,0:T(8,128)(2,1)S(1)}, f16[192,1152]{1,0:T(8,128)(2,1)S(1)}, u32[]{:S(2)}, u32[]{:S(2)}) collective-permute-start(f16[192,1152]{1,0:T(8,128)(2,1)S(1)} %fusion.2), channel_id=1, source_target_pairs={{0,2},{2,4},{4,6},{6,0},{1,3},{3,5},{5,7},{7,1},{8,10},{10,12},{12... | collective-permute-start | bytes 1327112 | tf_op jit(solution)/shard_map/ppermute | solution.py:31
  67.4 14.9 %collective-permute-start.1 = (f16[192,1152]{1,0:T(8,128)(2,1)S(1)}, f16[192,1152]{1,0:T(8,128)(2,1)S(1)}, u32[]{:S(2)}, u32[]{:S(2)}) collective-permute-start(f16[192,1152]{1,0:T(8,128)(2,1)S(1)} %fusion.3), channel_id=1, source_target_pairs={{0,6},{2,0},{4,2},{6,4},{1,7},{3,1},{5,3},{7,5},{8,14},{10,8},{12,... | collective-permute-start | bytes 1327112 | tf_op jit(solution)/shard_map/ppermute | solution.py:31
  70.5 19.4 %collective-permute-start.2 = (f16[192,1152]{1,0:T(8,128)(2,1)S(1)}, f16[192,1152]{1,0:T(8,128)(2,1)S(1)}, u32[]{:S(2)}, u32[]{:S(2)}) collective-permute-start(f16[192,1152]{1,0:T(8,128)(2,1)S(1)} %fusion.4), channel_id=1, source_target_pairs={{0,4},{2,6},{4,0},{6,2},{1,5},{3,7},{5,1},{7,3},{8,12},{10,14},{12... | collective-permute-start | bytes 1327112 | tf_op jit(solution)/shard_map/ppermute | solution.py:31
  76.5 19.5 %collective-permute-start.3 = (f32[256,1152]{1,0:T(8,128)}, f32[256,1152]{1,0:T(8,128)}, u32[]{:S(2)}, u32[]{:S(2)}) collective-permute-start(f32[256,1152]{1,0:T(8,128)} %fusion.6), channel_id=1, source_target_pairs={{0,1},{1,0},{2,3},{3,2},{4,5},{5,4},{6,7},{7,6},{8,9},{9,8},{10,11... | collective-permute-start | bytes 3538952 | tf_op jit(solution)/shard_map/ppermute | solution.py:31
  91.1 19.1 %all-to-all-start.2 = ((f16[8,24,1152]{2,1,0:T(8,128)(2,1)}), f16[8,24,1152]{2,1,0:T(8,128)(2,1)S(1)}, u32[]{:S(2)}, u32[]{:S(2)}) async-start(f16[8,24,1152]{2,1,0:T(8,128)(2,1)} %bitcast.36), calls=%async_computation.2 | async-start | bytes 884736 | tf_op jit(solution)/shard_map/all_to_all | solution.py:26
  99.0 64.4 %copy-start.2 = (bf16[24,1152]{1,0:T(8,128)(2,1)S(1)}, bf16[24,1152]{1,0:T(8,128)(2,1)}, u32[]{:S(2)}) copy-start(bf16[24,1152]{1,0:T(8,128)(2,1)} %param.6) | copy-start | bytes 165892
  110.3 54.0 %all-to-all-start.3 = ((f16[8,32,1152]{2,1,0:T(8,128)(2,1)}), f16[8,32,1152]{2,1,0:T(8,128)(2,1)S(1)}, u32[]{:S(2)}, u32[]{:S(2)}) async-start(f16[8,32,1152]{2,1,0:T(8,128)(2,1)} %bitcast.13), calls=%async_computation.3 | async-start | bytes 1179648 | tf_op jit(solution)/shard_map/all_to_all | solution.py:26

commit v4 on v2

v4 whole, which is shorter than its diff:
```python
import jax
import jax.numpy as jnp
from jax import lax
from jax.experimental import pallas as pl
from jax.experimental.pallas import tpu as pltpu
from jax.sharding import Mesh, PartitionSpec as P

AXES = ("y", "zh", "zl", "x", "core")
SIZES = (8, 2, 4, 4, 2)
Z = ("zh", "zl")
UNIT = 16384.0


def normalize(rows):
    values = rows.astype(jnp.float32)
    radius = jnp.sqrt(jnp.sum(values * values, -1, keepdims=True) + 1e-06)
    unit = values / radius
    return (unit, radius, lax.reduce_precision(unit, 8, 7))


def unnormalize(unit, radius, grad):
    return (grad - unit * jnp.sum(unit * grad, -1, keepdims=True)) / radius


def swap(value, axis):
    return lax.all_to_all(value, axis, 0, 0, tiled=False)


def shifted(value, axis, steps):
    count = lax.axis_size(axis)
    return lax.ppermute(value, axis, [(i, (i + steps) % count) for i in range(count)])


def spread(block, axis):
    count = lax.axis_size(axis)
    return swap(jnp.broadcast_to(block[None], (count,) + block.shape), axis)


def pairs_kernel(place, scalars, rows, cols, row_ids, col_ids, slopes, theirs, mine):
    parts = 4
    high = rows.shape[0] // parts
    half = mine.shape[0]
    sums = [0.0, 0.0, 0.0]
    for k in range(parts):
        part = pl.ds(pl.multiple_of(lax.rem(place[0] + k, parts) * high, high), high)
        dots = lax.dot_general(
            rows[part, :], cols[...], (((1,), (1,)), ((), ())), preferred_element_type=jnp.float32
        )
        logits = scalars[0] * dots + scalars[1]
        match = row_ids[part, :] == col_ids[...]
        against = jnp.where(match, -logits, logits)
        decay = jnp.exp(-jnp.abs(against))
        objective = jnp.maximum(against, 0.0) + jnp.log1p(decay)
        weight = jnp.where(against >= 0.0, 1.0, decay) / (1.0 + decay)
        slope = jnp.where(match, -weight, weight)
        slopeb = slope.astype(jnp.bfloat16)
        slopes[k * high : (k + 1) * high, :] = slopeb
        for side, out in ((slopeb[:, :half], mine), (slopeb[:, half:], theirs)):
            product = lax.dot_general(
                side, rows[part, :], (((0,), (0,)), ((), ())), preferred_element_type=jnp.float32
            )
            out[:half, :] = product if k == 0 else out[:half, :] + product
        for i, term in enumerate((objective, slope * dots, slope)):
            sums[i] += jnp.sum(term, 0, keepdims=True)
    lane = lax.broadcasted_iota(jnp.int32, (8, theirs.shape[1]), 1)
    totals = jnp.zeros(lane.shape, jnp.float32)
    for i in range(3):
        totals = jnp.where(lane == i, jnp.sum(sums[i], 1, keepdims=True), totals)
    theirs[half:, :] = totals


def pairs(x, scalars, rows, cols, row_ids, col_ids):
    wide, width = cols.shape
    half = wide // 2
    vmem = pl.BlockSpec(memory_space=pltpu.VMEM)
    smem = pl.BlockSpec(memory_space=pltpu.SMEM)
    return pl.pallas_call(
        pairs_kernel,
        in_specs=[smem, smem, vmem, vmem, vmem, vmem],
        out_specs=[vmem, vmem, vmem],
        out_shape=(
            jax.ShapeDtypeStruct((rows.shape[0], wide), jnp.bfloat16),
            jax.ShapeDtypeStruct((half + 8, width), jnp.float32),
            jax.ShapeDtypeStruct((half, width), jnp.float32),
        ),
        compiler_params=pltpu.CompilerParams(vmem_limit_bytes=48 * 2**20),
        cost_estimate=pl.CostEstimate(flops=2 * 10**9, bytes_accessed=6 * 10**6, transcendentals=10**6),
        name="pairs",
    )(x.reshape(1).astype(jnp.int32), scalars, rows, cols, row_ids, col_ids)


def swap_sum(blocks, stats, axis):
    count, high, width = blocks.shape
    rider = jnp.concatenate(half_pieces(stats * (1 / 2048.0)) + [jnp.zeros((high - 3, 128), jnp.float16)], 0)
    rider = jnp.broadcast_to(rider[None], (count, high, 128))
    got = swap(jnp.concatenate([blocks, rider], 2), axis)
    stats = jnp.sum(got[:, :3, width:].astype(jnp.float32), (0, 1)).reshape(1, 128) * 2048.0
    return (jnp.sum(got[:, :, :width].astype(jnp.float32), 0), stats)


def half_pieces(value):
    pieces = []
    for _ in range(3):
        piece = lax.reduce_precision(value, 5, 10)
        pieces.append(piece.astype(jnp.float16))
        value = value - piece
    return pieces


def body(images, texts, image_ids, text_ids, log_scale, bias):
    width = images.shape[1]
    img_rows = images.shape[0]
    txt_rows = texts.shape[0]
    y, x, core = (lax.axis_index(a) for a in ("y", "x", "core"))
    z = lax.axis_index(Z)
    scale = jnp.exp(log_scale[0])
    ux, rx, uxb = normalize(images)
    uy, ry, uyb = normalize(texts)

    own = spread(uxb.astype(jnp.bfloat16), "y").reshape(-1, width)
    cols = (uyb * UNIT).astype(jnp.float16)
    own, cols = lax.optimization_barrier((own, cols))
    rows = spread(own, "x").reshape(-1, width)
    cols = lax.all_gather(cols, Z + ("core",), axis=0, tiled=True)
    cols = (cols.astype(jnp.float32) * (1 / UNIT)).astype(jnp.bfloat16)
    cols = cols.reshape(8, 2, txt_rows, width)
    mine = lax.dynamic_index_in_dim(cols, core, 1, keepdims=False)
    theirs = lax.dynamic_index_in_dim(cols, 1 - core, 1, keepdims=False)
    cols = jnp.concatenate([mine, theirs], 0).reshape(-1, width)

    col_ids = text_ids.reshape(8, 8, 4, 2, txt_rows)
    col_ids = lax.dynamic_index_in_dim(col_ids, y, 0, keepdims=False)
    col_ids = lax.dynamic_index_in_dim(col_ids, x, 1, keepdims=False)
    mine = lax.dynamic_index_in_dim(col_ids, core, 1, keepdims=False)
    theirs = lax.dynamic_index_in_dim(col_ids, 1 - core, 1, keepdims=False)
    col_ids = jnp.concatenate([mine, theirs], 0).reshape(1, -1)
    row_ids = image_ids.reshape(8, 8, 4, 2, img_rows)
    row_ids = lax.dynamic_index_in_dim(row_ids, z, 1, keepdims=False)
    row_ids = lax.dynamic_index_in_dim(row_ids, core, 2, keepdims=False)
    row_ids = row_ids.transpose(1, 0, 2).reshape(-1, 1)

    half = cols.shape[0] // 2
    high = rows.shape[0] // 4
    near, theirs, mine = pairs(x, jnp.stack([scale, bias[0]]), rows, cols, row_ids, col_ids)
    stats = theirs[half : half + 1, :128]

    dcols = shifted(theirs[:half], "core", 1) + mine
    stats = stats + shifted(stats, "core", 1)
    dcols, stats = swap_sum((dcols * 32.0).astype(jnp.float16).reshape(8, txt_rows, width), stats, Z)

    back = {}
    for k in (2, 1, 3, 0):
        drows = 64.0 * jnp.dot(near[k * high : (k + 1) * high], cols, preferred_element_type=jnp.float32)
        back[k] = shifted(drows.astype(jnp.float16), "x", k) if k else drows
    drows = sum(part.astype(jnp.float32) for part in back.values())
    drows = (drows * 0.25).astype(jnp.float16).reshape(8, -1, width)
    drows, stats = swap_sum(drows, stats, "y")
    for steps in (1, 2):
        stats = stats + shifted(stats, "x", steps)
    stats = stats[0]

    total_texts = txt_rows * 512
    image_accum = drows * 0.0625
    text_accum = dcols * (1 / 32.0)
    image_grad = unnormalize(ux, rx, scale * image_accum)
    text_grad = unnormalize(uy, ry, scale * text_accum)
    loss = (stats[0] / total_texts).reshape(1)
    scale_grad = (scale * stats[1] / total_texts).reshape(1)
    bias_grad = (stats[2] / total_texts).reshape(1)
    return (image_grad, text_grad, loss, scale_grad, bias_grad)


def solution(mesh):
    fine = Mesh(mesh.devices.reshape(SIZES), AXES)
    split = P(AXES, None)
    return jax.shard_map(
        body,
        mesh=fine,
        in_specs=(split, split, P(), P(), P(), P()),
        out_specs=(split, split, P(), P(), P()),
        check_vma=False,
    )
```

time: 196 us -> 146 us (0.74)
  the two profiles are of different devices: /device:TPU:8 before, /device:TPU:1 now
where the time goes in v4:
time: 146 us; the launch traced here: 145 us
  waiting for transfers between devices  48.4 us (33%)
  starting transfers between devices  41.8 us (29%)
  blocking collectives  27.5 us (19%)
  between operations  7.6 us (5%)
  other arithmetic  6.96 us (5%)
  Pallas kernels  6.51 us (4%)
  local copies, waits for them, and re-layouts  4.13 us (3%)
  matrix products  1.78 us (1%)
    all_gather x1, blocking collectives, body(): cols = lax.all_gather(cols, Z + ('core',), axis=0, tiled=True)  27.5 us
    all_to_all x4, waiting for transfers between devices, swap(): return lax.all_to_all(value, axis, 0, 0, tiled=False)  26.1 us
    all_to_all x4, starting transfers between devices, swap(): return lax.all_to_all(value, axis, 0, 0, tiled=False)  24.3 us
    ppermute x7, waiting for transfers between devices, shifted(): lax.ppermute(value, axis, [(i, (i + steps) % count) for i in range(count)])  22.3 us
    ppermute x7, starting transfers between devices, shifted(): lax.ppermute(value, axis, [(i, (i + steps) % count) for i in range(count)])  17.5 us
    pallas_call x1, Pallas kernels, pairs(): pl.pallas_call(pairs_kernel, in_specs=[smem, smem, vmem, vmem, vmem, vmem...  6.51 us
  transfers between devices with their start and end apart: 11, of which 7 were waited for; matrix products, arithmetic and copies ran while one was open for 4% of the time, Pallas kernels for 0%

profile of v4, /device:TPU:1, one launch (start us, length us, event | category | flops | bytes accessed | tf_op | source)
XLA Modules:
  0.0 144.7 jit_solution(8938133595853330717)
XLA Ops:
  0.7 1.0 fusion.8
  1.7 0.9 reduce-precision_convert_fusion
  3.3 7.7 %all-to-all-start = ((bf16[8,24,1152]{2,1,0:T(8,128)(2,1)}), bf16[8,24,1152]{2,1,0:T(8,128)(2,1)S(1)}, u32[]{:S(2)}, u32[]{:S(2)}) async-start(bf16[8,24,1152]{2,1,0:T(8,128)(2,1)} %broadcast_in_dim.12), calls=%async_computation | async-start | bytes 884736 | tf_op jit(solution)/shard_map/all_to_all | solution.py:26
  13.7 10.0 %all-to-all-done = bf16[8,24,1152]{2,1,0:T(8,128)(2,1)S(1)} async-done(((bf16[8,24,1152]{2,1,0:T(8,128)(2,1)}), bf16[8,24,1152]{2,1,0:T(8,128)(2,1)S(1)}, u32[]{:S(2)}, u32[]{:S(2)}) %all-to-all-start) | async-done | bytes 442400 | tf_op jit(solution)/shard_map/all_to_all | solution.py:26
  23.7 1.3 broadcast_in_dim.13
  25.0 7.1 %all-to-all-start.1 = ((bf16[4,192,1152]{2,1,0:T(8,128)(2,1)}), bf16[4,192,1152]{2,1,0:T(8,128)(2,1)}, u32[]{:S(2)}, u32[]{:S(2)}) async-start(bf16[4,192,1152]{2,1,0:T(8,128)(2,1)} %broadcast_in_dim.13), calls=%async_computation.1 | async-start | bytes 3538944 | tf_op jit(solution)/shard_map/all_to_all | solution.py:26
  32.2 27.5 %all-gather.1 = f16[512,1152]{1,0:T(8,128)(2,1)S(1)} all-gather(f16[32,1152]{1,0:T(8,128)(2,1)S(1)} %multiply_convert_fusion.3), channel_id=1, replica_groups=mesh['y'=8,'zh'=2,'zl'=4,'x'=4,'core'=2] {'zh','zl','core'}, dimensions={0}, use_global_device_ids=true | all-gather | bytes 1253376 | tf_op jit(solution)/shard_map/all_gather | solution.py:124
  60.1 6.5 %pairs.1 = (bf16[768,512]{1,0:T(8,128)(2,1)S(1)}, f32[264,1152]{1,0:T(8,128)S(1)}, f32[256,1152]{1,0:T(8,128)S(1)}) custom-call(s32[1]{0:T(128)} %bitcast.place, f32[2]{0:T(128)S(1)} %pad_maximum_fusion.3.scalars, bf16[768,1152]{1,0:T(8,128)(2,1)} %bitcast.2.rows, bf16[512,1152]{1,0:T(8,128)(2,1)S(1)} %bitcast.38, s32[768,1]{1,0:T(8,128)S(1)} %reshape.163.row_ids, ...), custom_call_target="tpu_custom_call" | custom-call | flops 2000000000 | bytes 6000000 | tf_op jit(solution)/shard_map/pairs/pallas_call | solution.py:77
  66.7 2.1 %collective-permute-start.3 = (f32[256,1152]{1,0:T(8,128)S(1)}, f32[256,1152]{1,0:T(8,128)S(1)}, u32[]{:S(2)}, u32[]{:S(2)}) collective-permute-start(f32[256,1152]{1,0:T(8,128)S(1)} %slice.46), channel_id=1, source_target_pairs={{0,1},{1,0},{2,3},{3,2},{4,5},{5,4},{6,7},{7,6},{8,9},{9,8},{10,11... | collective-permute-start | bytes 3538952 | tf_op jit(solution)/shard_map/ppermute | solution.py:31
  68.9 2.2 %collective-permute-start.4 = (f32[1,128]{1,0:T(1,128)S(1)}, f32[1,128]{1,0:T(1,128)S(1)}, u32[]{:S(2)}, u32[]{:S(2)}) collective-permute-start(f32[1,128]{1,0:T(1,128)S(1)} %slice.47), channel_id=1, source_target_pairs={{0,1},{1,0},{2,3},{3,2},{4,5},{5,4},{6,7},{7,6},{8,9},{9,8},{10,11... | collective-permute-start | bytes 1544 | tf_op jit(solution)/shard_map/ppermute | solution.py:31
  72.3 1.0 pad_maximum_fusion.1
  73.3 6.1 %all-to-all-start.2 = ((f16[8,32,1280]{2,1,0:T(8,128)(2,1)}), f16[8,32,1280]{2,1,0:T(8,128)(2,1)S(1)}, u32[]{:S(2)}, u32[]{:S(2)}) async-start(f16[8,32,1280]{2,1,0:T(8,128)(2,1)} %pad_maximum_fusion.1), calls=%async_computation.2 | async-start | bytes 1310720 | tf_op jit(solution)/shard_map/all_to_all | solution.py:26
  80.2 2.6 %collective-permute-start = (f16[192,1152]{1,0:T(8,128)(2,1)S(1)}, f16[192,1152]{1,0:T(8,128)(2,1)S(1)}, u32[]{:S(2)}, u32[]{:S(2)}) collective-permute-start(f16[192,1152]{1,0:T(8,128)(2,1)S(1)} %fusion), channel_id=1, source_target_pairs={{0,4},{2,6},{4,0},{6,2},{1,5},{3,7},{5,1},{7,3},{8,12},{10,14},{12... | collective-permute-start | bytes 1327112 | tf_op jit(solution)/shard_map/ppermute | solution.py:31
  82.8 2.7 %collective-permute-start.1 = (f16[192,1152]{1,0:T(8,128)(2,1)S(1)}, f16[192,1152]{1,0:T(8,128)(2,1)S(1)}, u32[]{:S(2)}, u32[]{:S(2)}) collective-permute-start(f16[192,1152]{1,0:T(8,128)(2,1)S(1)} %fusion.1), channel_id=1, source_target_pairs={{0,2},{2,4},{4,6},{6,0},{1,3},{3,5},{5,7},{7,1},{8,10},{10,12},{12... | collective-permute-start | bytes 1327112 | tf_op jit(solution)/shard_map/ppermute | solution.py:31
  85.5 3.8 %collective-permute-start.2 = (f16[192,1152]{1,0:T(8,128)(2,1)S(1)}, f16[192,1152]{1,0:T(8,128)(2,1)S(1)}, u32[]{:S(2)}, u32[]{:S(2)}) collective-permute-start(f16[192,1152]{1,0:T(8,128)(2,1)S(1)} %fusion.2), channel_id=1, source_target_pairs={{0,6},{2,0},{4,2},{6,4},{1,7},{3,1},{5,3},{7,5},{8,14},{10,8},{12,... | collective-permute-start | bytes 1327112 | tf_op jit(solution)/shard_map/ppermute | solution.py:31
  89.4 5.5 %collective-permute-done = f16[192,1152]{1,0:T(8,128)(2,1)S(1)} collective-permute-done((f16[192,1152]{1,0:T(8,128)(2,1)S(1)}, f16[192,1152]{1,0:T(8,128)(2,1)S(1)}, u32[]{:S(2)}, u32[]{:S(2)}) %collective-permute-start) | collective-permute-done | bytes 442400 | tf_op jit(solution)/shard_map/ppermute | solution.py:31
  94.9 10.3 %collective-permute-done.1 = f16[192,1152]{1,0:T(8,128)(2,1)S(1)} collective-permute-done((f16[192,1152]{1,0:T(8,128)(2,1)S(1)}, f16[192,1152]{1,0:T(8,128)(2,1)S(1)}, u32[]{:S(2)}, u32[]{:S(2)}) %collective-permute-start.1) | collective-permute-done | bytes 442400 | tf_op jit(solution)/shard_map/ppermute | solution.py:31
  105.8 0.9 pad_maximum_fusion.2
  106.7 3.5 %all-to-all-start.3 = ((f16[8,24,1280]{2,1,0:T(8,128)(2,1)}), f16[8,24,1280]{2,1,0:T(8,128)(2,1)S(1)}, u32[]{:S(2)}, u32[]{:S(2)}) async-start(f16[8,24,1280]{2,1,0:T(8,128)(2,1)} %pad_maximum_fusion.2), calls=%async_computation.3 | async-start | bytes 983040 | tf_op jit(solution)/shard_map/all_to_all | solution.py:26
  111.3 16.1 %all-to-all-done.3 = f16[8,24,1280]{2,1,0:T(8,128)(2,1)S(1)} async-done(((f16[8,24,1280]{2,1,0:T(8,128)(2,1)}), f16[8,24,1280]{2,1,0:T(8,128)(2,1)S(1)}, u32[]{:S(2)}, u32[]{:S(2)}) %all-to-all-start.3) | async-done | bytes 491552 | tf_op jit(solution)/shard_map/all_to_all | solution.py:26
  127.4 2.2 %collective-permute-start.5 = (f32[1,128]{1,0:T(1,128)S(1)}, f32[1,128]{1,0:T(1,128)S(1)}, u32[]{:S(2)}, u32[]{:S(2)}) collective-permute-start(f32[1,128]{1,0:T(1,128)S(1)} %multiply_bitcast_fusion), channel_id=1, source_target_pairs={{0,2},{2,4},{4,6},{6,0},{1,3},{3,5},{5,7},{7,1},{8,10},{10,12},{12... | collective-permute-start | bytes 1544 | tf_op jit(solution)/shard_map/ppermute | solution.py:31
  129.9 3.0 %collective-permute-done.5 = f32[1,128]{1,0:T(1,128)S(1)} collective-permute-done((f32[1,128]{1,0:T(1,128)S(1)}, f32[1,128]{1,0:T(1,128)S(1)}, u32[]{:S(2)}, u32[]{:S(2)}) %collective-permute-start.5) | collective-permute-done | bytes 544 | tf_op jit(solution)/shard_map/ppermute | solution.py:31
  132.9 1.9 %collective-permute-start.6 = (f32[1,128]{1,0:T(1,128)S(1)}, f32[1,128]{1,0:T(1,128)S(1)}, u32[]{:S(2)}, u32[]{:S(2)}) collective-permute-start(f32[1,128]{1,0:T(1,128)S(1)} %fusion.13), channel_id=1, source_target_pairs={{0,4},{2,6},{4,0},{6,2},{1,5},{3,7},{5,1},{7,3},{8,12},{10,14},{12... | collective-permute-start | bytes 1544 | tf_op jit(solution)/shard_map/ppermute | solution.py:31
  135.6 3.1 %collective-permute-done.6 = f32[1,128]{1,0:T(1,128)S(1)} collective-permute-done((f32[1,128]{1,0:T(1,128)S(1)}, f32[1,128]{1,0:T(1,128)S(1)}, u32[]{:S(2)}, u32[]{:S(2)}) %collective-permute-start.6) | collective-permute-done | bytes 544 | tf_op jit(solution)/shard_map/ppermute | solution.py:31
  (60 shorter events, 8.1 us)
Async XLA Ops:
  0.6 10.4 %copy-start.2 = (s32[16384]{0:T(1024)S(1)}, s32[16384]{0:T(1024)}, u32[]{:S(2)}) copy-start(s32[16384]{0:T(1024)} %param.9) | copy-start | bytes 196612
  0.6 10.7 %copy-start = (bf16[32,1152]{1,0:T(8,128)(2,1)S(1)}, bf16[32,1152]{1,0:T(8,128)(2,1)}, u32[]{:S(2)}) copy-start(bf16[32,1152]{1,0:T(8,128)(2,1)} %param.7) | copy-start | bytes 221188
  0.7 10.9 %copy-start.3 = (s32[12288]{0:T(1024)S(1)}, s32[12288]{0:T(1024)}, u32[]{:S(2)}) copy-start(s32[12288]{0:T(1024)} %param.8) | copy-start | bytes 147460
  3.3 20.4 %all-to-all-start = ((bf16[8,24,1152]{2,1,0:T(8,128)(2,1)}), bf16[8,24,1152]{2,1,0:T(8,128)(2,1)S(1)}, u32[]{:S(2)}, u32[]{:S(2)}) async-start(bf16[8,24,1152]{2,1,0:T(8,128)(2,1)} %broadcast_in_dim.12), calls=%async_computation | async-start | bytes 884736 | tf_op jit(solution)/shard_map/all_to_all | solution.py:26
  25.0 35.1 %all-to-all-start.1 = ((bf16[4,192,1152]{2,1,0:T(8,128)(2,1)}), bf16[4,192,1152]{2,1,0:T(8,128)(2,1)}, u32[]{:S(2)}, u32[]{:S(2)}) async-start(bf16[4,192,1152]{2,1,0:T(8,128)(2,1)} %broadcast_in_dim.13), calls=%async_computation.1 | async-start | bytes 3538944 | tf_op jit(solution)/shard_map/all_to_all | solution.py:26
  66.7 5.4 %collective-permute-start.3 = (f32[256,1152]{1,0:T(8,128)S(1)}, f32[256,1152]{1,0:T(8,128)S(1)}, u32[]{:S(2)}, u32[]{:S(2)}) collective-permute-start(f32[256,1152]{1,0:T(8,128)S(1)} %slice.46), channel_id=1, source_target_pairs={{0,1},{1,0},{2,3},{3,2},{4,5},{5,4},{6,7},{7,6},{8,9},{9,8},{10,11... | collective-permute-start | bytes 3538952 | tf_op jit(solution)/shard_map/ppermute | solution.py:31
  68.9 3.0 %collective-permute-start.4 = (f32[1,128]{1,0:T(1,128)S(1)}, f32[1,128]{1,0:T(1,128)S(1)}, u32[]{:S(2)}, u32[]{:S(2)}) collective-permute-start(f32[1,128]{1,0:T(1,128)S(1)} %slice.47), channel_id=1, source_target_pairs={{0,1},{1,0},{2,3},{3,2},{4,5},{5,4},{6,7},{7,6},{8,9},{9,8},{10,11... | collective-permute-start | bytes 1544 | tf_op jit(solution)/shard_map/ppermute | solution.py:31
  73.3 32.4 %all-to-all-start.2 = ((f16[8,32,1280]{2,1,0:T(8,128)(2,1)}), f16[8,32,1280]{2,1,0:T(8,128)(2,1)S(1)}, u32[]{:S(2)}, u32[]{:S(2)}) async-start(f16[8,32,1280]{2,1,0:T(8,128)(2,1)} %pad_maximum_fusion.1), calls=%async_computation.2 | async-start | bytes 1310720 | tf_op jit(solution)/shard_map/all_to_all | solution.py:26
  80.2 14.7 %collective-permute-start = (f16[192,1152]{1,0:T(8,128)(2,1)S(1)}, f16[192,1152]{1,0:T(8,128)(2,1)S(1)}, u32[]{:S(2)}, u32[]{:S(2)}) collective-permute-start(f16[192,1152]{1,0:T(8,128)(2,1)S(1)} %fusion), channel_id=1, source_target_pairs={{0,4},{2,6},{4,0},{6,2},{1,5},{3,7},{5,1},{7,3},{8,12},{10,14},{12... | collective-permute-start | bytes 1327112 | tf_op jit(solution)/shard_map/ppermute | solution.py:31
  82.8 22.4 %collective-permute-start.1 = (f16[192,1152]{1,0:T(8,128)(2,1)S(1)}, f16[192,1152]{1,0:T(8,128)(2,1)S(1)}, u32[]{:S(2)}, u32[]{:S(2)}) collective-permute-start(f16[192,1152]{1,0:T(8,128)(2,1)S(1)} %fusion.1), channel_id=1, source_target_pairs={{0,2},{2,4},{4,6},{6,0},{1,3},{3,5},{5,7},{7,1},{8,10},{10,12},{12... | collective-permute-start | bytes 1327112 | tf_op jit(solution)/shard_map/ppermute | solution.py:31
  85.5 19.7 %collective-permute-start.2 = (f16[192,1152]{1,0:T(8,128)(2,1)S(1)}, f16[192,1152]{1,0:T(8,128)(2,1)S(1)}, u32[]{:S(2)}, u32[]{:S(2)}) collective-permute-start(f16[192,1152]{1,0:T(8,128)(2,1)S(1)} %fusion.2), channel_id=1, source_target_pairs={{0,6},{2,0},{4,2},{6,4},{1,7},{3,1},{5,3},{7,5},{8,14},{10,8},{12,... | collective-permute-start | bytes 1327112 | tf_op jit(solution)/shard_map/ppermute | solution.py:31
  106.7 20.7 %all-to-all-start.3 = ((f16[8,24,1280]{2,1,0:T(8,128)(2,1)}), f16[8,24,1280]{2,1,0:T(8,128)(2,1)S(1)}, u32[]{:S(2)}, u32[]{:S(2)}) async-start(f16[8,24,1280]{2,1,0:T(8,128)(2,1)} %pad_maximum_fusion.2), calls=%async_computation.3 | async-start | bytes 983040 | tf_op jit(solution)/shard_map/all_to_all | solution.py:26
  110.2 19.5 %copy-start.1 = (bf16[24,1152]{1,0:T(8,128)(2,1)S(1)}, bf16[24,1152]{1,0:T(8,128)(2,1)}, u32[]{:S(2)}) copy-start(bf16[24,1152]{1,0:T(8,128)(2,1)} %param.6) | copy-start | bytes 165892
  127.4 5.5 %collective-permute-start.5 = (f32[1,128]{1,0:T(1,128)S(1)}, f32[1,128]{1,0:T(1,128)S(1)}, u32[]{:S(2)}, u32[]{:S(2)}) collective-permute-start(f32[1,128]{1,0:T(1,128)S(1)} %multiply_bitcast_fusion), channel_id=1, source_target_pairs={{0,2},{2,4},{4,6},{6,0},{1,3},{3,5},{5,7},{7,1},{8,10},{10,12},{12... | collective-permute-start | bytes 1544 | tf_op jit(solution)/shard_map/ppermute | solution.py:31
  132.9 5.8 %collective-permute-start.6 = (f32[1,128]{1,0:T(1,128)S(1)}, f32[1,128]{1,0:T(1,128)S(1)}, u32[]{:S(2)}, u32[]{:S(2)}) collective-permute-start(f32[1,128]{1,0:T(1,128)S(1)} %fusion.13), channel_id=1, source_target_pairs={{0,4},{2,6},{4,0},{6,2},{1,5},{3,7},{5,1},{7,3},{8,12},{10,14},{12... | collective-permute-start | bytes 1544 | tf_op jit(solution)/shard_map/ppermute | solution.py:31

commit v5 on v4

--- a/solution.py
+++ b/solution.py
@@ -36,10 +36,9 @@
     return swap(jnp.broadcast_to(block[None], (count,) + block.shape), axis)
 
 
-def pairs_kernel(place, scalars, rows, cols, row_ids, col_ids, slopes, theirs, mine):
+def slopes_kernel(place, scalars, rows, cols, row_ids, col_ids, slopes, totals):
     parts = 4
     high = rows.shape[0] // parts
-    half = mine.shape[0]
     sums = [0.0, 0.0, 0.0]
     for k in range(parts):
         part = pl.ds(pl.multiple_of(lax.rem(place[0] + k, parts) * high, high), high)
@@ -53,40 +52,67 @@
         objective = jnp.maximum(against, 0.0) + jnp.log1p(decay)
         weight = jnp.where(against >= 0.0, 1.0, decay) / (1.0 + decay)
         slope = jnp.where(match, -weight, weight)
-        slopeb = slope.astype(jnp.bfloat16)
-        slopes[k * high : (k + 1) * high, :] = slopeb
-        for side, out in ((slopeb[:, :half], mine), (slopeb[:, half:], theirs)):
+        slopes[k * high : (k + 1) * high, :] = slope.astype(jnp.bfloat16)
+        for i, term in enumerate((objective, slope * dots, slope)):
+            sums[i] += jnp.sum(term, 0, keepdims=True)
+    lane = lax.broadcasted_iota(jnp.int32, totals.shape, 1)
+    total = jnp.zeros(totals.shape, jnp.float32)
+    for i in range(3):
+        total = jnp.where(lane == i, jnp.sum(sums[i], 1, keepdims=True), total)
+    totals[...] = total
+
+
+def text_kernel(place, rows, slopes, totals, theirs, mine):
+    parts = 4
+    high = rows.shape[0] // parts
+    half = mine.shape[0]
+    for side, out in ((slice(half, None), theirs), (slice(0, half), mine)):
+        for k in range(parts):
+            part = pl.ds(pl.multiple_of(lax.rem(place[0] + k, parts) * high, high), high)
             product = lax.dot_general(
-                side, rows[part, :], (((0,), (0,)), ((), ())), preferred_element_type=jnp.float32
+                slopes[k * high : (k + 1) * high, side],
+                rows[part, :],
+                (((0,), (0,)), ((), ())),
+                preferred_element_type=jnp.float32,
             )
             out[:half, :] = product if k == 0 else out[:half, :] + product
-        for i, term in enumerate((objective, slope * dots, slope)):
-            sums[i] += jnp.sum(term, 0, keepdims=True)
-    lane = lax.broadcasted_iota(jnp.int32, (8, theirs.shape[1]), 1)
-    totals = jnp.zeros(lane.shape, jnp.float32)
-    for i in range(3):
-        totals = jnp.where(lane == i, jnp.sum(sums[i], 1, keepdims=True), totals)
-    theirs[half:, :] = totals
-
-
-def pairs(x, scalars, rows, cols, row_ids, col_ids):
+    theirs[half:, :] = totals[...]
+
+
+VMEM = pl.BlockSpec(memory_space=pltpu.VMEM)
+SMEM = pl.BlockSpec(memory_space=pltpu.SMEM)
+
+
+def slopes_of(place, scalars, rows, cols, row_ids, col_ids):
     wide, width = cols.shape
-    half = wide // 2
-    vmem = pl.BlockSpec(memory_space=pltpu.VMEM)
-    smem = pl.BlockSpec(memory_space=pltpu.SMEM)
     return pl.pallas_call(
-        pairs_kernel,
-        in_specs=[smem, smem, vmem, vmem, vmem, vmem],
-        out_specs=[vmem, vmem, vmem],
+        slopes_kernel,
+        in_specs=[SMEM, SMEM, VMEM, VMEM, VMEM, VMEM],
+        out_specs=[VMEM, VMEM],
         out_shape=(
             jax.ShapeDtypeStruct((rows.shape[0], wide), jnp.bfloat16),
+            jax.ShapeDtypeStruct((8, width), jnp.float32),
+        ),
+        compiler_params=pltpu.CompilerParams(vmem_limit_bytes=48 * 2**20),
+        cost_estimate=pl.CostEstimate(flops=10**9, bytes_accessed=4 * 10**6, transcendentals=10**6),
+        name="slopes",
+    )(place, scalars, rows, cols, row_ids, col_ids)
+
+
+def text_products(place, rows, slopes, totals):
+    half, width = slopes.shape[1] // 2, rows.shape[1]
+    return pl.pallas_call(
+        text_kernel,
+        in_specs=[SMEM, VMEM, VMEM, VMEM],
+        out_specs=[VMEM, VMEM],
+        out_shape=(
             jax.ShapeDtypeStruct((half + 8, width), jnp.float32),
             jax.ShapeDtypeStruct((half, width), jnp.float32),
         ),
         compiler_params=pltpu.CompilerParams(vmem_limit_bytes=48 * 2**20),
-        cost_estimate=pl.CostEstimate(flops=2 * 10**9, bytes_accessed=6 * 10**6, transcendentals=10**6),
-        name="pairs",
-    )(x.reshape(1).astype(jnp.int32), scalars, rows, cols, row_ids, col_ids)
+        cost_estimate=pl.CostEstimate(flops=10**9, bytes_accessed=5 * 10**6, transcendentals=0),
+        name="text_products",
+    )(place, rows, slopes, totals)
 
 
 def swap_sum(blocks, stats, axis):
@@ -119,9 +145,11 @@
 
     own = spread(uxb.astype(jnp.bfloat16), "y").reshape(-1, width)
     cols = (uyb * UNIT).astype(jnp.float16)
-    own, cols = lax.optimization_barrier((own, cols))
+    first = lax.all_gather(cols[:, :640], Z + ("core",), axis=0, tiled=True)
+    own, second, first = lax.optimization_barrier((own, cols[:, 640:], first))
     rows = spread(own, "x").reshape(-1, width)
-    cols = lax.all_gather(cols, Z + ("core",), axis=0, tiled=True)
+    second = lax.all_gather(second, Z + ("core",), axis=0, tiled=True)
+    cols = jnp.concatenate([first, second], 1)
     cols = (cols.astype(jnp.float32) * (1 / UNIT)).astype(jnp.bfloat16)
     cols = cols.reshape(8, 2, txt_rows, width)
     mine = lax.dynamic_index_in_dim(cols, core, 1, keepdims=False)
@@ -141,22 +169,28 @@
 
     half = cols.shape[0] // 2
     high = rows.shape[0] // 4
-    near, theirs, mine = pairs(x, jnp.stack([scale, bias[0]]), rows, cols, row_ids, col_ids)
-    stats = theirs[half : half + 1, :128]
-
-    dcols = shifted(theirs[:half], "core", 1) + mine
-    stats = stats + shifted(stats, "core", 1)
-    dcols, stats = swap_sum((dcols * 32.0).astype(jnp.float16).reshape(8, txt_rows, width), stats, Z)
+    place = x.reshape(1).astype(jnp.int32)
+    near, totals = slopes_of(place, jnp.stack([scale, bias[0]]), rows, cols, row_ids, col_ids)
 
     back = {}
     for k in (2, 1, 3, 0):
         drows = 64.0 * jnp.dot(near[k * high : (k + 1) * high], cols, preferred_element_type=jnp.float32)
-        back[k] = shifted(drows.astype(jnp.float16), "x", k) if k else drows
+        back[k] = drows.astype(jnp.float16) if k else drows
+    near, back[1], back[2], back[3] = lax.optimization_barrier((near, back[1], back[2], back[3]))
+    for k in (1, 3, 2):
+        back[k] = shifted(back[k], "x", k)
+
+    theirs, mine = text_products(place, rows, near, totals)
+    got = shifted(theirs, "core", 1)
+    dcols = ((got[:half] + mine) * 32.0).astype(jnp.float16).reshape(8, txt_rows, width)
+    dcols, back[1], back[3] = lax.optimization_barrier((dcols, back[1], back[3]))
+    dcols, stats = swap_sum(dcols, got[half : half + 1, :128] + totals[:1, :128], Z)
+    for steps in (1, 2):
+        stats = stats + shifted(stats, "x", steps)
+
     drows = sum(part.astype(jnp.float32) for part in back.values())
     drows = (drows * 0.25).astype(jnp.float16).reshape(8, -1, width)
     drows, stats = swap_sum(drows, stats, "y")
-    for steps in (1, 2):
-        stats = stats + shifted(stats, "x", steps)
     stats = stats[0]
 
     total_texts = txt_rows * 512
@@ -164,9 +198,9 @@
     text_accum = dcols * (1 / 32.0)
     image_grad = unnormalize(ux, rx, scale * image_accum)
     text_grad = unnormalize(uy, ry, scale * text_accum)
-    loss = (stats[0] / total_texts).reshape(1)
-    scale_grad = (scale * stats[1] / total_texts).reshape(1)
-    bias_grad = (stats[2] / total_texts).reshape(1)
+    lane = lax.iota(jnp.int32, stats.shape[0])
+    stats = stats * jnp.where(lane == 1, scale, 1.0) * (1.0 / total_texts)
+    loss, scale_grad, bias_grad = stats[0:1], stats[1:2], stats[2:3]
     return (image_grad, text_grad, loss, scale_grad, bias_grad)
 
 

time: 146 us -> 155 us (1.062)
  blocking collectives: 27.5 us -> 41.7 us
  between operations: 7.6 us -> 2.3 us
  waiting for transfers between devices: 48.4 us -> 46.1 us
  matrix products: 1.78 us -> 3.42 us
    all_gather x1 -> x2, blocking collectives: 27.5 us -> 41.7 us  [the longest x1 25.7 us: body(): first = lax.all_gather(cols[:, :640], Z + ('core',), axis=0, tiled=True)]
    ppermute x7 -> x6, waiting for transfers between devices: 22.3 us -> 12.8 us  [shifted(): lax.ppermute(value, axis, [(i, (i + steps) % count) for i in range(count)])]
    all_to_all x4, waiting for transfers between devices: 26.1 us -> 33.4 us  [swap(): return lax.all_to_all(value, axis, 0, 0, tiled=False)]
    all_to_all x4, starting transfers between devices: 24.3 us -> 22.1 us  [swap(): return lax.all_to_all(value, axis, 0, 0, tiled=False)]
    ppermute x7 -> x6, starting transfers between devices: 17.5 us -> 19.4 us  [shifted(): lax.ppermute(value, axis, [(i, (i + steps) % count) for i in range(count)])]
    dot_general x4, matrix products: 1.78 us -> 3.42 us  [body(): jnp.dot(near[k * high:(k + 1) * high], cols, preferred_element_type=jnp.f...]
    pallas_call x1 -> x2, Pallas kernels: 6.51 us -> 5.03 us  [the longest x1 3.45 us: slopes_of(): pl.pallas_call(slopes_kernel, in_specs=[SMEM, SMEM, VMEM, VMEM, VMEM, VME...]
  transfers between devices with their start and end apart: 11 -> 10, of which waited for: 7 -> 7; matrix products, arithmetic and copies ran while one was open for 4% -> 4% of each run, Pallas kernels for 0% -> 0%
where the time goes in v5:
time: 155 us; the launch traced here: 153 us
  waiting for transfers between devices  46.1 us (30%)
  blocking collectives  41.7 us (27%)
  starting transfers between devices  41.5 us (27%)
  other arithmetic  8.39 us (5%)
  Pallas kernels  5.03 us (3%)
  local copies, waits for them, and re-layouts  4.06 us (3%)
  matrix products  3.42 us (2%)
  between operations  2.3 us (1%)
    all_to_all x4, waiting for transfers between devices, swap(): return lax.all_to_all(value, axis, 0, 0, tiled=False)  33.4 us
    all_gather x1, blocking collectives, body(): first = lax.all_gather(cols[:, :640], Z + ('core',), axis=0, tiled=True)  25.7 us
    all_to_all x4, starting transfers between devices, swap(): return lax.all_to_all(value, axis, 0, 0, tiled=False)  22.1 us
    ppermute x6, starting transfers between devices, shifted(): lax.ppermute(value, axis, [(i, (i + steps) % count) for i in range(count)])  19.4 us
    all_gather x1, blocking collectives, body(): second = lax.all_gather(second, Z + ('core',), axis=0, tiled=True)  16 us
    ppermute x6, waiting for transfers between devices, shifted(): lax.ppermute(value, axis, [(i, (i + steps) % count) for i in range(count)])  12.8 us
    pallas_call x1, Pallas kernels, slopes_of(): pl.pallas_call(slopes_kernel, in_specs=[SMEM, SMEM, VMEM, VMEM, VMEM, VME...  3.45 us
    dot_general x4, matrix products, body(): jnp.dot(near[k * high:(k + 1) * high], cols, preferred_element_type=jnp.f...  3.42 us
  transfers between devices with their start and end apart: 10, of which 7 were waited for; matrix products, arithmetic and copies ran while one was open for 4% of the time, Pallas kernels for 0%

profile of v5, /device:TPU:1, one launch (start us, length us, event | category | flops | bytes accessed | tf_op | source)
XLA Modules:
  0.0 152.6 jit_solution(11016525758527342869)
XLA Ops:
  3.4 7.7 %all-to-all-start = ((bf16[8,24,1152]{2,1,0:T(8,128)(2,1)}), bf16[8,24,1152]{2,1,0:T(8,128)(2,1)S(1)}, u32[]{:S(2)}, u32[]{:S(2)}) async-start(bf16[8,24,1152]{2,1,0:T(8,128)(2,1)} %broadcast_in_dim.18), calls=%async_computation | async-start | bytes 884736 | tf_op jit(solution)/shard_map/all_to_all | solution.py:26
  12.1 25.7 %all_gather.6 = f16[512,640]{1,0:T(8,128)(2,1)S(1)} all-gather(f16[32,640]{1,0:T(8,128)(2,1)S(1)} %slice.65), channel_id=1, replica_groups=mesh['y'=8,'zh'=2,'zl'=4,'x'=4,'core'=2] {'zh','zl','core'}, dimensions={0}, use_global_device_ids=true | all-gather | bytes 696320 | tf_op jit(solution)/shard_map/all_gather | solution.py:148
  37.8 1.4 broadcast_in_dim.19
  39.2 4.0 %all-to-all-start.1 = ((bf16[4,192,1152]{2,1,0:T(8,128)(2,1)}), bf16[4,192,1152]{2,1,0:T(8,128)(2,1)S(1)}, u32[]{:S(2)}, u32[]{:S(2)}) async-start(bf16[4,192,1152]{2,1,0:T(8,128)(2,1)} %broadcast_in_dim.19), calls=%async_computation.1 | async-start | bytes 3538944 | tf_op jit(solution)/shard_map/all_to_all | solution.py:26
  44.9 16.0 %all_gather.7 = f16[512,512]{1,0:T(8,128)(2,1)S(1)} all-gather(f16[32,512]{1,0:T(8,128)(2,1)S(1)} %slice.64), channel_id=1, replica_groups=mesh['y'=8,'zh'=2,'zl'=4,'x'=4,'core'=2] {'zh','zl','core'}, dimensions={0}, use_global_device_ids=true | all-gather | bytes 557056 | tf_op jit(solution)/shard_map/all_gather | solution.py:151
  61.4 4.3 %all-to-all-done.1 = bf16[4,192,1152]{2,1,0:T(8,128)(2,1)S(1)} async-done(((bf16[4,192,1152]{2,1,0:T(8,128)(2,1)}), bf16[4,192,1152]{2,1,0:T(8,128)(2,1)S(1)}, u32[]{:S(2)}, u32[]{:S(2)}) %all-to-all-start.1) | async-done | bytes 1769504 | tf_op jit(solution)/shard_map/all_to_all | solution.py:26
  65.7 3.5 %slopes.1 = (bf16[768,512]{1,0:T(8,128)(2,1)S(1)}, f32[8,1152]{1,0:T(8,128)S(1)}) custom-call(s32[1]{0:T(128)} %bitcast.place, f32[2]{0:T(128)S(1)} %pad_maximum_fusion.3.scalars, bf16[768,1152]{1,0:T(8,128)(2,1)S(1)} %bitcast.33, bf16[512,1152]{1,0:T(8,128)(2,1)S(1)} %bitcast.28, s32[768,1]{1,0:T(8,128)S(1)} %reshape.95.row_ids, s32[1,512]{1,0:T(1,128)S(1)} %reshape.92.col_ids), custom_call_target="tpu_custom_call" | custom-call | flops 1000000000 | bytes 4000000 | tf_op jit(solution)/shard_map/slopes/pallas_call | solution.py:88
  69.6 1.2 fusion.1
  71.2 1.6 %text_products.1 = (f32[264,1152]{1,0:T(8,128)S(1)}, f32[256,1152]{1,0:T(8,128)S(1)}) custom-call(s32[1]{0:T(128)} %bitcast.place, bf16[768,1152]{1,0:T(8,128)(2,1)S(1)} %bitcast.34, bf16[768,512]{1,0:T(8,128)(2,1)S(1)} %get-tuple-element.24.slopes, f32[8,1152]{1,0:T(8,128)S(1)} %get-tuple-element.25.totals), custom_call_target="tpu_custom_call" | custom-call | flops 1000000000 | bytes 5000000 | tf_op jit(solution)/shard_map/text_products/pallas_call | solution.py:104
  72.8 3.2 %collective-permute-start.1 = (f32[264,1152]{1,0:T(8,128)S(1)}, f32[264,1152]{1,0:T(8,128)S(1)}, u32[]{:S(2)}, u32[]{:S(2)}) collective-permute-start(f32[264,1152]{1,0:T(8,128)S(1)} %get-tuple-element.26), channel_id=1, source_target_pairs={{0,1},{1,0},{2,3},{3,2},{4,5},{5,4},{6,7},{7,6},{8,9},{9,8},{10,11... | collective-permute-start | bytes 3649544 | tf_op jit(solution)/shard_map/ppermute | solution.py:31
  76.1 2.2 %collective-permute-start.2 = (f16[192,1152]{1,0:T(8,128)(2,1)S(1)}, f16[192,1152]{1,0:T(8,128)(2,1)S(1)}, u32[]{:S(2)}, u32[]{:S(2)}) collective-permute-start(f16[192,1152]{1,0:T(8,128)(2,1)S(1)} %fusion), channel_id=1, source_target_pairs={{0,2},{2,4},{4,6},{6,0},{1,3},{3,5},{5,7},{7,1},{8,10},{10,12},{12... | collective-permute-start | bytes 1327112 | tf_op jit(solution)/shard_map/ppermute | solution.py:31
  78.3 4.3 %collective-permute-start.3 = (f16[192,1152]{1,0:T(8,128)(2,1)S(1)}, f16[192,1152]{1,0:T(8,128)(2,1)S(1)}, u32[]{:S(2)}, u32[]{:S(2)}) collective-permute-start(f16[192,1152]{1,0:T(8,128)(2,1)S(1)} %fusion.2), channel_id=1, source_target_pairs={{0,6},{2,0},{4,2},{6,4},{1,7},{3,1},{5,3},{7,5},{8,14},{10,8},{12,... | collective-permute-start | bytes 1327112 | tf_op jit(solution)/shard_map/ppermute | solution.py:31
  82.8 8.2 %collective-permute-done.2 = f16[192,1152]{1,0:T(8,128)(2,1)S(1)} collective-permute-done((f16[192,1152]{1,0:T(8,128)(2,1)S(1)}, f16[192,1152]{1,0:T(8,128)(2,1)S(1)}, u32[]{:S(2)}, u32[]{:S(2)}) %collective-permute-start.2) | collective-permute-done | bytes 442400 | tf_op jit(solution)/shard_map/ppermute | solution.py:31
  92.0 1.0 pad_maximum_fusion.1
  93.0 3.5 %all-to-all-start.2 = ((f16[8,32,1280]{2,1,0:T(8,128)(2,1)}), f16[8,32,1280]{2,1,0:T(8,128)(2,1)S(1)}, u32[]{:S(2)}, u32[]{:S(2)}) async-start(f16[8,32,1280]{2,1,0:T(8,128)(2,1)} %pad_maximum_fusion.1), calls=%async_computation.2 | async-start | bytes 1310720 | tf_op jit(solution)/shard_map/all_to_all | solution.py:26
  96.7 4.1 %collective-permute-start = (f16[192,1152]{1,0:T(8,128)(2,1)S(1)}, f16[192,1152]{1,0:T(8,128)(2,1)}, u32[]{:S(2)}, u32[]{:S(2)}) collective-permute-start(f16[192,1152]{1,0:T(8,128)(2,1)S(1)} %copy-done.3), channel_id=1, source_target_pairs={{0,4},{2,6},{4,0},{6,2},{1,5},{3,7},{5,1},{7,3},{8,12},{10,14},{12... | collective-permute-start | bytes 1327112 | tf_op jit(solution)/shard_map/ppermute | solution.py:31
  100.8 16.4 %all-to-all-done.2 = f16[8,32,1280]{2,1,0:T(8,128)(2,1)S(1)} async-done(((f16[8,32,1280]{2,1,0:T(8,128)(2,1)}), f16[8,32,1280]{2,1,0:T(8,128)(2,1)S(1)}, u32[]{:S(2)}, u32[]{:S(2)}) %all-to-all-start.2) | async-done | bytes 655392 | tf_op jit(solution)/shard_map/all_to_all | solution.py:26
  117.3 2.0 %collective-permute-start.4 = (f32[1,128]{1,0:T(1,128)S(1)}, f32[1,128]{1,0:T(1,128)S(1)}, u32[]{:S(2)}, u32[]{:S(2)}) collective-permute-start(f32[1,128]{1,0:T(1,128)S(1)} %multiply_bitcast_fusion), channel_id=1, source_target_pairs={{0,2},{2,4},{4,6},{6,0},{1,3},{3,5},{5,7},{7,1},{8,10},{10,12},{12... | collective-permute-start | bytes 1544 | tf_op jit(solution)/shard_map/ppermute | solution.py:31
  119.3 1.4 convolution_multiply_fusion
  120.7 2.8 %collective-permute-done.4 = f32[1,128]{1,0:T(1,128)S(1)} collective-permute-done((f32[1,128]{1,0:T(1,128)S(1)}, f32[1,128]{1,0:T(1,128)S(1)}, u32[]{:S(2)}, u32[]{:S(2)}) %collective-permute-start.4) | collective-permute-done | bytes 544 | tf_op jit(solution)/shard_map/ppermute | solution.py:31
  123.5 3.6 %collective-permute-start.5 = (f32[1,128]{1,0:T(1,128)S(1)}, f32[1,128]{1,0:T(1,128)S(1)}, u32[]{:S(2)}, u32[]{:S(2)}) collective-permute-start(f32[1,128]{1,0:T(1,128)S(1)} %fusion.18), channel_id=1, source_target_pairs={{0,4},{2,6},{4,0},{6,2},{1,5},{3,7},{5,1},{7,3},{8,12},{10,14},{12... | collective-permute-start | bytes 1544 | tf_op jit(solution)/shard_map/ppermute | solution.py:31
  127.1 1.3 multiply_convert_fusion.1
  130.3 6.9 %all-to-all-start.3 = ((f16[8,24,1280]{2,1,0:T(8,128)(2,1)}), f16[8,24,1280]{2,1,0:T(8,128)(2,1)S(1)}, u32[]{:S(2)}, u32[]{:S(2)}) async-start(f16[8,24,1280]{2,1,0:T(8,128)(2,1)} %pad_maximum_fusion.2), calls=%async_computation.3 | async-start | bytes 983040 | tf_op jit(solution)/shard_map/all_to_all | solution.py:26
  138.3 12.7 %all-to-all-done.3 = f16[8,24,1280]{2,1,0:T(8,128)(2,1)S(1)} async-done(((f16[8,24,1280]{2,1,0:T(8,128)(2,1)}), f16[8,24,1280]{2,1,0:T(8,128)(2,1)S(1)}, u32[]{:S(2)}, u32[]{:S(2)}) %all-to-all-start.3) | async-done | bytes 491552 | tf_op jit(solution)/shard_map/all_to_all | solution.py:26
  (65 shorter events, 11.4 us)
Async XLA Ops:
  0.6 10.4 %copy-start.1 = (bf16[32,1152]{1,0:T(8,128)(2,1)S(1)}, bf16[32,1152]{1,0:T(8,128)(2,1)}, u32[]{:S(2)}) copy-start(bf16[32,1152]{1,0:T(8,128)(2,1)} %param.7) | copy-start | bytes 221188
  0.6 10.7 %copy-start.5 = (s32[12288]{0:T(1024)S(1)}, s32[12288]{0:T(1024)}, u32[]{:S(2)}) copy-start(s32[12288]{0:T(1024)} %param.8) | copy-start | bytes 147460
  0.7 11.1 %copy-start.4 = (s32[16384]{0:T(1024)S(1)}, s32[16384]{0:T(1024)}, u32[]{:S(2)}) copy-start(s32[16384]{0:T(1024)} %param.9) | copy-start | bytes 196612
  3.4 34.5 %all-to-all-start = ((bf16[8,24,1152]{2,1,0:T(8,128)(2,1)}), bf16[8,24,1152]{2,1,0:T(8,128)(2,1)S(1)}, u32[]{:S(2)}, u32[]{:S(2)}) async-start(bf16[8,24,1152]{2,1,0:T(8,128)(2,1)} %broadcast_in_dim.18), calls=%async_computation | async-start | bytes 884736 | tf_op jit(solution)/shard_map/all_to_all | solution.py:26
  39.2 26.5 %all-to-all-start.1 = ((bf16[4,192,1152]{2,1,0:T(8,128)(2,1)}), bf16[4,192,1152]{2,1,0:T(8,128)(2,1)S(1)}, u32[]{:S(2)}, u32[]{:S(2)}) async-start(bf16[4,192,1152]{2,1,0:T(8,128)(2,1)} %broadcast_in_dim.19), calls=%async_computation.1 | async-start | bytes 3538944 | tf_op jit(solution)/shard_map/all_to_all | solution.py:26
  69.1 2.1 %copy-start = (bf16[768,512]{1,0:T(8,128)(2,1)}, bf16[768,512]{1,0:T(8,128)(2,1)S(1)}, u32[]{:S(2)}) copy-start(bf16[768,512]{1,0:T(8,128)(2,1)S(1)} %get-tuple-element.24.slopes) | copy-start | bytes 2359300
  72.8 9.8 %collective-permute-start.1 = (f32[264,1152]{1,0:T(8,128)S(1)}, f32[264,1152]{1,0:T(8,128)S(1)}, u32[]{:S(2)}, u32[]{:S(2)}) collective-permute-start(f32[264,1152]{1,0:T(8,128)S(1)} %get-tuple-element.26), channel_id=1, source_target_pairs={{0,1},{1,0},{2,3},{3,2},{4,5},{5,4},{6,7},{7,6},{8,9},{9,8},{10,11... | collective-permute-start | bytes 3649544 | tf_op jit(solution)/shard_map/ppermute | solution.py:31
  76.1 14.9 %collective-permute-start.2 = (f16[192,1152]{1,0:T(8,128)(2,1)S(1)}, f16[192,1152]{1,0:T(8,128)(2,1)S(1)}, u32[]{:S(2)}, u32[]{:S(2)}) collective-permute-start(f16[192,1152]{1,0:T(8,128)(2,1)S(1)} %fusion), channel_id=1, source_target_pairs={{0,2},{2,4},{4,6},{6,0},{1,3},{3,5},{5,7},{7,1},{8,10},{10,12},{12... | collective-permute-start | bytes 1327112 | tf_op jit(solution)/shard_map/ppermute | solution.py:31
  78.3 13.6 %collective-permute-start.3 = (f16[192,1152]{1,0:T(8,128)(2,1)S(1)}, f16[192,1152]{1,0:T(8,128)(2,1)S(1)}, u32[]{:S(2)}, u32[]{:S(2)}) collective-permute-start(f16[192,1152]{1,0:T(8,128)(2,1)S(1)} %fusion.2), channel_id=1, source_target_pairs={{0,6},{2,0},{4,2},{6,4},{1,7},{3,1},{5,3},{7,5},{8,14},{10,8},{12,... | collective-permute-start | bytes 1327112 | tf_op jit(solution)/shard_map/ppermute | solution.py:31
  92.0 4.7 %copy-start.3 = (f16[192,1152]{1,0:T(8,128)(2,1)S(1)}, f16[192,1152]{1,0:T(8,128)(2,1)}, u32[]{:S(2)}) copy-start(f16[192,1152]{1,0:T(8,128)(2,1)} %fusion.1) | copy-start | bytes 1327108
  93.0 24.2 %all-to-all-start.2 = ((f16[8,32,1280]{2,1,0:T(8,128)(2,1)}), f16[8,32,1280]{2,1,0:T(8,128)(2,1)S(1)}, u32[]{:S(2)}, u32[]{:S(2)}) async-start(f16[8,32,1280]{2,1,0:T(8,128)(2,1)} %pad_maximum_fusion.1), calls=%async_computation.2 | async-start | bytes 1310720 | tf_op jit(solution)/shard_map/all_to_all | solution.py:26
  96.7 30.4 %collective-permute-start = (f16[192,1152]{1,0:T(8,128)(2,1)S(1)}, f16[192,1152]{1,0:T(8,128)(2,1)}, u32[]{:S(2)}, u32[]{:S(2)}) collective-permute-start(f16[192,1152]{1,0:T(8,128)(2,1)S(1)} %copy-done.3), channel_id=1, source_target_pairs={{0,4},{2,6},{4,0},{6,2},{1,5},{3,7},{5,1},{7,3},{8,12},{10,14},{12... | collective-permute-start | bytes 1327112 | tf_op jit(solution)/shard_map/ppermute | solution.py:31
  117.3 6.2 %collective-permute-start.4 = (f32[1,128]{1,0:T(1,128)S(1)}, f32[1,128]{1,0:T(1,128)S(1)}, u32[]{:S(2)}, u32[]{:S(2)}) collective-permute-start(f32[1,128]{1,0:T(1,128)S(1)} %multiply_bitcast_fusion), channel_id=1, source_target_pairs={{0,2},{2,4},{4,6},{6,0},{1,3},{3,5},{5,7},{7,1},{8,10},{10,12},{12... | collective-permute-start | bytes 1544 | tf_op jit(solution)/shard_map/ppermute | solution.py:31
  123.5 5.8 %collective-permute-start.5 = (f32[1,128]{1,0:T(1,128)S(1)}, f32[1,128]{1,0:T(1,128)S(1)}, u32[]{:S(2)}, u32[]{:S(2)}) collective-permute-start(f32[1,128]{1,0:T(1,128)S(1)} %fusion.18), channel_id=1, source_target_pairs={{0,4},{2,6},{4,0},{6,2},{1,5},{3,7},{5,1},{7,3},{8,12},{10,14},{12... | collective-permute-start | bytes 1544 | tf_op jit(solution)/shard_map/ppermute | solution.py:31
  130.3 20.6 %all-to-all-start.3 = ((f16[8,24,1280]{2,1,0:T(8,128)(2,1)}), f16[8,24,1280]{2,1,0:T(8,128)(2,1)S(1)}, u32[]{:S(2)}, u32[]{:S(2)}) async-start(f16[8,24,1280]{2,1,0:T(8,128)(2,1)} %pad_maximum_fusion.2), calls=%async_computation.3 | async-start | bytes 983040 | tf_op jit(solution)/shard_map/all_to_all | solution.py:26
  137.3 13.8 %copy-start.2 = (bf16[24,1152]{1,0:T(8,128)(2,1)S(1)}, bf16[24,1152]{1,0:T(8,128)(2,1)}, u32[]{:S(2)}) copy-start(bf16[24,1152]{1,0:T(8,128)(2,1)} %param.6) | copy-start | bytes 165892

commit v6 on v5

--- a/solution.py
+++ b/solution.py
@@ -145,11 +145,9 @@
 
     own = spread(uxb.astype(jnp.bfloat16), "y").reshape(-1, width)
     cols = (uyb * UNIT).astype(jnp.float16)
-    first = lax.all_gather(cols[:, :640], Z + ("core",), axis=0, tiled=True)
-    own, second, first = lax.optimization_barrier((own, cols[:, 640:], first))
+    own, cols = lax.optimization_barrier((own, cols))
     rows = spread(own, "x").reshape(-1, width)
-    second = lax.all_gather(second, Z + ("core",), axis=0, tiled=True)
-    cols = jnp.concatenate([first, second], 1)
+    cols = lax.all_gather(cols, Z + ("core",), axis=0, tiled=True)
     cols = (cols.astype(jnp.float32) * (1 / UNIT)).astype(jnp.bfloat16)
     cols = cols.reshape(8, 2, txt_rows, width)
     mine = lax.dynamic_index_in_dim(cols, core, 1, keepdims=False)
@@ -176,14 +174,12 @@
     for k in (2, 1, 3, 0):
         drows = 64.0 * jnp.dot(near[k * high : (k + 1) * high], cols, preferred_element_type=jnp.float32)
         back[k] = drows.astype(jnp.float16) if k else drows
-    near, back[1], back[2], back[3] = lax.optimization_barrier((near, back[1], back[2], back[3]))
-    for k in (1, 3, 2):
+    for k in (2, 1, 3):
         back[k] = shifted(back[k], "x", k)
 
     theirs, mine = text_products(place, rows, near, totals)
     got = shifted(theirs, "core", 1)
     dcols = ((got[:half] + mine) * 32.0).astype(jnp.float16).reshape(8, txt_rows, width)
-    dcols, back[1], back[3] = lax.optimization_barrier((dcols, back[1], back[3]))
     dcols, stats = swap_sum(dcols, got[half : half + 1, :128] + totals[:1, :128], Z)
     for steps in (1, 2):
         stats = stats + shifted(stats, "x", steps)

time: 155 us -> 131 us (0.85)
  blocking collectives: 41.7 us -> 27.4 us
  waiting for transfers between devices: 46.1 us -> 38.4 us
    all_gather x2 -> x1, blocking collectives: 41.7 us -> 27.4 us  [body(): cols = lax.all_gather(cols, Z + ('core',), axis=0, tiled=True)]
    ppermute x6, waiting for transfers between devices: 12.8 us -> 7.48 us  [shifted(): lax.ppermute(value, axis, [(i, (i + steps) % count) for i in range(count)])]
    ppermute x6, starting transfers between devices: 19.4 us -> 16.2 us  [shifted(): lax.ppermute(value, axis, [(i, (i + steps) % count) for i in range(count)])]
    all_to_all x4, waiting for transfers between devices: 33.4 us -> 30.9 us  [swap(): return lax.all_to_all(value, axis, 0, 0, tiled=False)]
    all_to_all x4, starting transfers between devices: 22.1 us -> 23.8 us  [swap(): return lax.all_to_all(value, axis, 0, 0, tiled=False)]
  transfers between devices with their start and end apart: 10 -> 10, of which waited for: 7 -> 6; matrix products, arithmetic and copies ran while one was open for 4% -> 6% of each run, Pallas kernels for 0% -> 0%
where the time goes in v6:
time: 131 us; the launch traced here: 129 us
  starting transfers between devices  40 us (31%)
  waiting for transfers between devices  38.4 us (29%)
  blocking collectives  27.4 us (21%)
  other arithmetic  6.92 us (5%)
  Pallas kernels  5.07 us (4%)
  matrix products  4.62 us (4%)
  local copies, waits for them, and re-layouts  4.05 us (3%)
  between operations  2.29 us (2%)
    all_to_all x4, waiting for transfers between devices, swap(): return lax.all_to_all(value, axis, 0, 0, tiled=False)  30.9 us
    all_gather x1, blocking collectives, body(): cols = lax.all_gather(cols, Z + ('core',), axis=0, tiled=True)  27.4 us
    all_to_all x4, starting transfers between devices, swap(): return lax.all_to_all(value, axis, 0, 0, tiled=False)  23.8 us
    ppermute x6, starting transfers between devices, shifted(): lax.ppermute(value, axis, [(i, (i + steps) % count) for i in range(count)])  16.2 us
    ppermute x6, waiting for transfers between devices, shifted(): lax.ppermute(value, axis, [(i, (i + steps) % count) for i in range(count)])  7.48 us
    dot_general x4, matrix products, body(): jnp.dot(near[k * high:(k + 1) * high], cols, preferred_element_type=jnp.f...  4.62 us
    pallas_call x1, Pallas kernels, slopes_of(): pl.pallas_call(slopes_kernel, in_specs=[SMEM, SMEM, VMEM, VMEM, VMEM, VME...  3.48 us
  transfers between devices with their start and end apart: 10, of which 6 were waited for; matrix products, arithmetic and copies ran while one was open for 6% of the time, Pallas kernels for 0%

profile of v6, /device:TPU:1, one launch (start us, length us, event | category | flops | bytes accessed | tf_op | source)
XLA Modules:
  0.0 128.7 jit_solution(10725358145005407384)
XLA Ops:
  3.4 7.7 %all-to-all-start = ((bf16[8,24,1152]{2,1,0:T(8,128)(2,1)}), bf16[8,24,1152]{2,1,0:T(8,128)(2,1)S(1)}, u32[]{:S(2)}, u32[]{:S(2)}) async-start(bf16[8,24,1152]{2,1,0:T(8,128)(2,1)} %broadcast_in_dim.18), calls=%async_computation | async-start | bytes 884736 | tf_op jit(solution)/shard_map/all_to_all | solution.py:26
  13.7 10.0 %all-to-all-done = bf16[8,24,1152]{2,1,0:T(8,128)(2,1)S(1)} async-done(((bf16[8,24,1152]{2,1,0:T(8,128)(2,1)}), bf16[8,24,1152]{2,1,0:T(8,128)(2,1)S(1)}, u32[]{:S(2)}, u32[]{:S(2)}) %all-to-all-start) | async-done | bytes 442400 | tf_op jit(solution)/shard_map/all_to_all | solution.py:26
  23.7 1.4 %broadcast_in_dim.19 = bf16[4,192,1152]{2,1,0:T(8,128)(2,1)} broadcast(bf16[192,1152]{1,0:T(8,128)(2,1)S(1)} %bitcast.36), dimensions={1,2} | broadcast | bytes 2211840 | tf_op jit(solution)/shard_map/broadcast_in_dim | solution.py:36
  25.1 7.1 %all-to-all-start.1 = ((bf16[4,192,1152]{2,1,0:T(8,128)(2,1)}), bf16[4,192,1152]{2,1,0:T(8,128)(2,1)S(1)}, u32[]{:S(2)}, u32[]{:S(2)}) async-start(bf16[4,192,1152]{2,1,0:T(8,128)(2,1)} %broadcast_in_dim.19), calls=%async_computation.1 | async-start | bytes 3538944 | tf_op jit(solution)/shard_map/all_to_all | solution.py:26
  32.2 27.4 %all-gather.1 = f16[512,1152]{1,0:T(8,128)(2,1)S(1)} all-gather(f16[32,1152]{1,0:T(8,128)(2,1)S(1)} %multiply_convert_fusion.2), channel_id=1, replica_groups=mesh['y'=8,'zh'=2,'zl'=4,'x'=4,'core'=2] {'zh','zl','core'}, dimensions={0}, use_global_device_ids=true | all-gather | bytes 1253376 | tf_op jit(solution)/shard_map/all_gather | solution.py:150
  60.0 3.5 %slopes.1 = (bf16[768,512]{1,0:T(8,128)(2,1)S(1)}, f32[8,1152]{1,0:T(8,128)S(1)}) custom-call(s32[1]{0:T(128)} %bitcast.place, f32[2]{0:T(128)S(1)} %pad_maximum_fusion.3.scalars, bf16[768,1152]{1,0:T(8,128)(2,1)S(1)} %bitcast.32, bf16[512,1152]{1,0:T(8,128)(2,1)S(1)} %bitcast.27, s32[768,1]{1,0:T(8,128)S(1)} %reshape.96.row_ids, s32[1,512]{1,0:T(1,128)S(1)} %reshape.93.col_ids), custom_call_target="tpu_custom_call" | custom-call | flops 1000000000 | bytes 4000000 | tf_op jit(solution)/shard_map/slopes/pallas_call | solution.py:88
  63.5 1.6 %text_products.1 = (f32[264,1152]{1,0:T(8,128)S(1)}, f32[256,1152]{1,0:T(8,128)S(1)}) custom-call(s32[1]{0:T(128)} %bitcast.place, bf16[768,1152]{1,0:T(8,128)(2,1)S(1)} %bitcast.33, bf16[768,512]{1,0:T(8,128)(2,1)S(1)} %get-tuple-element.13.slopes, f32[8,1152]{1,0:T(8,128)S(1)} %get-tuple-element.14.totals), custom_call_target="tpu_custom_call" | custom-call | flops 1000000000 | bytes 5000000 | tf_op jit(solution)/shard_map/text_products/pallas_call | solution.py:104
  65.1 2.1 %collective-permute-start.3 = (f32[264,1152]{1,0:T(8,128)S(1)}, f32[264,1152]{1,0:T(8,128)S(1)}, u32[]{:S(2)}, u32[]{:S(2)}) collective-permute-start(f32[264,1152]{1,0:T(8,128)S(1)} %get-tuple-element.15), channel_id=1, source_target_pairs={{0,1},{1,0},{2,3},{3,2},{4,5},{5,4},{6,7},{7,6},{8,9},{9,8},{10,11... | collective-permute-start | bytes 3649544 | tf_op jit(solution)/shard_map/ppermute | solution.py:31
  67.3 2.6 %collective-permute-done.3 = f32[264,1152]{1,0:T(8,128)S(1)} collective-permute-done((f32[264,1152]{1,0:T(8,128)S(1)}, f32[264,1152]{1,0:T(8,128)S(1)}, u32[]{:S(2)}, u32[]{:S(2)}) %collective-permute-start.3) | collective-permute-done | bytes 1216544 | tf_op jit(solution)/shard_map/ppermute | solution.py:31
  70.2 1.0 pad_maximum_fusion.1
  71.2 5.6 %all-to-all-start.2 = ((f16[8,32,1280]{2,1,0:T(8,128)(2,1)}), f16[8,32,1280]{2,1,0:T(8,128)(2,1)S(1)}, u32[]{:S(2)}, u32[]{:S(2)}) async-start(f16[8,32,1280]{2,1,0:T(8,128)(2,1)} %pad_maximum_fusion.1), calls=%async_computation.2 | async-start | bytes 1310720 | tf_op jit(solution)/shard_map/all_to_all | solution.py:26
  77.3 3.1 %collective-permute-start = (f16[192,1152]{1,0:T(8,128)(2,1)S(1)}, f16[192,1152]{1,0:T(8,128)(2,1)}, u32[]{:S(2)}, u32[]{:S(2)}) collective-permute-start(f16[192,1152]{1,0:T(8,128)(2,1)S(1)} %fusion), channel_id=1, source_target_pairs={{0,4},{2,6},{4,0},{6,2},{1,5},{3,7},{5,1},{7,3},{8,12},{10,14},{12... | collective-permute-start | bytes 1327112 | tf_op jit(solution)/shard_map/ppermute | solution.py:31
  80.4 1.2 fusion.1
  81.6 2.2 %collective-permute-start.1 = (f16[192,1152]{1,0:T(8,128)(2,1)}, f16[192,1152]{1,0:T(8,128)(2,1)}, u32[]{:S(2)}, u32[]{:S(2)}) collective-permute-start(f16[192,1152]{1,0:T(8,128)(2,1)} %fusion.1), channel_id=1, source_target_pairs={{0,2},{2,4},{4,6},{6,0},{1,3},{3,5},{5,7},{7,1},{8,10},{10,12},{12... | collective-permute-start | bytes 1327112 | tf_op jit(solution)/shard_map/ppermute | solution.py:31
  83.8 1.2 fusion.2
  85.0 4.3 %collective-permute-start.2 = (f16[192,1152]{1,0:T(8,128)(2,1)}, f16[192,1152]{1,0:T(8,128)(2,1)}, u32[]{:S(2)}, u32[]{:S(2)}) collective-permute-start(f16[192,1152]{1,0:T(8,128)(2,1)} %fusion.2), channel_id=1, source_target_pairs={{0,6},{2,0},{4,2},{6,4},{1,7},{3,1},{5,3},{7,5},{8,14},{10,8},{12,... | collective-permute-start | bytes 1327112 | tf_op jit(solution)/shard_map/ppermute | solution.py:31
  89.3 8.3 %all-to-all-done.2 = f16[8,32,1280]{2,1,0:T(8,128)(2,1)S(1)} async-done(((f16[8,32,1280]{2,1,0:T(8,128)(2,1)}), f16[8,32,1280]{2,1,0:T(8,128)(2,1)S(1)}, u32[]{:S(2)}, u32[]{:S(2)}) %all-to-all-start.2) | async-done | bytes 655392 | tf_op jit(solution)/shard_map/all_to_all | solution.py:26
  97.6 2.2 %collective-permute-start.4 = (f32[1,128]{1,0:T(1,128)S(1)}, f32[1,128]{1,0:T(1,128)S(1)}, u32[]{:S(2)}, u32[]{:S(2)}) collective-permute-start(f32[1,128]{1,0:T(1,128)S(1)} %multiply_bitcast_fusion), channel_id=1, source_target_pairs={{0,2},{2,4},{4,6},{6,0},{1,3},{3,5},{5,7},{7,1},{8,10},{10,12},{12... | collective-permute-start | bytes 1544 | tf_op jit(solution)/shard_map/ppermute | solution.py:31
  99.9 3.2 %collective-permute-done.4 = f32[1,128]{1,0:T(1,128)S(1)} collective-permute-done((f32[1,128]{1,0:T(1,128)S(1)}, f32[1,128]{1,0:T(1,128)S(1)}, u32[]{:S(2)}, u32[]{:S(2)}) %collective-permute-start.4) | collective-permute-done | bytes 544 | tf_op jit(solution)/shard_map/ppermute | solution.py:31
  103.1 2.3 %collective-permute-start.5 = (f32[1,128]{1,0:T(1,128)S(1)}, f32[1,128]{1,0:T(1,128)S(1)}, u32[]{:S(2)}, u32[]{:S(2)}) collective-permute-start(f32[1,128]{1,0:T(1,128)S(1)} %fusion.18), channel_id=1, source_target_pairs={{0,4},{2,6},{4,0},{6,2},{1,5},{3,7},{5,1},{7,3},{8,12},{10,14},{12... | collective-permute-start | bytes 1544 | tf_op jit(solution)/shard_map/ppermute | solution.py:31
  105.5 1.8 %multiply_convert_fusion.1 = f16[192,1152]{1,0:T(8,128)(2,1)S(1)} fusion(f16[192,1152]{1,0:T(8,128)(2,1)} %collective-permute-done.2, f16[192,1152]{1,0:T(8,128)(2,1)} %collective-permute-done.1, f16[192,1152]{1,0:T(8,128)(2,1)} %collective-permute-done, bf16[512,1152]{1,0:T(8,128)(2,1)S(1)} %bitcast.31, bf16[768,512]{1,0:T(8,128)(2,1)S(1)} %copy-done.1), kind=kOutput, calls=%fused_computation.14 | convolution fusion | flops 228483072 | bytes 3145728 | tf_op jit(solution)/shard_map/dot_general | solution.py:175
  107.2 1.6 %collective-permute-done.5 = f32[1,128]{1,0:T(1,128)S(1)} collective-permute-done((f32[1,128]{1,0:T(1,128)S(1)}, f32[1,128]{1,0:T(1,128)S(1)}, u32[]{:S(2)}, u32[]{:S(2)}) %collective-permute-start.5) | collective-permute-done | bytes 544 | tf_op jit(solution)/shard_map/ppermute | solution.py:31
  109.9 3.5 %all-to-all-start.3 = ((f16[8,24,1280]{2,1,0:T(8,128)(2,1)}), f16[8,24,1280]{2,1,0:T(8,128)(2,1)S(1)}, u32[]{:S(2)}, u32[]{:S(2)}) async-start(f16[8,24,1280]{2,1,0:T(8,128)(2,1)} %pad_maximum_fusion.2), calls=%async_computation.3 | async-start | bytes 983040 | tf_op jit(solution)/shard_map/all_to_all | solution.py:26
  114.5 12.6 %all-to-all-done.3 = f16[8,24,1280]{2,1,0:T(8,128)(2,1)S(1)} async-done(((f16[8,24,1280]{2,1,0:T(8,128)(2,1)}), f16[8,24,1280]{2,1,0:T(8,128)(2,1)S(1)}, u32[]{:S(2)}, u32[]{:S(2)}) %all-to-all-start.3) | async-done | bytes 491552 | tf_op jit(solution)/shard_map/all_to_all | solution.py:26
  (61 shorter events, 9.1 us)
Async XLA Ops:
  0.6 11.7 %copy-start.2 = (bf16[32,1152]{1,0:T(8,128)(2,1)S(1)}, bf16[32,1152]{1,0:T(8,128)(2,1)}, u32[]{:S(2)}) copy-start(bf16[32,1152]{1,0:T(8,128)(2,1)} %param.7) | copy-start | bytes 221188
  0.6 11.8 %copy-start.5 = (s32[12288]{0:T(1024)S(1)}, s32[12288]{0:T(1024)}, u32[]{:S(2)}) copy-start(s32[12288]{0:T(1024)} %param.8) | copy-start | bytes 147460
  0.7 12.3 %copy-start.4 = (s32[16384]{0:T(1024)S(1)}, s32[16384]{0:T(1024)}, u32[]{:S(2)}) copy-start(s32[16384]{0:T(1024)} %param.9) | copy-start | bytes 196612
  3.4 20.4 %all-to-all-start = ((bf16[8,24,1152]{2,1,0:T(8,128)(2,1)}), bf16[8,24,1152]{2,1,0:T(8,128)(2,1)S(1)}, u32[]{:S(2)}, u32[]{:S(2)}) async-start(bf16[8,24,1152]{2,1,0:T(8,128)(2,1)} %broadcast_in_dim.18), calls=%async_computation | async-start | bytes 884736 | tf_op jit(solution)/shard_map/all_to_all | solution.py:26
  25.1 34.9 %all-to-all-start.1 = ((bf16[4,192,1152]{2,1,0:T(8,128)(2,1)}), bf16[4,192,1152]{2,1,0:T(8,128)(2,1)S(1)}, u32[]{:S(2)}, u32[]{:S(2)}) async-start(bf16[4,192,1152]{2,1,0:T(8,128)(2,1)} %broadcast_in_dim.19), calls=%async_computation.1 | async-start | bytes 3538944 | tf_op jit(solution)/shard_map/all_to_all | solution.py:26
  63.5 1.6 %copy-start = (bf16[768,512]{1,0:T(8,128)(2,1)}, bf16[768,512]{1,0:T(8,128)(2,1)S(1)}, u32[]{:S(2)}) copy-start(bf16[768,512]{1,0:T(8,128)(2,1)S(1)} %get-tuple-element.13.slopes) | copy-start | bytes 2359300
  65.1 4.8 %collective-permute-start.3 = (f32[264,1152]{1,0:T(8,128)S(1)}, f32[264,1152]{1,0:T(8,128)S(1)}, u32[]{:S(2)}, u32[]{:S(2)}) collective-permute-start(f32[264,1152]{1,0:T(8,128)S(1)} %get-tuple-element.15), channel_id=1, source_target_pairs={{0,1},{1,0},{2,3},{3,2},{4,5},{5,4},{6,7},{7,6},{8,9},{9,8},{10,11... | collective-permute-start | bytes 3649544 | tf_op jit(solution)/shard_map/ppermute | solution.py:31
  70.2 6.6 %copy-start.1 = (bf16[768,512]{1,0:T(8,128)(2,1)S(1)}, bf16[768,512]{1,0:T(8,128)(2,1)}, u32[]{:S(2)}) copy-start(bf16[768,512]{1,0:T(8,128)(2,1)} %copy-done) | copy-start | bytes 2359300
  71.2 26.4 %all-to-all-start.2 = ((f16[8,32,1280]{2,1,0:T(8,128)(2,1)}), f16[8,32,1280]{2,1,0:T(8,128)(2,1)S(1)}, u32[]{:S(2)}, u32[]{:S(2)}) async-start(f16[8,32,1280]{2,1,0:T(8,128)(2,1)} %pad_maximum_fusion.1), calls=%async_computation.2 | async-start | bytes 1310720 | tf_op jit(solution)/shard_map/all_to_all | solution.py:26
  77.3 28.2 %collective-permute-start = (f16[192,1152]{1,0:T(8,128)(2,1)S(1)}, f16[192,1152]{1,0:T(8,128)(2,1)}, u32[]{:S(2)}, u32[]{:S(2)}) collective-permute-start(f16[192,1152]{1,0:T(8,128)(2,1)S(1)} %fusion), channel_id=1, source_target_pairs={{0,4},{2,6},{4,0},{6,2},{1,5},{3,7},{5,1},{7,3},{8,12},{10,14},{12... | collective-permute-start | bytes 1327112 | tf_op jit(solution)/shard_map/ppermute | solution.py:31
  81.6 23.9 %collective-permute-start.1 = (f16[192,1152]{1,0:T(8,128)(2,1)}, f16[192,1152]{1,0:T(8,128)(2,1)}, u32[]{:S(2)}, u32[]{:S(2)}) collective-permute-start(f16[192,1152]{1,0:T(8,128)(2,1)} %fusion.1), channel_id=1, source_target_pairs={{0,2},{2,4},{4,6},{6,0},{1,3},{3,5},{5,7},{7,1},{8,10},{10,12},{12... | collective-permute-start | bytes 1327112 | tf_op jit(solution)/shard_map/ppermute | solution.py:31
  85.0 20.5 %collective-permute-start.2 = (f16[192,1152]{1,0:T(8,128)(2,1)}, f16[192,1152]{1,0:T(8,128)(2,1)}, u32[]{:S(2)}, u32[]{:S(2)}) collective-permute-start(f16[192,1152]{1,0:T(8,128)(2,1)} %fusion.2), channel_id=1, source_target_pairs={{0,6},{2,0},{4,2},{6,4},{1,7},{3,1},{5,3},{7,5},{8,14},{10,8},{12,... | collective-permute-start | bytes 1327112 | tf_op jit(solution)/shard_map/ppermute | solution.py:31
  97.6 5.5 %collective-permute-start.4 = (f32[1,128]{1,0:T(1,128)S(1)}, f32[1,128]{1,0:T(1,128)S(1)}, u32[]{:S(2)}, u32[]{:S(2)}) collective-permute-start(f32[1,128]{1,0:T(1,128)S(1)} %multiply_bitcast_fusion), channel_id=1, source_target_pairs={{0,2},{2,4},{4,6},{6,0},{1,3},{3,5},{5,7},{7,1},{8,10},{10,12},{12... | collective-permute-start | bytes 1544 | tf_op jit(solution)/shard_map/ppermute | solution.py:31
  103.1 5.8 %collective-permute-start.5 = (f32[1,128]{1,0:T(1,128)S(1)}, f32[1,128]{1,0:T(1,128)S(1)}, u32[]{:S(2)}, u32[]{:S(2)}) collective-permute-start(f32[1,128]{1,0:T(1,128)S(1)} %fusion.18), channel_id=1, source_target_pairs={{0,4},{2,6},{4,0},{6,2},{1,5},{3,7},{5,1},{7,3},{8,12},{10,14},{12... | collective-permute-start | bytes 1544 | tf_op jit(solution)/shard_map/ppermute | solution.py:31
  109.9 17.1 %all-to-all-start.3 = ((f16[8,24,1280]{2,1,0:T(8,128)(2,1)}), f16[8,24,1280]{2,1,0:T(8,128)(2,1)S(1)}, u32[]{:S(2)}, u32[]{:S(2)}) async-start(f16[8,24,1280]{2,1,0:T(8,128)(2,1)} %pad_maximum_fusion.2), calls=%async_computation.3 | async-start | bytes 983040 | tf_op jit(solution)/shard_map/all_to_all | solution.py:26
  113.4 13.7 %copy-start.3 = (bf16[24,1152]{1,0:T(8,128)(2,1)S(1)}, bf16[24,1152]{1,0:T(8,128)(2,1)}, u32[]{:S(2)}) copy-start(bf16[24,1152]{1,0:T(8,128)(2,1)} %param.6) | copy-start | bytes 165892

commit v7 on v6

--- a/solution.py
+++ b/solution.py
@@ -143,11 +143,11 @@
     ux, rx, uxb = normalize(images)
     uy, ry, uyb = normalize(texts)
 
-    own = spread(uxb.astype(jnp.bfloat16), "y").reshape(-1, width)
-    cols = (uyb * UNIT).astype(jnp.float16)
+    own = spread((uxb * UNIT).astype(jnp.float16), "y").reshape(-1, width)
+    cols = lax.all_gather((uyb * UNIT).astype(jnp.float16), Z + ("core",), axis=0, tiled=True)
     own, cols = lax.optimization_barrier((own, cols))
-    rows = spread(own, "x").reshape(-1, width)
-    cols = lax.all_gather(cols, Z + ("core",), axis=0, tiled=True)
+    rows = lax.all_gather(own, "x", axis=0, tiled=True)
+    rows = (rows.astype(jnp.float32) * (1 / UNIT)).astype(jnp.bfloat16)
     cols = (cols.astype(jnp.float32) * (1 / UNIT)).astype(jnp.bfloat16)
     cols = cols.reshape(8, 2, txt_rows, width)
     mine = lax.dynamic_index_in_dim(cols, core, 1, keepdims=False)
@@ -181,8 +181,7 @@
     got = shifted(theirs, "core", 1)
     dcols = ((got[:half] + mine) * 32.0).astype(jnp.float16).reshape(8, txt_rows, width)
     dcols, stats = swap_sum(dcols, got[half : half + 1, :128] + totals[:1, :128], Z)
-    for steps in (1, 2):
-        stats = stats + shifted(stats, "x", steps)
+    stats = jnp.sum(spread(stats, "x"), 0)
 
     drows = sum(part.astype(jnp.float32) for part in back.values())
     drows = (drows * 0.25).astype(jnp.float16).reshape(8, -1, width)

time: 131 us -> 133 us (1.015); the launches traced: 129 us -> 133 us
  blocking collectives: 27.4 us -> 45.4 us
  waiting for transfers between devices: 38.4 us -> 30.3 us
  starting transfers between devices: 40 us -> 34.5 us
    all_gather x1 -> x2, blocking collectives: 27.4 us -> 45.4 us  [the longest x1 27.2 us: body(): lax.all_gather((uyb * UNIT).astype(jnp.float16), Z + ('core',), axis=0, t...]
    all_to_all x4, waiting for transfers between devices: 30.9 us -> 24.4 us  [swap(): return lax.all_to_all(value, axis, 0, 0, tiled=False)]
    ppermute x6 -> x4, starting transfers between devices: 16.2 us -> 13.1 us  [shifted(): lax.ppermute(value, axis, [(i, (i + steps) % count) for i in range(count)])]
    all_to_all x4, starting transfers between devices: 23.8 us -> 21.3 us  [swap(): return lax.all_to_all(value, axis, 0, 0, tiled=False)]
    ppermute x6 -> x4, waiting for transfers between devices: 7.48 us -> 5.97 us  [shifted(): lax.ppermute(value, axis, [(i, (i + steps) % count) for i in range(count)])]
  transfers between devices with their start and end apart: 10 -> 8, of which waited for: 6 -> 4; matrix products, arithmetic and copies ran while one was open for 6% -> 6% of each run, Pallas kernels for 0% -> 0%
where the time goes in v7:
time: 133 us
  blocking collectives  45.4 us (34%)
  starting transfers between devices  34.5 us (26%)
  waiting for transfers between devices  30.3 us (23%)
  other arithmetic  7.33 us (6%)
  Pallas kernels  5.06 us (4%)
  matrix products  4.59 us (3%)
  local copies, waits for them, and re-layouts  3.26 us (2%)
  between operations  2.25 us (2%)
    all_gather x1, blocking collectives, body(): lax.all_gather((uyb * UNIT).astype(jnp.float16), Z + ('core',), axis=0, t...  27.2 us
    all_to_all x4, waiting for transfers between devices, swap(): return lax.all_to_all(value, axis, 0, 0, tiled=False)  24.4 us
    all_to_all x4, starting transfers between devices, swap(): return lax.all_to_all(value, axis, 0, 0, tiled=False)  21.3 us
    all_gather x1, blocking collectives, body(): rows = lax.all_gather(own, 'x', axis=0, tiled=True)  18.3 us
    ppermute x4, starting transfers between devices, shifted(): lax.ppermute(value, axis, [(i, (i + steps) % count) for i in range(count)])  13.1 us
    ppermute x4, waiting for transfers between devices, shifted(): lax.ppermute(value, axis, [(i, (i + steps) % count) for i in range(count)])  5.97 us
    dot_general x4, matrix products, body(): jnp.dot(near[k * high:(k + 1) * high], cols, preferred_element_type=jnp.f...  4.59 us
    pallas_call x1, Pallas kernels, slopes_of(): pl.pallas_call(slopes_kernel, in_specs=[SMEM, SMEM, VMEM, VMEM, VMEM, VME...  3.47 us
  transfers between devices with their start and end apart: 8, of which 4 were waited for; matrix products, arithmetic and copies ran while one was open for 6% of the time, Pallas kernels for 0%

profile of v7, /device:TPU:1, one launch (start us, length us, event | category | flops | bytes accessed | tf_op | source)
XLA Modules:
  0.0 132.7 jit_solution(9403896615878848523)
XLA Ops:
  0.7 1.0 fusion.10
  1.7 0.9 multiply_convert_fusion.4
  2.6 0.8 broadcast_in_dim.18
  3.4 7.7 %all-to-all-start = ((f16[8,24,1152]{2,1,0:T(8,128)(2,1)}), f16[8,24,1152]{2,1,0:T(8,128)(2,1)S(1)}, u32[]{:S(2)}, u32[]{:S(2)}) async-start(f16[8,24,1152]{2,1,0:T(8,128)(2,1)} %broadcast_in_dim.18), calls=%async_computation | async-start | bytes 884736 | tf_op jit(solution)/shard_map/all_to_all | solution.py:26
  13.7 27.2 %all-gather.2 = f16[512,1152]{1,0:T(8,128)(2,1)S(1)} all-gather(f16[32,1152]{1,0:T(8,128)(2,1)S(1)} %multiply_convert_fusion.3), channel_id=1, replica_groups=mesh['y'=8,'zh'=2,'zl'=4,'x'=4,'core'=2] {'zh','zl','core'}, dimensions={0}, use_global_device_ids=true | all-gather | bytes 1253376 | tf_op jit(solution)/shard_map/all_gather | solution.py:147
  41.2 18.3 %all-gather.3 = f16[768,1152]{1,0:T(8,128)(2,1)S(1)} all-gather(f16[192,1152]{1,0:T(8,128)(2,1)S(1)} %bitcast.37), channel_id=1, replica_groups=mesh['y'=8,'zh'=2,'zl'=4,'x'=4,'core'=2] {'x'}, dimensions={0}, use_global_device_ids=true | all-gather | bytes 2211840 | tf_op jit(solution)/shard_map/all_gather | solution.py:149
  60.0 3.5 %slopes.1 = (bf16[768,512]{1,0:T(8,128)(2,1)S(1)}, f32[8,1152]{1,0:T(8,128)S(1)}) custom-call(s32[1]{0:T(128)} %bitcast.place, f32[2]{0:T(128)S(1)} %pad_maximum_fusion.3.scalars, bf16[768,1152]{1,0:T(8,128)(2,1)S(1)} %multiply_convert_fusion.rows, bf16[512,1152]{1,0:T(8,128)(2,1)S(1)} %bitcast.30, s32[768,1]{1,0:T(8,128)S(1)} %reshape.137.row_ids, ...), custom_call_target="tpu_custom_call" | custom-call | flops 1000000000 | bytes 4000000 | tf_op jit(solution)/shard_map/slopes/pallas_call | solution.py:88
  63.5 1.6 %text_products.1 = (f32[264,1152]{1,0:T(8,128)S(1)}, f32[256,1152]{1,0:T(8,128)S(1)}) custom-call(s32[1]{0:T(128)} %bitcast.place, bf16[768,1152]{1,0:T(8,128)(2,1)S(1)} %multiply_convert_fusion.rows, bf16[768,512]{1,0:T(8,128)(2,1)S(1)} %get-tuple-element.13.slopes, f32[8,1152]{1,0:T(8,128)S(1)} %get-tuple-element.14.totals), custom_call_target="tpu_custom_call" | custom-call | flops 1000000000 | bytes 5000000 | tf_op jit(solution)/shard_map/text_products/pallas_call | solution.py:104
  65.1 3.5 %collective-permute-start.3 = (f32[264,1152]{1,0:T(8,128)S(1)}, f32[264,1152]{1,0:T(8,128)S(1)}, u32[]{:S(2)}, u32[]{:S(2)}) collective-permute-start(f32[264,1152]{1,0:T(8,128)S(1)} %get-tuple-element.15), channel_id=1, source_target_pairs={{0,1},{1,0},{2,3},{3,2},{4,5},{5,4},{6,7},{7,6},{8,9},{9,8},{10,11... | collective-permute-start | bytes 3649544 | tf_op jit(solution)/shard_map/ppermute | solution.py:31
  68.7 2.4 %collective-permute-done.3 = f32[264,1152]{1,0:T(8,128)S(1)} collective-permute-done((f32[264,1152]{1,0:T(8,128)S(1)}, f32[264,1152]{1,0:T(8,128)S(1)}, u32[]{:S(2)}, u32[]{:S(2)}) %collective-permute-start.3) | collective-permute-done | bytes 1216544 | tf_op jit(solution)/shard_map/ppermute | solution.py:31
  71.4 1.0 pad_maximum_fusion.1
  72.4 3.5 %all-to-all-start.1 = ((f16[8,32,1280]{2,1,0:T(8,128)(2,1)}), f16[8,32,1280]{2,1,0:T(8,128)(2,1)S(1)}, u32[]{:S(2)}, u32[]{:S(2)}) async-start(f16[8,32,1280]{2,1,0:T(8,128)(2,1)} %pad_maximum_fusion.1), calls=%async_computation.1 | async-start | bytes 1310720 | tf_op jit(solution)/shard_map/all_to_all | solution.py:26
  76.4 1.2 fusion.1
  77.6 1.2 fusion
  78.8 3.1 %collective-permute-start = (f16[192,1152]{1,0:T(8,128)(2,1)}, f16[192,1152]{1,0:T(8,128)(2,1)}, u32[]{:S(2)}, u32[]{:S(2)}) collective-permute-start(f16[192,1152]{1,0:T(8,128)(2,1)} %fusion), channel_id=1, source_target_pairs={{0,4},{2,6},{4,0},{6,2},{1,5},{3,7},{5,1},{7,3},{8,12},{10,14},{12... | collective-permute-start | bytes 1327112 | tf_op jit(solution)/shard_map/ppermute | solution.py:31
  81.9 3.1 %collective-permute-start.1 = (f16[192,1152]{1,0:T(8,128)(2,1)}, f16[192,1152]{1,0:T(8,128)(2,1)}, u32[]{:S(2)}, u32[]{:S(2)}) collective-permute-start(f16[192,1152]{1,0:T(8,128)(2,1)} %fusion.1), channel_id=1, source_target_pairs={{0,2},{2,4},{4,6},{6,0},{1,3},{3,5},{5,7},{7,1},{8,10},{10,12},{12... | collective-permute-start | bytes 1327112 | tf_op jit(solution)/shard_map/ppermute | solution.py:31
  85.0 3.4 %collective-permute-start.2 = (f16[192,1152]{1,0:T(8,128)(2,1)S(1)}, f16[192,1152]{1,0:T(8,128)(2,1)}, u32[]{:S(2)}, u32[]{:S(2)}) collective-permute-start(f16[192,1152]{1,0:T(8,128)(2,1)S(1)} %fusion.2), channel_id=1, source_target_pairs={{0,6},{2,0},{4,2},{6,4},{1,7},{3,1},{5,3},{7,5},{8,14},{10,8},{12,... | collective-permute-start | bytes 1327112 | tf_op jit(solution)/shard_map/ppermute | solution.py:31
  88.5 8.2 %all-to-all-done.1 = f16[8,32,1280]{2,1,0:T(8,128)(2,1)S(1)} async-done(((f16[8,32,1280]{2,1,0:T(8,128)(2,1)}), f16[8,32,1280]{2,1,0:T(8,128)(2,1)S(1)}, u32[]{:S(2)}, u32[]{:S(2)}) %all-to-all-start.1) | async-done | bytes 655392 | tf_op jit(solution)/shard_map/all_to_all | solution.py:26
  97.3 3.2 %all-to-all-start.2 = ((f32[4,1,128]{2,1,0:T(1,128)}), f32[4,1,128]{2,1,0:T(1,128)S(1)}, u32[]{:S(2)}, u32[]{:S(2)}) async-start(f32[4,1,128]{2,1,0:T(1,128)} %broadcast_in_dim.21), calls=%async_computation.2 | async-start | bytes 4096 | tf_op jit(solution)/shard_map/all_to_all | solution.py:26
  100.5 3.6 %collective-permute-done.1 = f16[192,1152]{1,0:T(8,128)(2,1)} collective-permute-done((f16[192,1152]{1,0:T(8,128)(2,1)}, f16[192,1152]{1,0:T(8,128)(2,1)}, u32[]{:S(2)}, u32[]{:S(2)}) %collective-permute-start.1) | collective-permute-done | bytes 442400 | tf_op jit(solution)/shard_map/ppermute | solution.py:31
  104.1 1.8 %multiply_convert_fusion.2 = f16[192,1152]{1,0:T(8,128)(2,1)S(1)} fusion(f16[192,1152]{1,0:T(8,128)(2,1)} %collective-permute-done.2, f16[192,1152]{1,0:T(8,128)(2,1)} %collective-permute-done.1, f16[192,1152]{1,0:T(8,128)(2,1)} %collective-permute-done, bf16[512,1152]{1,0:T(8,128)(2,1)S(1)} %bitcast.34, bf16[768,512]{1,0:T(8,128)(2,1)S(1)} %get-tuple-element.13.slopes), kind=kOutput, calls=%fused_computation.15 | convolution fusion | flops 228483072 | bytes 3145728 | tf_op jit(solution)/shard_map/dot_general | solution.py:175
  106.0 0.9 pad_maximum_fusion.2
  106.9 6.9 %all-to-all-start.3 = ((f16[8,24,1280]{2,1,0:T(8,128)(2,1)}), f16[8,24,1280]{2,1,0:T(8,128)(2,1)S(1)}, u32[]{:S(2)}, u32[]{:S(2)}) async-start(f16[8,24,1280]{2,1,0:T(8,128)(2,1)} %pad_maximum_fusion.2), calls=%async_computation.3 | async-start | bytes 983040 | tf_op jit(solution)/shard_map/all_to_all | solution.py:26
  114.9 16.2 %all-to-all-done.3 = f16[8,24,1280]{2,1,0:T(8,128)(2,1)S(1)} async-done(((f16[8,24,1280]{2,1,0:T(8,128)(2,1)}), f16[8,24,1280]{2,1,0:T(8,128)(2,1)S(1)}, u32[]{:S(2)}, u32[]{:S(2)}) %all-to-all-start.3) | async-done | bytes 491552 | tf_op jit(solution)/shard_map/all_to_all | solution.py:26
  (55 shorter events, 6.5 us)
Async XLA Ops:
  0.6 11.7 %copy-start = (bf16[32,1152]{1,0:T(8,128)(2,1)S(1)}, bf16[32,1152]{1,0:T(8,128)(2,1)}, u32[]{:S(2)}) copy-start(bf16[32,1152]{1,0:T(8,128)(2,1)} %param.7) | copy-start | bytes 221188
  0.6 12.0 %copy-start.3 = (s32[12288]{0:T(1024)S(1)}, s32[12288]{0:T(1024)}, u32[]{:S(2)}) copy-start(s32[12288]{0:T(1024)} %param.8) | copy-start | bytes 147460
  0.7 12.5 %copy-start.2 = (s32[16384]{0:T(1024)S(1)}, s32[16384]{0:T(1024)}, u32[]{:S(2)}) copy-start(s32[16384]{0:T(1024)} %param.9) | copy-start | bytes 196612
  3.4 37.6 %all-to-all-start = ((f16[8,24,1152]{2,1,0:T(8,128)(2,1)}), f16[8,24,1152]{2,1,0:T(8,128)(2,1)S(1)}, u32[]{:S(2)}, u32[]{:S(2)}) async-start(f16[8,24,1152]{2,1,0:T(8,128)(2,1)} %broadcast_in_dim.18), calls=%async_computation | async-start | bytes 884736 | tf_op jit(solution)/shard_map/all_to_all | solution.py:26
  65.1 6.1 %collective-permute-start.3 = (f32[264,1152]{1,0:T(8,128)S(1)}, f32[264,1152]{1,0:T(8,128)S(1)}, u32[]{:S(2)}, u32[]{:S(2)}) collective-permute-start(f32[264,1152]{1,0:T(8,128)S(1)} %get-tuple-element.15), channel_id=1, source_target_pairs={{0,1},{1,0},{2,3},{3,2},{4,5},{5,4},{6,7},{7,6},{8,9},{9,8},{10,11... | collective-permute-start | bytes 3649544 | tf_op jit(solution)/shard_map/ppermute | solution.py:31
  72.4 24.2 %all-to-all-start.1 = ((f16[8,32,1280]{2,1,0:T(8,128)(2,1)}), f16[8,32,1280]{2,1,0:T(8,128)(2,1)S(1)}, u32[]{:S(2)}, u32[]{:S(2)}) async-start(f16[8,32,1280]{2,1,0:T(8,128)(2,1)} %pad_maximum_fusion.1), calls=%async_computation.1 | async-start | bytes 1310720 | tf_op jit(solution)/shard_map/all_to_all | solution.py:26
  78.8 21.7 %collective-permute-start = (f16[192,1152]{1,0:T(8,128)(2,1)}, f16[192,1152]{1,0:T(8,128)(2,1)}, u32[]{:S(2)}, u32[]{:S(2)}) collective-permute-start(f16[192,1152]{1,0:T(8,128)(2,1)} %fusion), channel_id=1, source_target_pairs={{0,4},{2,6},{4,0},{6,2},{1,5},{3,7},{5,1},{7,3},{8,12},{10,14},{12... | collective-permute-start | bytes 1327112 | tf_op jit(solution)/shard_map/ppermute | solution.py:31
  81.9 22.2 %collective-permute-start.1 = (f16[192,1152]{1,0:T(8,128)(2,1)}, f16[192,1152]{1,0:T(8,128)(2,1)}, u32[]{:S(2)}, u32[]{:S(2)}) collective-permute-start(f16[192,1152]{1,0:T(8,128)(2,1)} %fusion.1), channel_id=1, source_target_pairs={{0,2},{2,4},{4,6},{6,0},{1,3},{3,5},{5,7},{7,1},{8,10},{10,12},{12... | collective-permute-start | bytes 1327112 | tf_op jit(solution)/shard_map/ppermute | solution.py:31
  85.0 19.1 %collective-permute-start.2 = (f16[192,1152]{1,0:T(8,128)(2,1)S(1)}, f16[192,1152]{1,0:T(8,128)(2,1)}, u32[]{:S(2)}, u32[]{:S(2)}) collective-permute-start(f16[192,1152]{1,0:T(8,128)(2,1)S(1)} %fusion.2), channel_id=1, source_target_pairs={{0,6},{2,0},{4,2},{6,4},{1,7},{3,1},{5,3},{7,5},{8,14},{10,8},{12,... | collective-permute-start | bytes 1327112 | tf_op jit(solution)/shard_map/ppermute | solution.py:31
  97.3 8.6 %all-to-all-start.2 = ((f32[4,1,128]{2,1,0:T(1,128)}), f32[4,1,128]{2,1,0:T(1,128)S(1)}, u32[]{:S(2)}, u32[]{:S(2)}) async-start(f32[4,1,128]{2,1,0:T(1,128)} %broadcast_in_dim.21), calls=%async_computation.2 | async-start | bytes 4096 | tf_op jit(solution)/shard_map/all_to_all | solution.py:26
  106.9 24.2 %all-to-all-start.3 = ((f16[8,24,1280]{2,1,0:T(8,128)(2,1)}), f16[8,24,1280]{2,1,0:T(8,128)(2,1)S(1)}, u32[]{:S(2)}, u32[]{:S(2)}) async-start(f16[8,24,1280]{2,1,0:T(8,128)(2,1)} %pad_maximum_fusion.2), calls=%async_computation.3 | async-start | bytes 983040 | tf_op jit(solution)/shard_map/all_to_all | solution.py:26
  113.8 17.4 %copy-start.1 = (bf16[24,1152]{1,0:T(8,128)(2,1)S(1)}, bf16[24,1152]{1,0:T(8,128)(2,1)}, u32[]{:S(2)}) copy-start(bf16[24,1152]{1,0:T(8,128)(2,1)} %param.6) | copy-start | bytes 165892

commit v8 on v7

--- a/solution.py
+++ b/solution.py
@@ -1,3 +1,5 @@
+import functools
+
 import jax
 import jax.numpy as jnp
 from jax import lax
@@ -11,11 +13,35 @@
 UNIT = 16384.0
 
 
-def normalize(rows):
-    values = rows.astype(jnp.float32)
-    radius = jnp.sqrt(jnp.sum(values * values, -1, keepdims=True) + 1e-06)
-    unit = values / radius
-    return (unit, radius, lax.reduce_precision(unit, 8, 7))
+VMEM = pl.BlockSpec(memory_space=pltpu.VMEM)
+SMEM = pl.BlockSpec(memory_space=pltpu.SMEM)
+
+
+def normalize_kernel(images, texts, spread_images, text_bits, ux, rx, uy, ry):
+    for rows, unit, radius in ((images, ux, rx), (texts, uy, ry)):
+        values = rows[...].astype(jnp.float32)
+        length = jnp.sqrt(jnp.sum(values * values, -1, keepdims=True) + 1e-06)
+        unit[...] = values / length
+        radius[...] = jnp.broadcast_to(length, radius.shape)
+    for i in range(spread_images.shape[0]):
+        spread_images[i] = ux[...].astype(jnp.bfloat16)
+    text_bits[...] = uy[...].astype(jnp.bfloat16)
+
+
+def normalize(images, texts, copies):
+    shape = jax.ShapeDtypeStruct
+    full = lambda rows: [shape(rows.shape, jnp.float32), shape((rows.shape[0], 128), jnp.float32)]
+    return pl.pallas_call(
+        normalize_kernel,
+        in_specs=[VMEM] * 2,
+        out_specs=[VMEM] * 6,
+        out_shape=[shape((copies,) + images.shape, jnp.bfloat16), shape(texts.shape, jnp.bfloat16)]
+        + full(images)
+        + full(texts),
+        compiler_params=pltpu.CompilerParams(vmem_limit_bytes=8 * 2**20),
+        cost_estimate=pl.CostEstimate(flops=10**6, bytes_accessed=10**6, transcendentals=1000),
+        name="normalize",
+    )(images, texts)
 
 
 def unnormalize(unit, radius, grad):
@@ -62,25 +88,21 @@
     totals[...] = total
 
 
-def text_kernel(place, rows, slopes, totals, theirs, mine):
+def text_kernel(side, place, rows, slopes, totals, out):
     parts = 4
     high = rows.shape[0] // parts
-    half = mine.shape[0]
-    for side, out in ((slice(half, None), theirs), (slice(0, half), mine)):
-        for k in range(parts):
-            part = pl.ds(pl.multiple_of(lax.rem(place[0] + k, parts) * high, high), high)
-            product = lax.dot_general(
-                slopes[k * high : (k + 1) * high, side],
-                rows[part, :],
-                (((0,), (0,)), ((), ())),
-                preferred_element_type=jnp.float32,
-            )
-            out[:half, :] = product if k == 0 else out[:half, :] + product
-    theirs[half:, :] = totals[...]
-
-
-VMEM = pl.BlockSpec(memory_space=pltpu.VMEM)
-SMEM = pl.BlockSpec(memory_space=pltpu.SMEM)
+    half = slopes.shape[1] // 2
+    for k in range(parts):
+        part = pl.ds(pl.multiple_of(lax.rem(place[0] + k, parts) * high, high), high)
+        product = lax.dot_general(
+            slopes[k * high : (k + 1) * high, side * half : (side + 1) * half],
+            rows[part, :],
+            (((0,), (0,)), ((), ())),
+            preferred_element_type=jnp.float32,
+        )
+        out[:half, :] = product if k == 0 else out[:half, :] + product
+    if side:
+        out[half:, :] = totals[...]
 
 
 def slopes_of(place, scalars, rows, cols, row_ids, col_ids):
@@ -93,25 +115,22 @@
             jax.ShapeDtypeStruct((rows.shape[0], wide), jnp.bfloat16),
             jax.ShapeDtypeStruct((8, width), jnp.float32),
         ),
-        compiler_params=pltpu.CompilerParams(vmem_limit_bytes=48 * 2**20),
+        compiler_params=pltpu.CompilerParams(vmem_limit_bytes=20 * 2**20),
         cost_estimate=pl.CostEstimate(flops=10**9, bytes_accessed=4 * 10**6, transcendentals=10**6),
         name="slopes",
     )(place, scalars, rows, cols, row_ids, col_ids)
 
 
-def text_products(place, rows, slopes, totals):
+def text_products(side, place, rows, slopes, totals):
     half, width = slopes.shape[1] // 2, rows.shape[1]
     return pl.pallas_call(
-        text_kernel,
+        functools.partial(text_kernel, side),
         in_specs=[SMEM, VMEM, VMEM, VMEM],
-        out_specs=[VMEM, VMEM],
-        out_shape=(
-            jax.ShapeDtypeStruct((half + 8, width), jnp.float32),
-            jax.ShapeDtypeStruct((half, width), jnp.float32),
-        ),
-        compiler_params=pltpu.CompilerParams(vmem_limit_bytes=48 * 2**20),
-        cost_estimate=pl.CostEstimate(flops=10**9, bytes_accessed=5 * 10**6, transcendentals=0),
-        name="text_products",
+        out_specs=VMEM,
+        out_shape=jax.ShapeDtypeStruct((half + 8 * side, width), jnp.float32),
+        compiler_params=pltpu.CompilerParams(vmem_limit_bytes=16 * 2**20),
+        cost_estimate=pl.CostEstimate(flops=5 * 10**8, bytes_accessed=4 * 10**6, transcendentals=0),
+        name="text_products_%d" % side,
     )(place, rows, slopes, totals)
 
 
@@ -140,11 +159,11 @@
     y, x, core = (lax.axis_index(a) for a in ("y", "x", "core"))
     z = lax.axis_index(Z)
     scale = jnp.exp(log_scale[0])
-    ux, rx, uxb = normalize(images)
-    uy, ry, uyb = normalize(texts)
-
-    own = spread((uxb * UNIT).astype(jnp.float16), "y").reshape(-1, width)
-    cols = lax.all_gather((uyb * UNIT).astype(jnp.float16), Z + ("core",), axis=0, tiled=True)
+    copies, uyb, ux, rx, uy, ry = normalize(images, texts, lax.axis_size("y"))
+
+    own = (swap(copies, "y").reshape(-1, width).astype(jnp.float32) * UNIT).astype(jnp.float16)
+    cols = (uyb.astype(jnp.float32) * UNIT).astype(jnp.float16)
+    cols = lax.all_gather(cols, Z + ("core",), axis=0, tiled=True)
     own, cols = lax.optimization_barrier((own, cols))
     rows = lax.all_gather(own, "x", axis=0, tiled=True)
     rows = (rows.astype(jnp.float32) * (1 / UNIT)).astype(jnp.bfloat16)
@@ -177,8 +196,8 @@
     for k in (2, 1, 3):
         back[k] = shifted(back[k], "x", k)
 
-    theirs, mine = text_products(place, rows, near, totals)
-    got = shifted(theirs, "core", 1)
+    got = shifted(text_products(1, place, rows, near, totals), "core", 1)
+    mine = text_products(0, place, rows, near, totals)
     dcols = ((got[:half] + mine) * 32.0).astype(jnp.float16).reshape(8, txt_rows, width)
     dcols, stats = swap_sum(dcols, got[half : half + 1, :128] + totals[:1, :128], Z)
     stats = jnp.sum(spread(stats, "x"), 0)
@@ -191,8 +210,8 @@
     total_texts = txt_rows * 512
     image_accum = drows * 0.0625
     text_accum = dcols * (1 / 32.0)
-    image_grad = unnormalize(ux, rx, scale * image_accum)
-    text_grad = unnormalize(uy, ry, scale * text_accum)
+    image_grad = unnormalize(ux, rx[:, :1], scale * image_accum)
+    text_grad = unnormalize(uy, ry[:, :1], scale * text_accum)
     lane = lax.iota(jnp.int32, stats.shape[0])
     stats = stats * jnp.where(lane == 1, scale, 1.0) * (1.0 / total_texts)
     loss, scale_grad, bias_grad = stats[0:1], stats[1:2], stats[2:3]

time: 133 us -> 136 us (1.023)
  local copies, waits for them, and re-layouts: 3.26 us -> 5.15 us
  matrix products: 4.59 us -> 6.16 us
    unnamed x8 -> x6, local copies, waits for them, and re-layouts: 0.02 us -> 1.69 us
    dot_general x4, matrix products: 4.59 us -> 6.16 us  [body(): jnp.dot(near[k * high:(k + 1) * high], cols, preferred_element_type=jnp.f...]
  transfers between devices with their start and end apart: 8 -> 8, of which waited for: 4 -> 4; matrix products, arithmetic and copies ran while one was open for 6% -> 7% of each run, Pallas kernels for 0% -> 1%
where the time goes in v8:
time: 136 us; the launch traced here: 135 us
  blocking collectives  45.4 us (33%)
  starting transfers between devices  34.4 us (25%)
  waiting for transfers between devices  29.3 us (22%)
  other arithmetic  6.17 us (5%)
  matrix products  6.16 us (5%)
  Pallas kernels  6.14 us (5%)
  local copies, waits for them, and re-layouts  5.15 us (4%)
  between operations  2.2 us (2%)
    all_gather x1, blocking collectives, body(): cols = lax.all_gather(cols, Z + ('core',), axis=0, tiled=True)  27.2 us
    all_to_all x4, waiting for transfers between devices, swap(): return lax.all_to_all(value, axis, 0, 0, tiled=False)  23.4 us
    all_to_all x4, starting transfers between devices, swap(): return lax.all_to_all(value, axis, 0, 0, tiled=False)  21.3 us
    all_gather x1, blocking collectives, body(): rows = lax.all_gather(own, 'x', axis=0, tiled=True)  18.3 us
    ppermute x4, starting transfers between devices, shifted(): lax.ppermute(value, axis, [(i, (i + steps) % count) for i in range(count)])  13.1 us
    dot_general x4, matrix products, body(): jnp.dot(near[k * high:(k + 1) * high], cols, preferred_element_type=jnp.f...  6.16 us
    ppermute x4, waiting for transfers between devices, shifted(): lax.ppermute(value, axis, [(i, (i + steps) % count) for i in range(count)])  5.88 us
    pallas_call x1, Pallas kernels, slopes_of(): pl.pallas_call(slopes_kernel, in_specs=[SMEM, SMEM, VMEM, VMEM, VMEM, VME...  3.48 us
  transfers between devices with their start and end apart: 8, of which 4 were waited for; matrix products, arithmetic and copies ran while one was open for 7% of the time, Pallas kernels for 1%

profile of v8, /device:TPU:1, one launch (start us, length us, event | category | flops | bytes accessed | tf_op | source)
XLA Modules:
  0.0 135.0 jit_solution(4103187343865754059)
XLA Ops:
  0.6 0.9 copy-done
  2.3 0.9 normalize.1
  3.3 7.7 %all-to-all-start = ((bf16[8,24,1152]{2,1,0:T(8,128)(2,1)}), bf16[8,24,1152]{2,1,0:T(8,128)(2,1)S(1)}, u32[]{:S(2)}, u32[]{:S(2)}) async-start(bf16[8,24,1152]{2,1,0:T(8,128)(2,1)} %get-tuple-element.15), calls=%async_computation | async-start | bytes 884736 | tf_op jit(solution)/shard_map/all_to_all | solution.py:52
  12.2 1.2 reshape.119
  14.2 27.2 %all-gather.2 = f16[512,1152]{1,0:T(8,128)(2,1)S(1)} all-gather(f16[32,1152]{1,0:T(8,128)(2,1)S(1)} %multiply_convert_fusion.4), channel_id=1, replica_groups=mesh['y'=8,'zh'=2,'zl'=4,'x'=4,'core'=2] {'zh','zl','core'}, dimensions={0}, use_global_device_ids=true | all-gather | bytes 1253376 | tf_op jit(solution)/shard_map/all_gather | solution.py:166
  41.8 18.3 %all-gather.3 = f16[768,1152]{1,0:T(8,128)(2,1)S(1)} all-gather(f16[192,1152]{1,0:T(8,128)(2,1)S(1)} %bitcast.37), channel_id=1, replica_groups=mesh['y'=8,'zh'=2,'zl'=4,'x'=4,'core'=2] {'x'}, dimensions={0}, use_global_device_ids=true | all-gather | bytes 2211840 | tf_op jit(solution)/shard_map/all_gather | solution.py:168
  60.5 3.5 %slopes.1 = (bf16[768,512]{1,0:T(8,128)(2,1)S(1)}, f32[8,1152]{1,0:T(8,128)S(1)}) custom-call(s32[1]{0:T(128)} %bitcast.place, f32[2]{0:T(128)S(1)} %pad_maximum_fusion.3.scalars, bf16[768,1152]{1,0:T(8,128)(2,1)S(1)} %multiply_convert_fusion.rows, bf16[512,1152]{1,0:T(8,128)(2,1)S(1)} %bitcast.30, s32[768,1]{1,0:T(8,128)S(1)} %reshape.125.row_ids, ...), custom_call_target="tpu_custom_call" | custom-call | flops 1000000000 | bytes 4000000 | tf_op jit(solution)/shard_map/slopes/pallas_call | solution.py:110
  64.9 3.5 %collective-permute-start.3 = (f32[264,1152]{1,0:T(8,128)S(1)}, f32[264,1152]{1,0:T(8,128)S(1)}, u32[]{:S(2)}, u32[]{:S(2)}) collective-permute-start(f32[264,1152]{1,0:T(8,128)S(1)} %text_products_1.1), channel_id=1, source_target_pairs={{0,1},{1,0},{2,3},{3,2},{4,5},{5,4},{6,7},{7,6},{8,9},{9,8},{10,11... | collective-permute-start | bytes 3649544 | tf_op jit(solution)/shard_map/ppermute | solution.py:57
  69.4 1.5 %collective-permute-done.3 = f32[264,1152]{1,0:T(8,128)S(1)} collective-permute-done((f32[264,1152]{1,0:T(8,128)S(1)}, f32[264,1152]{1,0:T(8,128)S(1)}, u32[]{:S(2)}, u32[]{:S(2)}) %collective-permute-start.3) | collective-permute-done | bytes 1216544 | tf_op jit(solution)/shard_map/ppermute | solution.py:57
  71.3 1.0 pad_maximum_fusion.1
  72.3 3.5 %all-to-all-start.1 = ((f16[8,32,1280]{2,1,0:T(8,128)(2,1)}), f16[8,32,1280]{2,1,0:T(8,128)(2,1)S(1)}, u32[]{:S(2)}, u32[]{:S(2)}) async-start(f16[8,32,1280]{2,1,0:T(8,128)(2,1)} %pad_maximum_fusion.1), calls=%async_computation.1 | async-start | bytes 1310720 | tf_op jit(solution)/shard_map/all_to_all | solution.py:52
  75.8 1.2 fusion.2
  77.0 1.2 fusion.1
  78.2 1.2 fusion
  79.4 3.1 %collective-permute-start = (f16[192,1152]{1,0:T(8,128)(2,1)}, f16[192,1152]{1,0:T(8,128)(2,1)}, u32[]{:S(2)}, u32[]{:S(2)}) collective-permute-start(f16[192,1152]{1,0:T(8,128)(2,1)} %fusion), channel_id=1, source_target_pairs={{0,4},{2,6},{4,0},{6,2},{1,5},{3,7},{5,1},{7,3},{8,12},{10,14},{12... | collective-permute-start | bytes 1327112 | tf_op jit(solution)/shard_map/ppermute | solution.py:57
  82.5 3.1 %collective-permute-start.1 = (f16[192,1152]{1,0:T(8,128)(2,1)}, f16[192,1152]{1,0:T(8,128)(2,1)}, u32[]{:S(2)}, u32[]{:S(2)}) collective-permute-start(f16[192,1152]{1,0:T(8,128)(2,1)} %fusion.1), channel_id=1, source_target_pairs={{0,2},{2,4},{4,6},{6,0},{1,3},{3,5},{5,7},{7,1},{8,10},{10,12},{12... | collective-permute-start | bytes 1327112 | tf_op jit(solution)/shard_map/ppermute | solution.py:57
  85.6 3.4 %collective-permute-start.2 = (f16[192,1152]{1,0:T(8,128)(2,1)}, f16[192,1152]{1,0:T(8,128)(2,1)}, u32[]{:S(2)}, u32[]{:S(2)}) collective-permute-start(f16[192,1152]{1,0:T(8,128)(2,1)} %fusion.2), channel_id=1, source_target_pairs={{0,6},{2,0},{4,2},{6,4},{1,7},{3,1},{5,3},{7,5},{8,14},{10,8},{12,... | collective-permute-start | bytes 1327112 | tf_op jit(solution)/shard_map/ppermute | solution.py:57
  89.1 7.4 %all-to-all-done.1 = f16[8,32,1280]{2,1,0:T(8,128)(2,1)S(1)} async-done(((f16[8,32,1280]{2,1,0:T(8,128)(2,1)}), f16[8,32,1280]{2,1,0:T(8,128)(2,1)S(1)}, u32[]{:S(2)}, u32[]{:S(2)}) %all-to-all-start.1) | async-done | bytes 655392 | tf_op jit(solution)/shard_map/all_to_all | solution.py:52
  97.1 3.2 %all-to-all-start.2 = ((f32[4,1,128]{2,1,0:T(1,128)}), f32[4,1,128]{2,1,0:T(1,128)S(1)}, u32[]{:S(2)}, u32[]{:S(2)}) async-start(f32[4,1,128]{2,1,0:T(1,128)} %broadcast_in_dim.36), calls=%async_computation.2 | async-start | bytes 4096 | tf_op jit(solution)/shard_map/all_to_all | solution.py:52
  100.4 4.3 %collective-permute-done.1 = f16[192,1152]{1,0:T(8,128)(2,1)} collective-permute-done((f16[192,1152]{1,0:T(8,128)(2,1)}, f16[192,1152]{1,0:T(8,128)(2,1)}, u32[]{:S(2)}, u32[]{:S(2)}) %collective-permute-start.1) | collective-permute-done | bytes 442400 | tf_op jit(solution)/shard_map/ppermute | solution.py:57
  104.7 2.5 %multiply_convert_fusion.2 = f16[192,1152]{1,0:T(8,128)(2,1)} fusion(f16[192,1152]{1,0:T(8,128)(2,1)} %collective-permute-done.2, f16[192,1152]{1,0:T(8,128)(2,1)} %collective-permute-done.1, f16[192,1152]{1,0:T(8,128)(2,1)} %collective-permute-done, bf16[512,1152]{1,0:T(8,128)(2,1)S(1)} %bitcast.34, bf16[768,512]{1,0:T(8,128)(2,1)S(1)} %get-tuple-element.19.slopes), kind=kOutput, calls=%fused_computation.15 | convolution fusion | flops 228483072 | bytes 3145728 | tf_op jit(solution)/shard_map/dot_general | solution.py:194
  107.4 1.9 %pad_maximum_fusion.2 = f16[8,24,1280]{2,1,0:T(8,128)(2,1)} fusion(f16[8,24,128]{2,1,0:T(8,128)(2,1)S(1)} %broadcast_in_dim.38, f16[8,24,1152]{2,1,0:T(8,128)(2,1)} %bitcast.38), kind=kLoop, calls=%fused_computation.20 | loop fusion | flops 245760 | bytes 983040 | tf_op jit(solution)/shard_map/concatenate | solution.py:141
  109.3 6.9 %all-to-all-start.3 = ((f16[8,24,1280]{2,1,0:T(8,128)(2,1)}), f16[8,24,1280]{2,1,0:T(8,128)(2,1)S(1)}, u32[]{:S(2)}, u32[]{:S(2)}) async-start(f16[8,24,1280]{2,1,0:T(8,128)(2,1)} %pad_maximum_fusion.2), calls=%async_computation.3 | async-start | bytes 983040 | tf_op jit(solution)/shard_map/all_to_all | solution.py:52
  117.4 16.1 %all-to-all-done.3 = f16[8,24,1280]{2,1,0:T(8,128)(2,1)S(1)} async-done(((f16[8,24,1280]{2,1,0:T(8,128)(2,1)}), f16[8,24,1280]{2,1,0:T(8,128)(2,1)S(1)}, u32[]{:S(2)}, u32[]{:S(2)}) %all-to-all-start.3) | async-done | bytes 491552 | tf_op jit(solution)/shard_map/all_to_all | solution.py:52
  (52 shorter events, 8.1 us)
Async XLA Ops:
  0.6 0.9 copy-start
  1.5 0.8 copy-start.1
  2.3 11.2 %copy-start.2 = (s32[16384]{0:T(1024)S(1)}, s32[16384]{0:T(1024)}, u32[]{:S(2)}) copy-start(s32[16384]{0:T(1024)} %param.9) | copy-start | bytes 196612
  3.3 38.1 %all-to-all-start = ((bf16[8,24,1152]{2,1,0:T(8,128)(2,1)}), bf16[8,24,1152]{2,1,0:T(8,128)(2,1)S(1)}, u32[]{:S(2)}, u32[]{:S(2)}) async-start(bf16[8,24,1152]{2,1,0:T(8,128)(2,1)} %get-tuple-element.15), calls=%async_computation | async-start | bytes 884736 | tf_op jit(solution)/shard_map/all_to_all | solution.py:52
  64.9 6.1 %collective-permute-start.3 = (f32[264,1152]{1,0:T(8,128)S(1)}, f32[264,1152]{1,0:T(8,128)S(1)}, u32[]{:S(2)}, u32[]{:S(2)}) collective-permute-start(f32[264,1152]{1,0:T(8,128)S(1)} %text_products_1.1), channel_id=1, source_target_pairs={{0,1},{1,0},{2,3},{3,2},{4,5},{5,4},{6,7},{7,6},{8,9},{9,8},{10,11... | collective-permute-start | bytes 3649544 | tf_op jit(solution)/shard_map/ppermute | solution.py:57
  72.3 24.2 %all-to-all-start.1 = ((f16[8,32,1280]{2,1,0:T(8,128)(2,1)}), f16[8,32,1280]{2,1,0:T(8,128)(2,1)S(1)}, u32[]{:S(2)}, u32[]{:S(2)}) async-start(f16[8,32,1280]{2,1,0:T(8,128)(2,1)} %pad_maximum_fusion.1), calls=%async_computation.1 | async-start | bytes 1310720 | tf_op jit(solution)/shard_map/all_to_all | solution.py:52
  79.4 20.9 %collective-permute-start = (f16[192,1152]{1,0:T(8,128)(2,1)}, f16[192,1152]{1,0:T(8,128)(2,1)}, u32[]{:S(2)}, u32[]{:S(2)}) collective-permute-start(f16[192,1152]{1,0:T(8,128)(2,1)} %fusion), channel_id=1, source_target_pairs={{0,4},{2,6},{4,0},{6,2},{1,5},{3,7},{5,1},{7,3},{8,12},{10,14},{12... | collective-permute-start | bytes 1327112 | tf_op jit(solution)/shard_map/ppermute | solution.py:57
  82.5 22.2 %collective-permute-start.1 = (f16[192,1152]{1,0:T(8,128)(2,1)}, f16[192,1152]{1,0:T(8,128)(2,1)}, u32[]{:S(2)}, u32[]{:S(2)}) collective-permute-start(f16[192,1152]{1,0:T(8,128)(2,1)} %fusion.1), channel_id=1, source_target_pairs={{0,2},{2,4},{4,6},{6,0},{1,3},{3,5},{5,7},{7,1},{8,10},{10,12},{12... | collective-permute-start | bytes 1327112 | tf_op jit(solution)/shard_map/ppermute | solution.py:57
  85.6 19.1 %collective-permute-start.2 = (f16[192,1152]{1,0:T(8,128)(2,1)}, f16[192,1152]{1,0:T(8,128)(2,1)}, u32[]{:S(2)}, u32[]{:S(2)}) collective-permute-start(f16[192,1152]{1,0:T(8,128)(2,1)} %fusion.2), channel_id=1, source_target_pairs={{0,6},{2,0},{4,2},{6,4},{1,7},{3,1},{5,3},{7,5},{8,14},{10,8},{12,... | collective-permute-start | bytes 1327112 | tf_op jit(solution)/shard_map/ppermute | solution.py:57
  97.1 10.1 %all-to-all-start.2 = ((f32[4,1,128]{2,1,0:T(1,128)}), f32[4,1,128]{2,1,0:T(1,128)S(1)}, u32[]{:S(2)}, u32[]{:S(2)}) async-start(f32[4,1,128]{2,1,0:T(1,128)} %broadcast_in_dim.36), calls=%async_computation.2 | async-start | bytes 4096 | tf_op jit(solution)/shard_map/all_to_all | solution.py:52
  109.3 24.2 %all-to-all-start.3 = ((f16[8,24,1280]{2,1,0:T(8,128)(2,1)}), f16[8,24,1280]{2,1,0:T(8,128)(2,1)S(1)}, u32[]{:S(2)}, u32[]{:S(2)}) async-start(f16[8,24,1280]{2,1,0:T(8,128)(2,1)} %pad_maximum_fusion.2), calls=%async_computation.3 | async-start | bytes 983040 | tf_op jit(solution)/shard_map/all_to_all | solution.py:52

commit v9 on v8

--- a/solution.py
+++ b/solution.py
@@ -17,31 +17,30 @@
 SMEM = pl.BlockSpec(memory_space=pltpu.SMEM)
 
 
-def normalize_kernel(images, texts, spread_images, text_bits, ux, rx, uy, ry):
-    for rows, unit, radius in ((images, ux, rx), (texts, uy, ry)):
-        values = rows[...].astype(jnp.float32)
-        length = jnp.sqrt(jnp.sum(values * values, -1, keepdims=True) + 1e-06)
-        unit[...] = values / length
-        radius[...] = jnp.broadcast_to(length, radius.shape)
-    for i in range(spread_images.shape[0]):
-        spread_images[i] = ux[...].astype(jnp.bfloat16)
-    text_bits[...] = uy[...].astype(jnp.bfloat16)
-
-
-def normalize(images, texts, copies):
-    shape = jax.ShapeDtypeStruct
-    full = lambda rows: [shape(rows.shape, jnp.float32), shape((rows.shape[0], 128), jnp.float32)]
+def normalize_kernel(rows, copies, unit, radius):
+    values = rows[...].astype(jnp.float32)
+    length = jnp.sqrt(jnp.sum(values * values, -1, keepdims=True) + 1e-06)
+    values = values / length
+    unit[...] = values
+    radius[...] = jnp.broadcast_to(length, radius.shape)
+    for i in range(copies.shape[0]):
+        copies[i] = values.astype(jnp.bfloat16)
+
+
+def normalize(rows, count):
+    shapes = ((count,) + rows.shape, rows.shape, (rows.shape[0], 128))
+    whole = lambda shape: pl.BlockSpec(shape, lambda i: (0,) * len(shape))
+    types = (jnp.bfloat16, jnp.float32, jnp.float32)
     return pl.pallas_call(
         normalize_kernel,
-        in_specs=[VMEM] * 2,
-        out_specs=[VMEM] * 6,
-        out_shape=[shape((copies,) + images.shape, jnp.bfloat16), shape(texts.shape, jnp.bfloat16)]
-        + full(images)
-        + full(texts),
+        grid=(1,),
+        in_specs=[whole(rows.shape)],
+        out_specs=[whole(shape) for shape in shapes],
+        out_shape=[jax.ShapeDtypeStruct(*pair) for pair in zip(shapes, types)],
         compiler_params=pltpu.CompilerParams(vmem_limit_bytes=8 * 2**20),
         cost_estimate=pl.CostEstimate(flops=10**6, bytes_accessed=10**6, transcendentals=1000),
-        name="normalize",
-    )(images, texts)
+        name="normalize_%d" % count,
+    )(rows)
 
 
 def unnormalize(unit, radius, grad):
@@ -159,14 +158,14 @@
     y, x, core = (lax.axis_index(a) for a in ("y", "x", "core"))
     z = lax.axis_index(Z)
     scale = jnp.exp(log_scale[0])
-    copies, uyb, ux, rx, uy, ry = normalize(images, texts, lax.axis_size("y"))
-
-    own = (swap(copies, "y").reshape(-1, width).astype(jnp.float32) * UNIT).astype(jnp.float16)
-    cols = (uyb.astype(jnp.float32) * UNIT).astype(jnp.float16)
+    copies, ux, rx = normalize(images, lax.axis_size("y"))
+    uyb, uy, ry = normalize(texts, 1)
+
+    own = swap(copies, "y").reshape(-1, width)
+    cols = (uyb[0].astype(jnp.float32) * UNIT).astype(jnp.float16)
+    own, cols = lax.optimization_barrier((own, cols))
+    rows = spread(own, "x").reshape(-1, width)
     cols = lax.all_gather(cols, Z + ("core",), axis=0, tiled=True)
-    own, cols = lax.optimization_barrier((own, cols))
-    rows = lax.all_gather(own, "x", axis=0, tiled=True)
-    rows = (rows.astype(jnp.float32) * (1 / UNIT)).astype(jnp.bfloat16)
     cols = (cols.astype(jnp.float32) * (1 / UNIT)).astype(jnp.bfloat16)
     cols = cols.reshape(8, 2, txt_rows, width)
     mine = lax.dynamic_index_in_dim(cols, core, 1, keepdims=False)
@@ -193,15 +192,17 @@
     for k in (2, 1, 3, 0):
         drows = 64.0 * jnp.dot(near[k * high : (k + 1) * high], cols, preferred_element_type=jnp.float32)
         back[k] = drows.astype(jnp.float16) if k else drows
-    for k in (2, 1, 3):
-        back[k] = shifted(back[k], "x", k)
 
     got = shifted(text_products(1, place, rows, near, totals), "core", 1)
     mine = text_products(0, place, rows, near, totals)
     dcols = ((got[:half] + mine) * 32.0).astype(jnp.float16).reshape(8, txt_rows, width)
+    dcols, back[1], back[2], back[3] = lax.optimization_barrier((dcols, back[1], back[2], back[3]))
     dcols, stats = swap_sum(dcols, got[half : half + 1, :128] + totals[:1, :128], Z)
     stats = jnp.sum(spread(stats, "x"), 0)
 
+    back[0] = lax.optimization_barrier(back[0])
+    for k in (2, 1, 3):
+        back[k] = shifted(back[k], "x", k)
     drows = sum(part.astype(jnp.float32) for part in back.values())
     drows = (drows * 0.25).astype(jnp.float16).reshape(8, -1, width)
     drows, stats = swap_sum(drows, stats, "y")

time: 136 us -> 128 us (0.941)
  blocking collectives: 45.4 us -> 27.4 us
  waiting for transfers between devices: 29.3 us -> 36.2 us
  starting transfers between devices: 34.4 us -> 37.5 us
  local copies, waits for them, and re-layouts: 5.15 us -> 7.36 us
  matrix products: 6.16 us -> 4.2 us
    all_gather x1 -> x0, blocking collectives: 18.3 us -> none  [body(): rows = lax.all_gather(own, 'x', axis=0, tiled=True)]
    all_to_all x4 -> x5, waiting for transfers between devices: 23.4 us -> 35 us  [swap(): return lax.all_to_all(value, axis, 0, 0, tiled=False)]
    all_to_all x4 -> x5, starting transfers between devices: 21.3 us -> 27.3 us  [swap(): return lax.all_to_all(value, axis, 0, 0, tiled=False)]
    ppermute x4, waiting for transfers between devices: 5.88 us -> 1.14 us  [shifted(): lax.ppermute(value, axis, [(i, (i + steps) % count) for i in range(count)])]
    ppermute x4, starting transfers between devices: 13.1 us -> 10.2 us  [shifted(): lax.ppermute(value, axis, [(i, (i + steps) % count) for i in range(count)])]
    dot_general x4, matrix products: 6.16 us -> 4.2 us  [body(): jnp.dot(near[k * high:(k + 1) * high], cols, preferred_element_type=jnp.f...]
  transfers between devices with their start and end apart: 8 -> 9, of which waited for: 4 -> 5; matrix products, arithmetic and copies ran while one was open for 7% -> 8% of each run, Pallas kernels for 1% -> 1%
where the time goes in v9:
time: 128 us; the launch traced here: 127 us
  starting transfers between devices  37.5 us (29%)
  waiting for transfers between devices  36.2 us (28%)
  blocking collectives  27.4 us (21%)
  local copies, waits for them, and re-layouts  7.36 us (6%)
  other arithmetic  6.26 us (5%)
  Pallas kernels  6.25 us (5%)
  matrix products  4.2 us (3%)
  between operations  2.24 us (2%)
    all_to_all x5, waiting for transfers between devices, swap(): return lax.all_to_all(value, axis, 0, 0, tiled=False)  35 us
    all_gather x1, blocking collectives, body(): cols = lax.all_gather(cols, Z + ('core',), axis=0, tiled=True)  27.4 us
    all_to_all x5, starting transfers between devices, swap(): return lax.all_to_all(value, axis, 0, 0, tiled=False)  27.3 us
    ppermute x4, starting transfers between devices, shifted(): lax.ppermute(value, axis, [(i, (i + steps) % count) for i in range(count)])  10.2 us
    dot_general x4, matrix products, body(): jnp.dot(near[k * high:(k + 1) * high], cols, preferred_element_type=jnp.f...  4.2 us
    pallas_call x1, Pallas kernels, slopes_of(): pl.pallas_call(slopes_kernel, in_specs=[SMEM, SMEM, VMEM, VMEM, VMEM, VME...  3.48 us
  transfers between devices with their start and end apart: 9, of which 5 were waited for; matrix products, arithmetic and copies ran while one was open for 8% of the time, Pallas kernels for 1%

profile of v9, /device:TPU:1, one launch (start us, length us, event | category | flops | bytes accessed | tf_op | source)
XLA Modules:
  0.0 127.4 jit_solution(6396780477056115926)
XLA Ops:
  2.4 7.7 %all-to-all-start = ((bf16[8,24,1152]{2,1,0:T(8,128)(2,1)}), bf16[8,24,1152]{2,1,0:T(8,128)(2,1)S(1)}, u32[]{:S(2)}, u32[]{:S(2)}) async-start(bf16[8,24,1152]{2,1,0:T(8,128)(2,1)} %get-tuple-element.19), calls=%async_computation | async-start | bytes 884736 | tf_op jit(solution)/shard_map/all_to_all | solution.py:51
  11.3 1.2 reshape.127
  14.2 8.6 %all-to-all-done = bf16[8,24,1152]{2,1,0:T(8,128)(2,1)S(1)} async-done(((bf16[8,24,1152]{2,1,0:T(8,128)(2,1)}), bf16[8,24,1152]{2,1,0:T(8,128)(2,1)S(1)}, u32[]{:S(2)}, u32[]{:S(2)}) %all-to-all-start) | async-done | bytes 442400 | tf_op jit(solution)/shard_map/all_to_all | solution.py:51
  22.7 1.4 %broadcast_in_dim.18 = bf16[4,192,1152]{2,1,0:T(8,128)(2,1)} broadcast(bf16[192,1152]{1,0:T(8,128)(2,1)S(1)} %bitcast.43), dimensions={1,2} | broadcast | bytes 2211840 | tf_op jit(solution)/shard_map/broadcast_in_dim | solution.py:61
  24.1 7.1 %all-to-all-start.1 = ((bf16[4,192,1152]{2,1,0:T(8,128)(2,1)}), bf16[4,192,1152]{2,1,0:T(8,128)(2,1)S(1)}, u32[]{:S(2)}, u32[]{:S(2)}) async-start(bf16[4,192,1152]{2,1,0:T(8,128)(2,1)} %broadcast_in_dim.18), calls=%async_computation.1 | async-start | bytes 3538944 | tf_op jit(solution)/shard_map/all_to_all | solution.py:51
  31.2 27.4 %all-gather.1 = f16[512,1152]{1,0:T(8,128)(2,1)S(1)} all-gather(f16[32,1152]{1,0:T(8,128)(2,1)S(1)} %fusion.9), channel_id=1, replica_groups=mesh['y'=8,'zh'=2,'zl'=4,'x'=4,'core'=2] {'zh','zl','core'}, dimensions={0}, use_global_device_ids=true | all-gather | bytes 1253376 | tf_op jit(solution)/shard_map/all_gather | solution.py:168
  59.0 1.0 copy-done.1
  60.0 3.5 %slopes.1 = (bf16[768,512]{1,0:T(8,128)(2,1)S(1)}, f32[8,1152]{1,0:T(8,128)S(1)}) custom-call(s32[1]{0:T(128)} %bitcast.place, f32[2]{0:T(128)S(1)} %pad_maximum_fusion.3.scalars, bf16[768,1152]{1,0:T(8,128)(2,1)S(1)} %bitcast.38, bf16[512,1152]{1,0:T(8,128)(2,1)S(1)} %bitcast.33, s32[768,1]{1,0:T(8,128)S(1)} %copy-done.1, s32[1,512]{1,0:T(1,128)S(1)} %reshape.130.col_ids), custom_call_target="tpu_custom_call" | custom-call | flops 1000000000 | bytes 4000000 | tf_op jit(solution)/shard_map/slopes/pallas_call | solution.py:109
  64.4 2.1 %collective-permute-start = (f32[264,1152]{1,0:T(8,128)S(1)}, f32[264,1152]{1,0:T(8,128)S(1)}, u32[]{:S(2)}, u32[]{:S(2)}) collective-permute-start(f32[264,1152]{1,0:T(8,128)S(1)} %text_products_1.1), channel_id=1, source_target_pairs={{0,1},{1,0},{2,3},{3,2},{4,5},{5,4},{6,7},{7,6},{8,9},{9,8},{10,11... | collective-permute-start | bytes 3649544 | tf_op jit(solution)/shard_map/ppermute | solution.py:56
  67.4 1.2 fusion
  69.1 1.2 fusion.2
  70.6 1.0 pad_maximum_fusion.1
  71.6 5.8 %all-to-all-start.2 = ((f16[8,32,1280]{2,1,0:T(8,128)(2,1)}), f16[8,32,1280]{2,1,0:T(8,128)(2,1)S(1)}, u32[]{:S(2)}, u32[]{:S(2)}) async-start(f16[8,32,1280]{2,1,0:T(8,128)(2,1)} %pad_maximum_fusion.1), calls=%async_computation.2 | async-start | bytes 1310720 | tf_op jit(solution)/shard_map/all_to_all | solution.py:51
  77.5 2.8 %collective-permute-start.3 = (f16[192,1152]{1,0:T(8,128)(2,1)}, f16[192,1152]{1,0:T(8,128)(2,1)}, u32[]{:S(2)}, u32[]{:S(2)}) collective-permute-start(f16[192,1152]{1,0:T(8,128)(2,1)} %fusion.2), channel_id=1, source_target_pairs={{0,6},{2,0},{4,2},{6,4},{1,7},{3,1},{5,3},{7,5},{8,14},{10,8},{12,... | collective-permute-start | bytes 1327112 | tf_op jit(solution)/shard_map/ppermute | solution.py:56
  80.3 2.5 %collective-permute-start.2 = (f16[192,1152]{1,0:T(8,128)(2,1)}, f16[192,1152]{1,0:T(8,128)(2,1)}, u32[]{:S(2)}, u32[]{:S(2)}) collective-permute-start(f16[192,1152]{1,0:T(8,128)(2,1)} %fusion), channel_id=1, source_target_pairs={{0,2},{2,4},{4,6},{6,0},{1,3},{3,5},{5,7},{7,1},{8,10},{10,12},{12... | collective-permute-start | bytes 1327112 | tf_op jit(solution)/shard_map/ppermute | solution.py:56
  82.8 2.9 %collective-permute-start.1 = (f16[192,1152]{1,0:T(8,128)(2,1)S(1)}, f16[192,1152]{1,0:T(8,128)(2,1)}, u32[]{:S(2)}, u32[]{:S(2)}) collective-permute-start(f16[192,1152]{1,0:T(8,128)(2,1)S(1)} %fusion.1), channel_id=1, source_target_pairs={{0,4},{2,6},{4,0},{6,2},{1,5},{3,7},{5,1},{7,3},{8,12},{10,14},{12... | collective-permute-start | bytes 1327112 | tf_op jit(solution)/shard_map/ppermute | solution.py:56
  85.7 1.4 %convolution_multiply_fusion = f32[192,1152]{1,0:T(8,128)S(1)} fusion(bf16[512,1152]{1,0:T(8,128)(2,1)S(1)} %bitcast.37, bf16[768,512]{1,0:T(8,128)(2,1)} %copy-done), kind=kOutput, calls=%fused_computation | convolution fusion | flops 226713600 | bytes 2260992 | tf_op jit(solution)/shard_map/dot_general | solution.py:193
  87.0 11.2 %all-to-all-done.2 = f16[8,32,1280]{2,1,0:T(8,128)(2,1)S(1)} async-done(((f16[8,32,1280]{2,1,0:T(8,128)(2,1)}), f16[8,32,1280]{2,1,0:T(8,128)(2,1)S(1)}, u32[]{:S(2)}, u32[]{:S(2)}) %all-to-all-start.2) | async-done | bytes 655392 | tf_op jit(solution)/shard_map/all_to_all | solution.py:51
  98.8 3.2 %all-to-all-start.3 = ((f32[4,1,128]{2,1,0:T(1,128)}), f32[4,1,128]{2,1,0:T(1,128)S(1)}, u32[]{:S(2)}, u32[]{:S(2)}) async-start(f32[4,1,128]{2,1,0:T(1,128)} %broadcast_in_dim.21), calls=%async_computation.3 | async-start | bytes 4096 | tf_op jit(solution)/shard_map/all_to_all | solution.py:51
  102.1 1.1 collective-permute-done.1
  103.2 1.6 %multiply_convert_fusion.1 = f16[192,1152]{1,0:T(8,128)(2,1)S(1)} fusion(f32[192,1152]{1,0:T(8,128)S(1)} %convolution_multiply_fusion, f16[192,1152]{1,0:T(8,128)(2,1)} %collective-permute-done.3, f16[192,1152]{1,0:T(8,128)(2,1)} %collective-permute-done.2, f16[192,1152]{1,0:T(8,128)(2,1)} %collective-permute-done.1), kind=kLoop, calls=%fused_computation.14 | loop fusion | flops 1769472 | bytes 2654208 | tf_op jit(solution)/shard_map/convert_element_type | solution.py:207
  104.8 1.3 %all-to-all-done.3 = f32[4,1,128]{2,1,0:T(1,128)S(1)} async-done(((f32[4,1,128]{2,1,0:T(1,128)}), f32[4,1,128]{2,1,0:T(1,128)S(1)}, u32[]{:S(2)}, u32[]{:S(2)}) %all-to-all-start.3) | async-done | bytes 2080 | tf_op jit(solution)/shard_map/all_to_all | solution.py:51
  107.1 3.5 %all-to-all-start.4 = ((f16[8,24,1280]{2,1,0:T(8,128)(2,1)}), f16[8,24,1280]{2,1,0:T(8,128)(2,1)S(1)}, u32[]{:S(2)}, u32[]{:S(2)}) async-start(f16[8,24,1280]{2,1,0:T(8,128)(2,1)} %pad_maximum_fusion.2), calls=%async_computation.4 | async-start | bytes 983040 | tf_op jit(solution)/shard_map/all_to_all | solution.py:51
  111.8 14.0 %all-to-all-done.4 = f16[8,24,1280]{2,1,0:T(8,128)(2,1)S(1)} async-done(((f16[8,24,1280]{2,1,0:T(8,128)(2,1)}), f16[8,24,1280]{2,1,0:T(8,128)(2,1)S(1)}, u32[]{:S(2)}, u32[]{:S(2)}) %all-to-all-start.4) | async-done | bytes 491552 | tf_op jit(solution)/shard_map/all_to_all | solution.py:51
  (58 shorter events, 10.7 us)
Async XLA Ops:
  0.6 0.8 copy-start.3
  1.4 12.1 %copy-start.4 = (s32[16384]{0:T(1024)S(1)}, s32[16384]{0:T(1024)}, u32[]{:S(2)}) copy-start(s32[16384]{0:T(1024)} %param.9) | copy-start | bytes 196612
  1.4 12.5 %copy-start.2 = (bf16[32,1152]{1,0:T(8,128)(2,1)S(1)}, bf16[32,1152]{1,0:T(8,128)(2,1)}, u32[]{:S(2)}) copy-start(bf16[32,1152]{1,0:T(8,128)(2,1)} %rows.3) | copy-start | bytes 221188
  2.4 20.4 %all-to-all-start = ((bf16[8,24,1152]{2,1,0:T(8,128)(2,1)}), bf16[8,24,1152]{2,1,0:T(8,128)(2,1)S(1)}, u32[]{:S(2)}, u32[]{:S(2)}) async-start(bf16[8,24,1152]{2,1,0:T(8,128)(2,1)} %get-tuple-element.19), calls=%async_computation | async-start | bytes 884736 | tf_op jit(solution)/shard_map/all_to_all | solution.py:51
  24.1 35.0 %all-to-all-start.1 = ((bf16[4,192,1152]{2,1,0:T(8,128)(2,1)}), bf16[4,192,1152]{2,1,0:T(8,128)(2,1)S(1)}, u32[]{:S(2)}, u32[]{:S(2)}) async-start(bf16[4,192,1152]{2,1,0:T(8,128)(2,1)} %broadcast_in_dim.18), calls=%async_computation.1 | async-start | bytes 3538944 | tf_op jit(solution)/shard_map/all_to_all | solution.py:51
  59.0 1.0 copy-start.1
  63.5 5.5 %copy-start = (bf16[768,512]{1,0:T(8,128)(2,1)}, bf16[768,512]{1,0:T(8,128)(2,1)S(1)}, u32[]{:S(2)}) copy-start(bf16[768,512]{1,0:T(8,128)(2,1)S(1)} %get-tuple-element.23.slopes) | copy-start | bytes 2359300
  64.4 5.9 %collective-permute-start = (f32[264,1152]{1,0:T(8,128)S(1)}, f32[264,1152]{1,0:T(8,128)S(1)}, u32[]{:S(2)}, u32[]{:S(2)}) collective-permute-start(f32[264,1152]{1,0:T(8,128)S(1)} %text_products_1.1), channel_id=1, source_target_pairs={{0,1},{1,0},{2,3},{3,2},{4,5},{5,4},{6,7},{7,6},{8,9},{9,8},{10,11... | collective-permute-start | bytes 3649544 | tf_op jit(solution)/shard_map/ppermute | solution.py:56
  71.6 26.6 %all-to-all-start.2 = ((f16[8,32,1280]{2,1,0:T(8,128)(2,1)}), f16[8,32,1280]{2,1,0:T(8,128)(2,1)S(1)}, u32[]{:S(2)}, u32[]{:S(2)}) async-start(f16[8,32,1280]{2,1,0:T(8,128)(2,1)} %pad_maximum_fusion.1), calls=%async_computation.2 | async-start | bytes 1310720 | tf_op jit(solution)/shard_map/all_to_all | solution.py:51
  77.5 24.6 %collective-permute-start.3 = (f16[192,1152]{1,0:T(8,128)(2,1)}, f16[192,1152]{1,0:T(8,128)(2,1)}, u32[]{:S(2)}, u32[]{:S(2)}) collective-permute-start(f16[192,1152]{1,0:T(8,128)(2,1)} %fusion.2), channel_id=1, source_target_pairs={{0,6},{2,0},{4,2},{6,4},{1,7},{3,1},{5,3},{7,5},{8,14},{10,8},{12,... | collective-permute-start | bytes 1327112 | tf_op jit(solution)/shard_map/ppermute | solution.py:56
  80.3 21.8 %collective-permute-start.2 = (f16[192,1152]{1,0:T(8,128)(2,1)}, f16[192,1152]{1,0:T(8,128)(2,1)}, u32[]{:S(2)}, u32[]{:S(2)}) collective-permute-start(f16[192,1152]{1,0:T(8,128)(2,1)} %fusion), channel_id=1, source_target_pairs={{0,2},{2,4},{4,6},{6,0},{1,3},{3,5},{5,7},{7,1},{8,10},{10,12},{12... | collective-permute-start | bytes 1327112 | tf_op jit(solution)/shard_map/ppermute | solution.py:56
  82.8 20.4 %collective-permute-start.1 = (f16[192,1152]{1,0:T(8,128)(2,1)S(1)}, f16[192,1152]{1,0:T(8,128)(2,1)}, u32[]{:S(2)}, u32[]{:S(2)}) collective-permute-start(f16[192,1152]{1,0:T(8,128)(2,1)S(1)} %fusion.1), channel_id=1, source_target_pairs={{0,4},{2,6},{4,0},{6,2},{1,5},{3,7},{5,1},{7,3},{8,12},{10,14},{12... | collective-permute-start | bytes 1327112 | tf_op jit(solution)/shard_map/ppermute | solution.py:56
  98.8 7.2 %all-to-all-start.3 = ((f32[4,1,128]{2,1,0:T(1,128)}), f32[4,1,128]{2,1,0:T(1,128)S(1)}, u32[]{:S(2)}, u32[]{:S(2)}) async-start(f32[4,1,128]{2,1,0:T(1,128)} %broadcast_in_dim.21), calls=%async_computation.3 | async-start | bytes 4096 | tf_op jit(solution)/shard_map/all_to_all | solution.py:51
  107.1 18.7 %all-to-all-start.4 = ((f16[8,24,1280]{2,1,0:T(8,128)(2,1)}), f16[8,24,1280]{2,1,0:T(8,128)(2,1)S(1)}, u32[]{:S(2)}, u32[]{:S(2)}) async-start(f16[8,24,1280]{2,1,0:T(8,128)(2,1)} %pad_maximum_fusion.2), calls=%async_computation.4 | async-start | bytes 983040 | tf_op jit(solution)/shard_map/all_to_all | solution.py:51

commit v10 on v9

--- a/solution.py
+++ b/solution.py
@@ -65,13 +65,17 @@
     parts = 4
     high = rows.shape[0] // parts
     sums = [0.0, 0.0, 0.0]
+    ones = jnp.ones((row_ids.shape[1], cols.shape[0]), jnp.bfloat16)
     for k in range(parts):
         part = pl.ds(pl.multiple_of(lax.rem(place[0] + k, parts) * high, high), high)
         dots = lax.dot_general(
             rows[part, :], cols[...], (((1,), (1,)), ((), ())), preferred_element_type=jnp.float32
         )
         logits = scalars[0] * dots + scalars[1]
-        match = row_ids[part, :] == col_ids[...]
+        spot = lax.dot_general(
+            row_ids[lax.rem(place[0] + k, parts)], ones, (((0,), (0,)), ((), ())), preferred_element_type=jnp.float32
+        )
+        match = spot == col_ids[...]
         against = jnp.where(match, -logits, logits)
         decay = jnp.exp(-jnp.abs(against))
         objective = jnp.maximum(against, 0.0) + jnp.log1p(decay)
@@ -177,11 +181,13 @@
     col_ids = lax.dynamic_index_in_dim(col_ids, x, 1, keepdims=False)
     mine = lax.dynamic_index_in_dim(col_ids, core, 1, keepdims=False)
     theirs = lax.dynamic_index_in_dim(col_ids, 1 - core, 1, keepdims=False)
-    col_ids = jnp.concatenate([mine, theirs], 0).reshape(1, -1)
+    col_ids = jnp.concatenate([mine, theirs], 0).reshape(1, -1).astype(jnp.float32)
     row_ids = image_ids.reshape(8, 8, 4, 2, img_rows)
     row_ids = lax.dynamic_index_in_dim(row_ids, z, 1, keepdims=False)
     row_ids = lax.dynamic_index_in_dim(row_ids, core, 2, keepdims=False)
-    row_ids = row_ids.transpose(1, 0, 2).reshape(-1, 1)
+    row_ids = row_ids.transpose(1, 0, 2).reshape(4, 1, -1)
+    row_ids = jnp.concatenate([row_ids & -128, row_ids & 127, jnp.zeros((4, 6, 8 * img_rows), jnp.int32)], 1)
+    row_ids = row_ids.astype(jnp.bfloat16)
 
     half = cols.shape[0] // 2
     high = rows.shape[0] // 4
@@ -200,7 +206,6 @@
     dcols, stats = swap_sum(dcols, got[half : half + 1, :128] + totals[:1, :128], Z)
     stats = jnp.sum(spread(stats, "x"), 0)
 
-    back[0] = lax.optimization_barrier(back[0])
     for k in (2, 1, 3):
         back[k] = shifted(back[k], "x", k)
     drows = sum(part.astype(jnp.float32) for part in back.values())

time: 128 us -> 126 us (0.984)
  other arithmetic: 6.26 us -> 4.77 us
    convert_element_type x1, other arithmetic: 1.57 us -> 0.01 us  [body(): jnp.concatenate([mine, theirs], 0).reshape(1, -1).astype(jnp.float32)]
  transfers between devices with their start and end apart: 9 -> 9, of which waited for: 5 -> 6; matrix products, arithmetic and copies ran while one was open for 8% -> 6% of each run, Pallas kernels for 1% -> 1%
where the time goes in v10:
time: 126 us; the launch traced here: 125 us
  starting transfers between devices  37.5 us (30%)
  waiting for transfers between devices  37.1 us (29%)
  blocking collectives  27.4 us (22%)
  local copies, waits for them, and re-layouts  6.6 us (5%)
  Pallas kernels  6.24 us (5%)
  other arithmetic  4.77 us (4%)
  matrix products  3.16 us (3%)
  between operations  2.26 us (2%)
    all_to_all x5, waiting for transfers between devices, swap(): return lax.all_to_all(value, axis, 0, 0, tiled=False)  35.3 us
    all_gather x1, blocking collectives, body(): cols = lax.all_gather(cols, Z + ('core',), axis=0, tiled=True)  27.4 us
    all_to_all x5, starting transfers between devices, swap(): return lax.all_to_all(value, axis, 0, 0, tiled=False)  27.1 us
    ppermute x4, starting transfers between devices, shifted(): lax.ppermute(value, axis, [(i, (i + steps) % count) for i in range(count)])  10.5 us
    pallas_call x1, Pallas kernels, slopes_of(): pl.pallas_call(slopes_kernel, in_specs=[SMEM, SMEM, VMEM, VMEM, VMEM, VME...  3.47 us
    dot_general x4, matrix products, body(): jnp.dot(near[k * high:(k + 1) * high], cols, preferred_element_type=jnp.f...  3.16 us
  transfers between devices with their start and end apart: 9, of which 6 were waited for; matrix products, arithmetic and copies ran while one was open for 6% of the time, Pallas kernels for 1%

profile of v10, /device:TPU:1, one launch (start us, length us, event | category | flops | bytes accessed | tf_op | source)
XLA Modules:
  0.0 125.0 jit_solution(8756814707667328913)
XLA Ops:
  1.4 0.9 normalize_8.1
  2.3 7.7 %all-to-all-start = ((bf16[8,24,1152]{2,1,0:T(8,128)(2,1)}), bf16[8,24,1152]{2,1,0:T(8,128)(2,1)S(1)}, u32[]{:S(2)}, u32[]{:S(2)}) async-start(bf16[8,24,1152]{2,1,0:T(8,128)(2,1)} %get-tuple-element.19), calls=%async_computation | async-start | bytes 884736 | tf_op jit(solution)/shard_map/all_to_all | solution.py:51
  11.4 0.9 copy-done.1
  12.4 1.2 reshape.172
  14.5 8.2 %all-to-all-done = bf16[8,24,1152]{2,1,0:T(8,128)(2,1)S(1)} async-done(((bf16[8,24,1152]{2,1,0:T(8,128)(2,1)}), bf16[8,24,1152]{2,1,0:T(8,128)(2,1)S(1)}, u32[]{:S(2)}, u32[]{:S(2)}) %all-to-all-start) | async-done | bytes 442400 | tf_op jit(solution)/shard_map/all_to_all | solution.py:51
  22.7 1.4 %broadcast_in_dim.20 = bf16[4,192,1152]{2,1,0:T(8,128)(2,1)} broadcast(bf16[192,1152]{1,0:T(8,128)(2,1)S(1)} %bitcast.46), dimensions={1,2} | broadcast | bytes 2211840 | tf_op jit(solution)/shard_map/broadcast_in_dim | solution.py:61
  24.1 7.1 %all-to-all-start.1 = ((bf16[4,192,1152]{2,1,0:T(8,128)(2,1)}), bf16[4,192,1152]{2,1,0:T(8,128)(2,1)S(1)}, u32[]{:S(2)}, u32[]{:S(2)}) async-start(bf16[4,192,1152]{2,1,0:T(8,128)(2,1)} %broadcast_in_dim.20), calls=%async_computation.1 | async-start | bytes 3538944 | tf_op jit(solution)/shard_map/all_to_all | solution.py:51
  31.2 27.4 %all-gather.1 = f16[512,1152]{1,0:T(8,128)(2,1)S(1)} all-gather(f16[32,1152]{1,0:T(8,128)(2,1)S(1)} %fusion.9), channel_id=1, replica_groups=mesh['y'=8,'zh'=2,'zl'=4,'x'=4,'core'=2] {'zh','zl','core'}, dimensions={0}, use_global_device_ids=true | all-gather | bytes 1253376 | tf_op jit(solution)/shard_map/all_gather | solution.py:172
  59.0 3.5 %slopes.1 = (bf16[768,512]{1,0:T(8,128)(2,1)S(1)}, f32[8,1152]{1,0:T(8,128)S(1)}) custom-call(s32[1]{0:T(128)} %bitcast.place, f32[2]{0:T(128)S(1)} %pad_maximum_fusion.3.scalars, bf16[768,1152]{1,0:T(8,128)(2,1)S(1)} %bitcast.41, bf16[512,1152]{1,0:T(8,128)(2,1)S(1)} %bitcast.36, bf16[4,8,192]{2,1,0:T(8,128)(2,1)S(1)} %maximum_maximum_fusion.row_ids, ...), custom_call_target="tpu_custom_call" | custom-call | flops 1000000000 | bytes 4000000 | tf_op jit(solution)/shard_map/slopes/pallas_call | solution.py:113
  62.5 0.9 text_products_1.1
  63.4 2.1 %collective-permute-start = (f32[264,1152]{1,0:T(8,128)S(1)}, f32[264,1152]{1,0:T(8,128)S(1)}, u32[]{:S(2)}, u32[]{:S(2)}) collective-permute-start(f32[264,1152]{1,0:T(8,128)S(1)} %text_products_1.1), channel_id=1, source_target_pairs={{0,1},{1,0},{2,3},{3,2},{4,5},{5,4},{6,7},{7,6},{8,9},{9,8},{10,11... | collective-permute-start | bytes 3649544 | tf_op jit(solution)/shard_map/ppermute | solution.py:56
  65.5 0.9 text_products_0.1
  68.5 1.0 pad_maximum_fusion.1
  69.5 5.6 %all-to-all-start.2 = ((f16[8,32,1280]{2,1,0:T(8,128)(2,1)}), f16[8,32,1280]{2,1,0:T(8,128)(2,1)S(1)}, u32[]{:S(2)}, u32[]{:S(2)}) async-start(f16[8,32,1280]{2,1,0:T(8,128)(2,1)} %pad_maximum_fusion.1), calls=%async_computation.2 | async-start | bytes 1310720 | tf_op jit(solution)/shard_map/all_to_all | solution.py:51
  75.1 2.8 %collective-permute-start.3 = (f16[192,1152]{1,0:T(8,128)(2,1)S(1)}, f16[192,1152]{1,0:T(8,128)(2,1)}, u32[]{:S(2)}, u32[]{:S(2)}) collective-permute-start(f16[192,1152]{1,0:T(8,128)(2,1)S(1)} %fusion.2), channel_id=1, source_target_pairs={{0,6},{2,0},{4,2},{6,4},{1,7},{3,1},{5,3},{7,5},{8,14},{10,8},{12,... | collective-permute-start | bytes 1327112 | tf_op jit(solution)/shard_map/ppermute | solution.py:56
  77.9 2.5 %collective-permute-start.2 = (f16[192,1152]{1,0:T(8,128)(2,1)S(1)}, f16[192,1152]{1,0:T(8,128)(2,1)}, u32[]{:S(2)}, u32[]{:S(2)}) collective-permute-start(f16[192,1152]{1,0:T(8,128)(2,1)S(1)} %fusion), channel_id=1, source_target_pairs={{0,2},{2,4},{4,6},{6,0},{1,3},{3,5},{5,7},{7,1},{8,10},{10,12},{12... | collective-permute-start | bytes 1327112 | tf_op jit(solution)/shard_map/ppermute | solution.py:56
  80.4 3.1 %collective-permute-start.1 = (f16[192,1152]{1,0:T(8,128)(2,1)S(1)}, f16[192,1152]{1,0:T(8,128)(2,1)}, u32[]{:S(2)}, u32[]{:S(2)}) collective-permute-start(f16[192,1152]{1,0:T(8,128)(2,1)S(1)} %fusion.1), channel_id=1, source_target_pairs={{0,4},{2,6},{4,0},{6,2},{1,5},{3,7},{5,1},{7,3},{8,12},{10,14},{12... | collective-permute-start | bytes 1327112 | tf_op jit(solution)/shard_map/ppermute | solution.py:56
  83.6 12.3 %all-to-all-done.2 = f16[8,32,1280]{2,1,0:T(8,128)(2,1)S(1)} async-done(((f16[8,32,1280]{2,1,0:T(8,128)(2,1)}), f16[8,32,1280]{2,1,0:T(8,128)(2,1)S(1)}, u32[]{:S(2)}, u32[]{:S(2)}) %all-to-all-start.2) | async-done | bytes 655392 | tf_op jit(solution)/shard_map/all_to_all | solution.py:51
  96.4 3.2 %all-to-all-start.3 = ((f32[4,1,128]{2,1,0:T(1,128)}), f32[4,1,128]{2,1,0:T(1,128)S(1)}, u32[]{:S(2)}, u32[]{:S(2)}) async-start(f32[4,1,128]{2,1,0:T(1,128)} %broadcast_in_dim.47), calls=%async_computation.3 | async-start | bytes 4096 | tf_op jit(solution)/shard_map/all_to_all | solution.py:51
  99.7 1.3 %collective-permute-done.1 = f16[192,1152]{1,0:T(8,128)(2,1)} collective-permute-done((f16[192,1152]{1,0:T(8,128)(2,1)S(1)}, f16[192,1152]{1,0:T(8,128)(2,1)}, u32[]{:S(2)}, u32[]{:S(2)}) %collective-permute-start.1) | collective-permute-done | bytes 442400 | tf_op jit(solution)/shard_map/ppermute | solution.py:56
  101.0 1.9 %multiply_convert_fusion.1 = f16[192,1152]{1,0:T(8,128)(2,1)S(1)} fusion(f16[192,1152]{1,0:T(8,128)(2,1)} %collective-permute-done.3, f16[192,1152]{1,0:T(8,128)(2,1)} %collective-permute-done.2, f16[192,1152]{1,0:T(8,128)(2,1)} %collective-permute-done.1, bf16[512,1152]{1,0:T(8,128)(2,1)S(1)} %bitcast.40, bf16[768,512]{1,0:T(8,128)(2,1)} %copy-done), kind=kOutput, calls=%fused_computation.14 | convolution fusion | flops 228483072 | bytes 3145728 | tf_op jit(solution)/shard_map/dot_general | solution.py:199
  103.8 0.9 pad_maximum_fusion.2
  104.7 3.5 %all-to-all-start.4 = ((f16[8,24,1280]{2,1,0:T(8,128)(2,1)}), f16[8,24,1280]{2,1,0:T(8,128)(2,1)S(1)}, u32[]{:S(2)}, u32[]{:S(2)}) async-start(f16[8,24,1280]{2,1,0:T(8,128)(2,1)} %pad_maximum_fusion.2), calls=%async_computation.4 | async-start | bytes 983040 | tf_op jit(solution)/shard_map/all_to_all | solution.py:51
  109.4 14.0 %all-to-all-done.4 = f16[8,24,1280]{2,1,0:T(8,128)(2,1)S(1)} async-done(((f16[8,24,1280]{2,1,0:T(8,128)(2,1)}), f16[8,24,1280]{2,1,0:T(8,128)(2,1)S(1)}, u32[]{:S(2)}, u32[]{:S(2)}) %all-to-all-start.4) | async-done | bytes 491552 | tf_op jit(solution)/shard_map/all_to_all | solution.py:51
  (59 shorter events, 8.7 us)
Async XLA Ops:
  0.6 0.8 copy-start.2
  1.4 12.4 %copy-start.3 = (s32[16384]{0:T(1024)S(1)}, s32[16384]{0:T(1024)}, u32[]{:S(2)}) copy-start(s32[16384]{0:T(1024)} %param.9) | copy-start | bytes 196612
  2.3 20.4 %all-to-all-start = ((bf16[8,24,1152]{2,1,0:T(8,128)(2,1)}), bf16[8,24,1152]{2,1,0:T(8,128)(2,1)S(1)}, u32[]{:S(2)}, u32[]{:S(2)}) async-start(bf16[8,24,1152]{2,1,0:T(8,128)(2,1)} %get-tuple-element.19), calls=%async_computation | async-start | bytes 884736 | tf_op jit(solution)/shard_map/all_to_all | solution.py:51
  11.3 0.9 copy-start.1
  24.1 35.0 %all-to-all-start.1 = ((bf16[4,192,1152]{2,1,0:T(8,128)(2,1)}), bf16[4,192,1152]{2,1,0:T(8,128)(2,1)S(1)}, u32[]{:S(2)}, u32[]{:S(2)}) async-start(bf16[4,192,1152]{2,1,0:T(8,128)(2,1)} %broadcast_in_dim.20), calls=%async_computation.1 | async-start | bytes 3538944 | tf_op jit(solution)/shard_map/all_to_all | solution.py:51
  62.5 4.8 %copy-start = (bf16[768,512]{1,0:T(8,128)(2,1)}, bf16[768,512]{1,0:T(8,128)(2,1)S(1)}, u32[]{:S(2)}) copy-start(bf16[768,512]{1,0:T(8,128)(2,1)S(1)} %get-tuple-element.23.slopes) | copy-start | bytes 2359300
  63.4 4.8 %collective-permute-start = (f32[264,1152]{1,0:T(8,128)S(1)}, f32[264,1152]{1,0:T(8,128)S(1)}, u32[]{:S(2)}, u32[]{:S(2)}) collective-permute-start(f32[264,1152]{1,0:T(8,128)S(1)} %text_products_1.1), channel_id=1, source_target_pairs={{0,1},{1,0},{2,3},{3,2},{4,5},{5,4},{6,7},{7,6},{8,9},{9,8},{10,11... | collective-permute-start | bytes 3649544 | tf_op jit(solution)/shard_map/ppermute | solution.py:56
  69.5 26.4 %all-to-all-start.2 = ((f16[8,32,1280]{2,1,0:T(8,128)(2,1)}), f16[8,32,1280]{2,1,0:T(8,128)(2,1)S(1)}, u32[]{:S(2)}, u32[]{:S(2)}) async-start(f16[8,32,1280]{2,1,0:T(8,128)(2,1)} %pad_maximum_fusion.1), calls=%async_computation.2 | async-start | bytes 1310720 | tf_op jit(solution)/shard_map/all_to_all | solution.py:51
  75.1 24.6 %collective-permute-start.3 = (f16[192,1152]{1,0:T(8,128)(2,1)S(1)}, f16[192,1152]{1,0:T(8,128)(2,1)}, u32[]{:S(2)}, u32[]{:S(2)}) collective-permute-start(f16[192,1152]{1,0:T(8,128)(2,1)S(1)} %fusion.2), channel_id=1, source_target_pairs={{0,6},{2,0},{4,2},{6,4},{1,7},{3,1},{5,3},{7,5},{8,14},{10,8},{12,... | collective-permute-start | bytes 1327112 | tf_op jit(solution)/shard_map/ppermute | solution.py:56
  77.9 21.8 %collective-permute-start.2 = (f16[192,1152]{1,0:T(8,128)(2,1)S(1)}, f16[192,1152]{1,0:T(8,128)(2,1)}, u32[]{:S(2)}, u32[]{:S(2)}) collective-permute-start(f16[192,1152]{1,0:T(8,128)(2,1)S(1)} %fusion), channel_id=1, source_target_pairs={{0,2},{2,4},{4,6},{6,0},{1,3},{3,5},{5,7},{7,1},{8,10},{10,12},{12... | collective-permute-start | bytes 1327112 | tf_op jit(solution)/shard_map/ppermute | solution.py:56
  80.4 20.7 %collective-permute-start.1 = (f16[192,1152]{1,0:T(8,128)(2,1)S(1)}, f16[192,1152]{1,0:T(8,128)(2,1)}, u32[]{:S(2)}, u32[]{:S(2)}) collective-permute-start(f16[192,1152]{1,0:T(8,128)(2,1)S(1)} %fusion.1), channel_id=1, source_target_pairs={{0,4},{2,6},{4,0},{6,2},{1,5},{3,7},{5,1},{7,3},{8,12},{10,14},{12... | collective-permute-start | bytes 1327112 | tf_op jit(solution)/shard_map/ppermute | solution.py:56
  96.4 7.2 %all-to-all-start.3 = ((f32[4,1,128]{2,1,0:T(1,128)}), f32[4,1,128]{2,1,0:T(1,128)S(1)}, u32[]{:S(2)}, u32[]{:S(2)}) async-start(f32[4,1,128]{2,1,0:T(1,128)} %broadcast_in_dim.47), calls=%async_computation.3 | async-start | bytes 4096 | tf_op jit(solution)/shard_map/all_to_all | solution.py:51
  104.7 18.7 %all-to-all-start.4 = ((f16[8,24,1280]{2,1,0:T(8,128)(2,1)}), f16[8,24,1280]{2,1,0:T(8,128)(2,1)S(1)}, u32[]{:S(2)}, u32[]{:S(2)}) async-start(f16[8,24,1280]{2,1,0:T(8,128)(2,1)} %pad_maximum_fusion.2), calls=%async_computation.4 | async-start | bytes 983040 | tf_op jit(solution)/shard_map/all_to_all | solution.py:51

commit v11 on v10

--- a/solution.py
+++ b/solution.py
@@ -137,6 +137,28 @@
     )(place, rows, slopes, totals)
 
 
+def finish_kernel(last, scale, unit, radius, accum, sums, grad, loss, scale_grad, bias_grad):
+    values = unit[...]
+    total = accum[...] * (scale[0] * last[0])
+    grad[...] = (total - values * jnp.sum(values * total, -1, keepdims=True)) / radius[:, :1]
+    loss[0] = sums[0, 0] * last[1]
+    scale_grad[0] = sums[0, 1] * (scale[0] * last[1])
+    bias_grad[0] = sums[0, 2] * last[1]
+
+
+def finish(last, scale, unit, radius, accum, sums):
+    one = jax.ShapeDtypeStruct((1,), jnp.float32)
+    return pl.pallas_call(
+        functools.partial(finish_kernel, last),
+        in_specs=[SMEM, VMEM, VMEM, VMEM, VMEM],
+        out_specs=[VMEM, SMEM, SMEM, SMEM],
+        out_shape=[jax.ShapeDtypeStruct(unit.shape, jnp.float32), one, one, one],
+        compiler_params=pltpu.CompilerParams(vmem_limit_bytes=8 * 2**20),
+        cost_estimate=pl.CostEstimate(flops=10**6, bytes_accessed=10**6, transcendentals=0),
+        name="finish",
+    )(scale.reshape(1), unit, radius, accum, sums)
+
+
 def swap_sum(blocks, stats, axis):
     count, high, width = blocks.shape
     rider = jnp.concatenate(half_pieces(stats * (1 / 2048.0)) + [jnp.zeros((high - 3, 128), jnp.float16)], 0)
@@ -211,16 +233,10 @@
     drows = sum(part.astype(jnp.float32) for part in back.values())
     drows = (drows * 0.25).astype(jnp.float16).reshape(8, -1, width)
     drows, stats = swap_sum(drows, stats, "y")
-    stats = stats[0]
-
-    total_texts = txt_rows * 512
-    image_accum = drows * 0.0625
-    text_accum = dcols * (1 / 32.0)
-    image_grad = unnormalize(ux, rx[:, :1], scale * image_accum)
-    text_grad = unnormalize(uy, ry[:, :1], scale * text_accum)
-    lane = lax.iota(jnp.int32, stats.shape[0])
-    stats = stats * jnp.where(lane == 1, scale, 1.0) * (1.0 / total_texts)
-    loss, scale_grad, bias_grad = stats[0:1], stats[1:2], stats[2:3]
+    text_grad = unnormalize(uy, ry[:, :1], scale * (dcols * (1 / 32.0)))
+    image_grad, loss, scale_grad, bias_grad = finish(
+        (0.0625, 1.0 / (txt_rows * 512)), scale, ux, rx, drows, stats
+    )
     return (image_grad, text_grad, loss, scale_grad, bias_grad)
 
 

time: 126 us -> 125 us (level)
  no operation moved by 1% of the time
where the time goes in v11:
time: 125 us; the launch traced here: 124 us
  starting transfers between devices  37.5 us (30%)
  waiting for transfers between devices  37.2 us (30%)
  blocking collectives  27.4 us (22%)
  Pallas kernels  7.02 us (6%)
  local copies, waits for them, and re-layouts  5.9 us (5%)
  other arithmetic  3.92 us (3%)
  matrix products  3.15 us (3%)
  between operations  2.26 us (2%)
    all_to_all x5, waiting for transfers between devices, swap(): return lax.all_to_all(value, axis, 0, 0, tiled=False)  35.5 us
    all_gather x1, blocking collectives, body(): cols = lax.all_gather(cols, Z + ('core',), axis=0, tiled=True)  27.4 us
    all_to_all x5, starting transfers between devices, swap(): return lax.all_to_all(value, axis, 0, 0, tiled=False)  27.1 us
    ppermute x4, starting transfers between devices, shifted(): lax.ppermute(value, axis, [(i, (i + steps) % count) for i in range(count)])  10.4 us
    pallas_call x1, Pallas kernels, slopes_of(): pl.pallas_call(slopes_kernel, in_specs=[SMEM, SMEM, VMEM, VMEM, VMEM, VME...  3.48 us
    dot_general x4, matrix products, body(): jnp.dot(near[k * high:(k + 1) * high], cols, preferred_element_type=jnp.f...  3.15 us
  transfers between devices with their start and end apart: 9, of which 6 were waited for; matrix products, arithmetic and copies ran while one was open for 6% of the time, Pallas kernels for 1%

profile of v11, /device:TPU:1, one launch (start us, length us, event | category | flops | bytes accessed | tf_op | source)
XLA Modules:
  0.0 124.4 jit_solution(12747758246970089946)
XLA Ops:
  1.4 0.9 normalize_8.1
  2.4 7.7 %all-to-all-start = ((bf16[8,24,1152]{2,1,0:T(8,128)(2,1)}), bf16[8,24,1152]{2,1,0:T(8,128)(2,1)S(1)}, u32[]{:S(2)}, u32[]{:S(2)}) async-start(bf16[8,24,1152]{2,1,0:T(8,128)(2,1)} %get-tuple-element.25), calls=%async_computation | async-start | bytes 884736 | tf_op jit(solution)/shard_map/all_to_all | solution.py:51
  11.4 0.9 copy-done.1
  12.4 1.2 reshape.182
  14.5 8.2 %all-to-all-done = bf16[8,24,1152]{2,1,0:T(8,128)(2,1)S(1)} async-done(((bf16[8,24,1152]{2,1,0:T(8,128)(2,1)}), bf16[8,24,1152]{2,1,0:T(8,128)(2,1)S(1)}, u32[]{:S(2)}, u32[]{:S(2)}) %all-to-all-start) | async-done | bytes 442400 | tf_op jit(solution)/shard_map/all_to_all | solution.py:51
  22.7 1.4 %broadcast_in_dim.14 = bf16[4,192,1152]{2,1,0:T(8,128)(2,1)} broadcast(bf16[192,1152]{1,0:T(8,128)(2,1)S(1)} %bitcast.48), dimensions={1,2} | broadcast | bytes 2211840 | tf_op jit(solution)/shard_map/broadcast_in_dim | solution.py:61
  24.1 7.1 %all-to-all-start.1 = ((bf16[4,192,1152]{2,1,0:T(8,128)(2,1)}), bf16[4,192,1152]{2,1,0:T(8,128)(2,1)S(1)}, u32[]{:S(2)}, u32[]{:S(2)}) async-start(bf16[4,192,1152]{2,1,0:T(8,128)(2,1)} %broadcast_in_dim.14), calls=%async_computation.1 | async-start | bytes 3538944 | tf_op jit(solution)/shard_map/all_to_all | solution.py:51
  31.2 27.4 %all-gather.1 = f16[512,1152]{1,0:T(8,128)(2,1)S(1)} all-gather(f16[32,1152]{1,0:T(8,128)(2,1)S(1)} %fusion.9), channel_id=1, replica_groups=mesh['y'=8,'zh'=2,'zl'=4,'x'=4,'core'=2] {'zh','zl','core'}, dimensions={0}, use_global_device_ids=true | all-gather | bytes 1253376 | tf_op jit(solution)/shard_map/all_gather | solution.py:194
  59.0 3.5 %slopes.1 = (bf16[768,512]{1,0:T(8,128)(2,1)S(1)}, f32[8,1152]{1,0:T(8,128)S(1)}) custom-call(s32[1]{0:T(128)} %bitcast.place, f32[2]{0:T(128)S(1)} %pad_maximum_fusion.3.scalars, bf16[768,1152]{1,0:T(8,128)(2,1)S(1)} %bitcast.43, bf16[512,1152]{1,0:T(8,128)(2,1)S(1)} %bitcast.38, bf16[4,8,192]{2,1,0:T(8,128)(2,1)S(1)} %maximum_maximum_fusion.row_ids, ...), custom_call_target="tpu_custom_call" | custom-call | flops 1000000000 | bytes 4000000 | tf_op jit(solution)/shard_map/slopes/pallas_call | solution.py:113
  62.5 0.9 text_products_1.1
  63.4 2.1 %collective-permute-start = (f32[264,1152]{1,0:T(8,128)S(1)}, f32[264,1152]{1,0:T(8,128)S(1)}, u32[]{:S(2)}, u32[]{:S(2)}) collective-permute-start(f32[264,1152]{1,0:T(8,128)S(1)} %text_products_1.1), channel_id=1, source_target_pairs={{0,1},{1,0},{2,3},{3,2},{4,5},{5,4},{6,7},{7,6},{8,9},{9,8},{10,11... | collective-permute-start | bytes 3649544 | tf_op jit(solution)/shard_map/ppermute | solution.py:56
  65.5 0.9 text_products_0.1
  68.5 1.0 pad_maximum_fusion.1
  69.5 5.6 %all-to-all-start.2 = ((f16[8,32,1280]{2,1,0:T(8,128)(2,1)}), f16[8,32,1280]{2,1,0:T(8,128)(2,1)S(1)}, u32[]{:S(2)}, u32[]{:S(2)}) async-start(f16[8,32,1280]{2,1,0:T(8,128)(2,1)} %pad_maximum_fusion.1), calls=%async_computation.2 | async-start | bytes 1310720 | tf_op jit(solution)/shard_map/all_to_all | solution.py:51
  75.1 2.8 %collective-permute-start.3 = (f16[192,1152]{1,0:T(8,128)(2,1)S(1)}, f16[192,1152]{1,0:T(8,128)(2,1)}, u32[]{:S(2)}, u32[]{:S(2)}) collective-permute-start(f16[192,1152]{1,0:T(8,128)(2,1)S(1)} %fusion.2), channel_id=1, source_target_pairs={{0,6},{2,0},{4,2},{6,4},{1,7},{3,1},{5,3},{7,5},{8,14},{10,8},{12,... | collective-permute-start | bytes 1327112 | tf_op jit(solution)/shard_map/ppermute | solution.py:56
  77.9 2.5 %collective-permute-start.2 = (f16[192,1152]{1,0:T(8,128)(2,1)S(1)}, f16[192,1152]{1,0:T(8,128)(2,1)}, u32[]{:S(2)}, u32[]{:S(2)}) collective-permute-start(f16[192,1152]{1,0:T(8,128)(2,1)S(1)} %fusion), channel_id=1, source_target_pairs={{0,2},{2,4},{4,6},{6,0},{1,3},{3,5},{5,7},{7,1},{8,10},{10,12},{12... | collective-permute-start | bytes 1327112 | tf_op jit(solution)/shard_map/ppermute | solution.py:56
  80.4 3.1 %collective-permute-start.1 = (f16[192,1152]{1,0:T(8,128)(2,1)S(1)}, f16[192,1152]{1,0:T(8,128)(2,1)}, u32[]{:S(2)}, u32[]{:S(2)}) collective-permute-start(f16[192,1152]{1,0:T(8,128)(2,1)S(1)} %fusion.1), channel_id=1, source_target_pairs={{0,4},{2,6},{4,0},{6,2},{1,5},{3,7},{5,1},{7,3},{8,12},{10,14},{12... | collective-permute-start | bytes 1327112 | tf_op jit(solution)/shard_map/ppermute | solution.py:56
  83.6 12.3 %all-to-all-done.2 = f16[8,32,1280]{2,1,0:T(8,128)(2,1)S(1)} async-done(((f16[8,32,1280]{2,1,0:T(8,128)(2,1)}), f16[8,32,1280]{2,1,0:T(8,128)(2,1)S(1)}, u32[]{:S(2)}, u32[]{:S(2)}) %all-to-all-start.2) | async-done | bytes 655392 | tf_op jit(solution)/shard_map/all_to_all | solution.py:51
  96.5 3.2 %all-to-all-start.3 = ((f32[4,1,128]{2,1,0:T(1,128)}), f32[4,1,128]{2,1,0:T(1,128)S(1)}, u32[]{:S(2)}, u32[]{:S(2)}) async-start(f32[4,1,128]{2,1,0:T(1,128)} %broadcast_in_dim.18), calls=%async_computation.3 | async-start | bytes 4096 | tf_op jit(solution)/shard_map/all_to_all | solution.py:51
  99.7 1.3 %collective-permute-done.1 = f16[192,1152]{1,0:T(8,128)(2,1)} collective-permute-done((f16[192,1152]{1,0:T(8,128)(2,1)S(1)}, f16[192,1152]{1,0:T(8,128)(2,1)}, u32[]{:S(2)}, u32[]{:S(2)}) %collective-permute-start.1) | collective-permute-done | bytes 442400 | tf_op jit(solution)/shard_map/ppermute | solution.py:56
  101.0 1.9 %multiply_convert_fusion.1 = f16[192,1152]{1,0:T(8,128)(2,1)S(1)} fusion(f16[192,1152]{1,0:T(8,128)(2,1)} %collective-permute-done.3, f16[192,1152]{1,0:T(8,128)(2,1)} %collective-permute-done.2, f16[192,1152]{1,0:T(8,128)(2,1)} %collective-permute-done.1, bf16[512,1152]{1,0:T(8,128)(2,1)S(1)} %bitcast.42, bf16[768,512]{1,0:T(8,128)(2,1)} %copy-done), kind=kOutput, calls=%fused_computation.14 | convolution fusion | flops 228483072 | bytes 3145728 | tf_op jit(solution)/shard_map/dot_general | solution.py:221
  103.9 0.9 pad_maximum_fusion.2
  104.8 3.5 %all-to-all-start.4 = ((f16[8,24,1280]{2,1,0:T(8,128)(2,1)}), f16[8,24,1280]{2,1,0:T(8,128)(2,1)S(1)}, u32[]{:S(2)}, u32[]{:S(2)}) async-start(f16[8,24,1280]{2,1,0:T(8,128)(2,1)} %pad_maximum_fusion.2), calls=%async_computation.4 | async-start | bytes 983040 | tf_op jit(solution)/shard_map/all_to_all | solution.py:51
  109.3 14.2 %all-to-all-done.4 = f16[8,24,1280]{2,1,0:T(8,128)(2,1)S(1)} async-done(((f16[8,24,1280]{2,1,0:T(8,128)(2,1)}), f16[8,24,1280]{2,1,0:T(8,128)(2,1)S(1)}, u32[]{:S(2)}, u32[]{:S(2)}) %all-to-all-start.4) | async-done | bytes 491552 | tf_op jit(solution)/shard_map/all_to_all | solution.py:51
  (56 shorter events, 7.9 us)
Async XLA Ops:
  0.6 0.8 copy-start.2
  1.4 12.4 %copy-start.3 = (s32[16384]{0:T(1024)S(1)}, s32[16384]{0:T(1024)}, u32[]{:S(2)}) copy-start(s32[16384]{0:T(1024)} %param.9) | copy-start | bytes 196612
  2.4 20.4 %all-to-all-start = ((bf16[8,24,1152]{2,1,0:T(8,128)(2,1)}), bf16[8,24,1152]{2,1,0:T(8,128)(2,1)S(1)}, u32[]{:S(2)}, u32[]{:S(2)}) async-start(bf16[8,24,1152]{2,1,0:T(8,128)(2,1)} %get-tuple-element.25), calls=%async_computation | async-start | bytes 884736 | tf_op jit(solution)/shard_map/all_to_all | solution.py:51
  11.3 0.9 copy-start.1
  24.1 35.0 %all-to-all-start.1 = ((bf16[4,192,1152]{2,1,0:T(8,128)(2,1)}), bf16[4,192,1152]{2,1,0:T(8,128)(2,1)S(1)}, u32[]{:S(2)}, u32[]{:S(2)}) async-start(bf16[4,192,1152]{2,1,0:T(8,128)(2,1)} %broadcast_in_dim.14), calls=%async_computation.1 | async-start | bytes 3538944 | tf_op jit(solution)/shard_map/all_to_all | solution.py:51
  62.5 4.8 %copy-start = (bf16[768,512]{1,0:T(8,128)(2,1)}, bf16[768,512]{1,0:T(8,128)(2,1)S(1)}, u32[]{:S(2)}) copy-start(bf16[768,512]{1,0:T(8,128)(2,1)S(1)} %get-tuple-element.29.slopes) | copy-start | bytes 2359300
  63.4 4.8 %collective-permute-start = (f32[264,1152]{1,0:T(8,128)S(1)}, f32[264,1152]{1,0:T(8,128)S(1)}, u32[]{:S(2)}, u32[]{:S(2)}) collective-permute-start(f32[264,1152]{1,0:T(8,128)S(1)} %text_products_1.1), channel_id=1, source_target_pairs={{0,1},{1,0},{2,3},{3,2},{4,5},{5,4},{6,7},{7,6},{8,9},{9,8},{10,11... | collective-permute-start | bytes 3649544 | tf_op jit(solution)/shard_map/ppermute | solution.py:56
  69.5 26.4 %all-to-all-start.2 = ((f16[8,32,1280]{2,1,0:T(8,128)(2,1)}), f16[8,32,1280]{2,1,0:T(8,128)(2,1)S(1)}, u32[]{:S(2)}, u32[]{:S(2)}) async-start(f16[8,32,1280]{2,1,0:T(8,128)(2,1)} %pad_maximum_fusion.1), calls=%async_computation.2 | async-start | bytes 1310720 | tf_op jit(solution)/shard_map/all_to_all | solution.py:51
  75.1 24.6 %collective-permute-start.3 = (f16[192,1152]{1,0:T(8,128)(2,1)S(1)}, f16[192,1152]{1,0:T(8,128)(2,1)}, u32[]{:S(2)}, u32[]{:S(2)}) collective-permute-start(f16[192,1152]{1,0:T(8,128)(2,1)S(1)} %fusion.2), channel_id=1, source_target_pairs={{0,6},{2,0},{4,2},{6,4},{1,7},{3,1},{5,3},{7,5},{8,14},{10,8},{12,... | collective-permute-start | bytes 1327112 | tf_op jit(solution)/shard_map/ppermute | solution.py:56
  77.9 21.8 %collective-permute-start.2 = (f16[192,1152]{1,0:T(8,128)(2,1)S(1)}, f16[192,1152]{1,0:T(8,128)(2,1)}, u32[]{:S(2)}, u32[]{:S(2)}) collective-permute-start(f16[192,1152]{1,0:T(8,128)(2,1)S(1)} %fusion), channel_id=1, source_target_pairs={{0,2},{2,4},{4,6},{6,0},{1,3},{3,5},{5,7},{7,1},{8,10},{10,12},{12... | collective-permute-start | bytes 1327112 | tf_op jit(solution)/shard_map/ppermute | solution.py:56
  80.4 20.7 %collective-permute-start.1 = (f16[192,1152]{1,0:T(8,128)(2,1)S(1)}, f16[192,1152]{1,0:T(8,128)(2,1)}, u32[]{:S(2)}, u32[]{:S(2)}) collective-permute-start(f16[192,1152]{1,0:T(8,128)(2,1)S(1)} %fusion.1), channel_id=1, source_target_pairs={{0,4},{2,6},{4,0},{6,2},{1,5},{3,7},{5,1},{7,3},{8,12},{10,14},{12... | collective-permute-start | bytes 1327112 | tf_op jit(solution)/shard_map/ppermute | solution.py:56
  96.5 7.2 %all-to-all-start.3 = ((f32[4,1,128]{2,1,0:T(1,128)}), f32[4,1,128]{2,1,0:T(1,128)S(1)}, u32[]{:S(2)}, u32[]{:S(2)}) async-start(f32[4,1,128]{2,1,0:T(1,128)} %broadcast_in_dim.18), calls=%async_computation.3 | async-start | bytes 4096 | tf_op jit(solution)/shard_map/all_to_all | solution.py:51
  104.8 18.7 %all-to-all-start.4 = ((f16[8,24,1280]{2,1,0:T(8,128)(2,1)}), f16[8,24,1280]{2,1,0:T(8,128)(2,1)S(1)}, u32[]{:S(2)}, u32[]{:S(2)}) async-start(f16[8,24,1280]{2,1,0:T(8,128)(2,1)} %pad_maximum_fusion.2), calls=%async_computation.4 | async-start | bytes 983040 | tf_op jit(solution)/shard_map/all_to_all | solution.py:51

commit v12 on v11

--- a/solution.py
+++ b/solution.py
@@ -159,12 +159,12 @@
     )(scale.reshape(1), unit, radius, accum, sums)
 
 
-def swap_sum(blocks, stats, axis):
+def swap_sum(blocks, stats, axis, unit):
     count, high, width = blocks.shape
-    rider = jnp.concatenate(half_pieces(stats * (1 / 2048.0)) + [jnp.zeros((high - 3, 128), jnp.float16)], 0)
+    rider = jnp.concatenate(half_pieces(stats * (1 / unit)) + [jnp.zeros((high - 3, 128), jnp.float16)], 0)
     rider = jnp.broadcast_to(rider[None], (count, high, 128))
     got = swap(jnp.concatenate([blocks, rider], 2), axis)
-    stats = jnp.sum(got[:, :3, width:].astype(jnp.float32), (0, 1)).reshape(1, 128) * 2048.0
+    stats = jnp.sum(got[:, :3, width:].astype(jnp.float32), (0, 1)).reshape(1, 128) * unit
     return (jnp.sum(got[:, :, :width].astype(jnp.float32), 0), stats)
 
 
@@ -225,14 +225,14 @@
     mine = text_products(0, place, rows, near, totals)
     dcols = ((got[:half] + mine) * 32.0).astype(jnp.float16).reshape(8, txt_rows, width)
     dcols, back[1], back[2], back[3] = lax.optimization_barrier((dcols, back[1], back[2], back[3]))
-    dcols, stats = swap_sum(dcols, got[half : half + 1, :128] + totals[:1, :128], Z)
+    dcols, stats = swap_sum(dcols, got[half : half + 1, :128] + totals[:1, :128], Z, 128.0)
     stats = jnp.sum(spread(stats, "x"), 0)
 
     for k in (2, 1, 3):
         back[k] = shifted(back[k], "x", k)
     drows = sum(part.astype(jnp.float32) for part in back.values())
     drows = (drows * 0.25).astype(jnp.float16).reshape(8, -1, width)
-    drows, stats = swap_sum(drows, stats, "y")
+    drows, stats = swap_sum(drows, stats, "y", 4096.0)
     text_grad = unnormalize(uy, ry[:, :1], scale * (dcols * (1 / 32.0)))
     image_grad, loss, scale_grad, bias_grad = finish(
         (0.0625, 1.0 / (txt_rows * 512)), scale, ux, rx, drows, stats

time: 125 us -> 125 us (level)
  no operation moved by 1% of the time
where the time goes in v12:
time: 125 us; the launch traced here: 124 us
  starting transfers between devices  37.5 us (30%)
  waiting for transfers between devices  37.2 us (30%)
  blocking collectives  27.4 us (22%)
  Pallas kernels  7.02 us (6%)
  local copies, waits for them, and re-layouts  5.9 us (5%)
  other arithmetic  3.92 us (3%)
  matrix products  3.15 us (3%)
  between operations  2.26 us (2%)
    all_to_all x5, waiting for transfers between devices, swap(): return lax.all_to_all(value, axis, 0, 0, tiled=False)  35.5 us
    all_gather x1, blocking collectives, body(): cols = lax.all_gather(cols, Z + ('core',), axis=0, tiled=True)  27.4 us
    all_to_all x5, starting transfers between devices, swap(): return lax.all_to_all(value, axis, 0, 0, tiled=False)  27.1 us
    ppermute x4, starting transfers between devices, shifted(): lax.ppermute(value, axis, [(i, (i + steps) % count) for i in range(count)])  10.4 us
    pallas_call x1, Pallas kernels, slopes_of(): pl.pallas_call(slopes_kernel, in_specs=[SMEM, SMEM, VMEM, VMEM, VMEM, VME...  3.48 us
    dot_general x4, matrix products, body(): jnp.dot(near[k * high:(k + 1) * high], cols, preferred_element_type=jnp.f...  3.15 us
  transfers between devices with their start and end apart: 9, of which 6 were waited for; matrix products, arithmetic and copies ran while one was open for 6% of the time, Pallas kernels for 1%

profile of v12, /device:TPU:1, one launch (start us, length us, event | category | flops | bytes accessed | tf_op | source)
XLA Modules:
  0.0 124.4 jit_solution(3467481037463452802)
XLA Ops:
  1.4 0.9 normalize_8.1
  2.4 7.7 %all-to-all-start = ((bf16[8,24,1152]{2,1,0:T(8,128)(2,1)}), bf16[8,24,1152]{2,1,0:T(8,128)(2,1)S(1)}, u32[]{:S(2)}, u32[]{:S(2)}) async-start(bf16[8,24,1152]{2,1,0:T(8,128)(2,1)} %get-tuple-element.25), calls=%async_computation | async-start | bytes 884736 | tf_op jit(solution)/shard_map/all_to_all | solution.py:51
  11.4 0.9 copy-done.1
  12.4 1.2 reshape.182
  14.5 8.2 %all-to-all-done = bf16[8,24,1152]{2,1,0:T(8,128)(2,1)S(1)} async-done(((bf16[8,24,1152]{2,1,0:T(8,128)(2,1)}), bf16[8,24,1152]{2,1,0:T(8,128)(2,1)S(1)}, u32[]{:S(2)}, u32[]{:S(2)}) %all-to-all-start) | async-done | bytes 442400 | tf_op jit(solution)/shard_map/all_to_all | solution.py:51
  22.7 1.4 %broadcast_in_dim.14 = bf16[4,192,1152]{2,1,0:T(8,128)(2,1)} broadcast(bf16[192,1152]{1,0:T(8,128)(2,1)S(1)} %bitcast.48), dimensions={1,2} | broadcast | bytes 2211840 | tf_op jit(solution)/shard_map/broadcast_in_dim | solution.py:61
  24.1 7.1 %all-to-all-start.1 = ((bf16[4,192,1152]{2,1,0:T(8,128)(2,1)}), bf16[4,192,1152]{2,1,0:T(8,128)(2,1)S(1)}, u32[]{:S(2)}, u32[]{:S(2)}) async-start(bf16[4,192,1152]{2,1,0:T(8,128)(2,1)} %broadcast_in_dim.14), calls=%async_computation.1 | async-start | bytes 3538944 | tf_op jit(solution)/shard_map/all_to_all | solution.py:51
  31.2 27.4 %all-gather.1 = f16[512,1152]{1,0:T(8,128)(2,1)S(1)} all-gather(f16[32,1152]{1,0:T(8,128)(2,1)S(1)} %fusion.9), channel_id=1, replica_groups=mesh['y'=8,'zh'=2,'zl'=4,'x'=4,'core'=2] {'zh','zl','core'}, dimensions={0}, use_global_device_ids=true | all-gather | bytes 1253376 | tf_op jit(solution)/shard_map/all_gather | solution.py:194
  59.0 3.5 %slopes.1 = (bf16[768,512]{1,0:T(8,128)(2,1)S(1)}, f32[8,1152]{1,0:T(8,128)S(1)}) custom-call(s32[1]{0:T(128)} %bitcast.place, f32[2]{0:T(128)S(1)} %pad_maximum_fusion.3.scalars, bf16[768,1152]{1,0:T(8,128)(2,1)S(1)} %bitcast.43, bf16[512,1152]{1,0:T(8,128)(2,1)S(1)} %bitcast.38, bf16[4,8,192]{2,1,0:T(8,128)(2,1)S(1)} %maximum_maximum_fusion.row_ids, ...), custom_call_target="tpu_custom_call" | custom-call | flops 1000000000 | bytes 4000000 | tf_op jit(solution)/shard_map/slopes/pallas_call | solution.py:113
  62.5 0.9 text_products_1.1
  63.4 2.1 %collective-permute-start = (f32[264,1152]{1,0:T(8,128)S(1)}, f32[264,1152]{1,0:T(8,128)S(1)}, u32[]{:S(2)}, u32[]{:S(2)}) collective-permute-start(f32[264,1152]{1,0:T(8,128)S(1)} %text_products_1.1), channel_id=1, source_target_pairs={{0,1},{1,0},{2,3},{3,2},{4,5},{5,4},{6,7},{7,6},{8,9},{9,8},{10,11... | collective-permute-start | bytes 3649544 | tf_op jit(solution)/shard_map/ppermute | solution.py:56
  65.5 0.9 text_products_0.1
  68.5 1.0 pad_maximum_fusion.1
  69.5 5.6 %all-to-all-start.2 = ((f16[8,32,1280]{2,1,0:T(8,128)(2,1)}), f16[8,32,1280]{2,1,0:T(8,128)(2,1)S(1)}, u32[]{:S(2)}, u32[]{:S(2)}) async-start(f16[8,32,1280]{2,1,0:T(8,128)(2,1)} %pad_maximum_fusion.1), calls=%async_computation.2 | async-start | bytes 1310720 | tf_op jit(solution)/shard_map/all_to_all | solution.py:51
  75.1 2.8 %collective-permute-start.3 = (f16[192,1152]{1,0:T(8,128)(2,1)S(1)}, f16[192,1152]{1,0:T(8,128)(2,1)}, u32[]{:S(2)}, u32[]{:S(2)}) collective-permute-start(f16[192,1152]{1,0:T(8,128)(2,1)S(1)} %fusion.2), channel_id=1, source_target_pairs={{0,6},{2,0},{4,2},{6,4},{1,7},{3,1},{5,3},{7,5},{8,14},{10,8},{12,... | collective-permute-start | bytes 1327112 | tf_op jit(solution)/shard_map/ppermute | solution.py:56
  77.9 2.5 %collective-permute-start.2 = (f16[192,1152]{1,0:T(8,128)(2,1)S(1)}, f16[192,1152]{1,0:T(8,128)(2,1)}, u32[]{:S(2)}, u32[]{:S(2)}) collective-permute-start(f16[192,1152]{1,0:T(8,128)(2,1)S(1)} %fusion), channel_id=1, source_target_pairs={{0,2},{2,4},{4,6},{6,0},{1,3},{3,5},{5,7},{7,1},{8,10},{10,12},{12... | collective-permute-start | bytes 1327112 | tf_op jit(solution)/shard_map/ppermute | solution.py:56
  80.4 3.1 %collective-permute-start.1 = (f16[192,1152]{1,0:T(8,128)(2,1)S(1)}, f16[192,1152]{1,0:T(8,128)(2,1)}, u32[]{:S(2)}, u32[]{:S(2)}) collective-permute-start(f16[192,1152]{1,0:T(8,128)(2,1)S(1)} %fusion.1), channel_id=1, source_target_pairs={{0,4},{2,6},{4,0},{6,2},{1,5},{3,7},{5,1},{7,3},{8,12},{10,14},{12... | collective-permute-start | bytes 1327112 | tf_op jit(solution)/shard_map/ppermute | solution.py:56
  83.6 12.3 %all-to-all-done.2 = f16[8,32,1280]{2,1,0:T(8,128)(2,1)S(1)} async-done(((f16[8,32,1280]{2,1,0:T(8,128)(2,1)}), f16[8,32,1280]{2,1,0:T(8,128)(2,1)S(1)}, u32[]{:S(2)}, u32[]{:S(2)}) %all-to-all-start.2) | async-done | bytes 655392 | tf_op jit(solution)/shard_map/all_to_all | solution.py:51
  96.5 3.2 %all-to-all-start.3 = ((f32[4,1,128]{2,1,0:T(1,128)}), f32[4,1,128]{2,1,0:T(1,128)S(1)}, u32[]{:S(2)}, u32[]{:S(2)}) async-start(f32[4,1,128]{2,1,0:T(1,128)} %broadcast_in_dim.18), calls=%async_computation.3 | async-start | bytes 4096 | tf_op jit(solution)/shard_map/all_to_all | solution.py:51
  99.7 1.3 %collective-permute-done.1 = f16[192,1152]{1,0:T(8,128)(2,1)} collective-permute-done((f16[192,1152]{1,0:T(8,128)(2,1)S(1)}, f16[192,1152]{1,0:T(8,128)(2,1)}, u32[]{:S(2)}, u32[]{:S(2)}) %collective-permute-start.1) | collective-permute-done | bytes 442400 | tf_op jit(solution)/shard_map/ppermute | solution.py:56
  101.0 1.9 %multiply_convert_fusion.1 = f16[192,1152]{1,0:T(8,128)(2,1)S(1)} fusion(f16[192,1152]{1,0:T(8,128)(2,1)} %collective-permute-done.3, f16[192,1152]{1,0:T(8,128)(2,1)} %collective-permute-done.2, f16[192,1152]{1,0:T(8,128)(2,1)} %collective-permute-done.1, bf16[512,1152]{1,0:T(8,128)(2,1)S(1)} %bitcast.42, bf16[768,512]{1,0:T(8,128)(2,1)} %copy-done), kind=kOutput, calls=%fused_computation.14 | convolution fusion | flops 228483072 | bytes 3145728 | tf_op jit(solution)/shard_map/dot_general | solution.py:221
  103.9 0.9 pad_maximum_fusion.2
  104.8 3.5 %all-to-all-start.4 = ((f16[8,24,1280]{2,1,0:T(8,128)(2,1)}), f16[8,24,1280]{2,1,0:T(8,128)(2,1)S(1)}, u32[]{:S(2)}, u32[]{:S(2)}) async-start(f16[8,24,1280]{2,1,0:T(8,128)(2,1)} %pad_maximum_fusion.2), calls=%async_computation.4 | async-start | bytes 983040 | tf_op jit(solution)/shard_map/all_to_all | solution.py:51
  109.3 14.2 %all-to-all-done.4 = f16[8,24,1280]{2,1,0:T(8,128)(2,1)S(1)} async-done(((f16[8,24,1280]{2,1,0:T(8,128)(2,1)}), f16[8,24,1280]{2,1,0:T(8,128)(2,1)S(1)}, u32[]{:S(2)}, u32[]{:S(2)}) %all-to-all-start.4) | async-done | bytes 491552 | tf_op jit(solution)/shard_map/all_to_all | solution.py:51
  (56 shorter events, 7.9 us)
Async XLA Ops:
  0.6 0.8 copy-start.2
  1.4 12.4 %copy-start.3 = (s32[16384]{0:T(1024)S(1)}, s32[16384]{0:T(1024)}, u32[]{:S(2)}) copy-start(s32[16384]{0:T(1024)} %param.9) | copy-start | bytes 196612
  2.4 20.4 %all-to-all-start = ((bf16[8,24,1152]{2,1,0:T(8,128)(2,1)}), bf16[8,24,1152]{2,1,0:T(8,128)(2,1)S(1)}, u32[]{:S(2)}, u32[]{:S(2)}) async-start(bf16[8,24,1152]{2,1,0:T(8,128)(2,1)} %get-tuple-element.25), calls=%async_computation | async-start | bytes 884736 | tf_op jit(solution)/shard_map/all_to_all | solution.py:51
  11.3 0.9 copy-start.1
  24.1 35.0 %all-to-all-start.1 = ((bf16[4,192,1152]{2,1,0:T(8,128)(2,1)}), bf16[4,192,1152]{2,1,0:T(8,128)(2,1)S(1)}, u32[]{:S(2)}, u32[]{:S(2)}) async-start(bf16[4,192,1152]{2,1,0:T(8,128)(2,1)} %broadcast_in_dim.14), calls=%async_computation.1 | async-start | bytes 3538944 | tf_op jit(solution)/shard_map/all_to_all | solution.py:51
  62.5 4.8 %copy-start = (bf16[768,512]{1,0:T(8,128)(2,1)}, bf16[768,512]{1,0:T(8,128)(2,1)S(1)}, u32[]{:S(2)}) copy-start(bf16[768,512]{1,0:T(8,128)(2,1)S(1)} %get-tuple-element.29.slopes) | copy-start | bytes 2359300
  63.4 4.8 %collective-permute-start = (f32[264,1152]{1,0:T(8,128)S(1)}, f32[264,1152]{1,0:T(8,128)S(1)}, u32[]{:S(2)}, u32[]{:S(2)}) collective-permute-start(f32[264,1152]{1,0:T(8,128)S(1)} %text_products_1.1), channel_id=1, source_target_pairs={{0,1},{1,0},{2,3},{3,2},{4,5},{5,4},{6,7},{7,6},{8,9},{9,8},{10,11... | collective-permute-start | bytes 3649544 | tf_op jit(solution)/shard_map/ppermute | solution.py:56
  69.5 26.4 %all-to-all-start.2 = ((f16[8,32,1280]{2,1,0:T(8,128)(2,1)}), f16[8,32,1280]{2,1,0:T(8,128)(2,1)S(1)}, u32[]{:S(2)}, u32[]{:S(2)}) async-start(f16[8,32,1280]{2,1,0:T(8,128)(2,1)} %pad_maximum_fusion.1), calls=%async_computation.2 | async-start | bytes 1310720 | tf_op jit(solution)/shard_map/all_to_all | solution.py:51
  75.1 24.6 %collective-permute-start.3 = (f16[192,1152]{1,0:T(8,128)(2,1)S(1)}, f16[192,1152]{1,0:T(8,128)(2,1)}, u32[]{:S(2)}, u32[]{:S(2)}) collective-permute-start(f16[192,1152]{1,0:T(8,128)(2,1)S(1)} %fusion.2), channel_id=1, source_target_pairs={{0,6},{2,0},{4,2},{6,4},{1,7},{3,1},{5,3},{7,5},{8,14},{10,8},{12,... | collective-permute-start | bytes 1327112 | tf_op jit(solution)/shard_map/ppermute | solution.py:56
  77.9 21.8 %collective-permute-start.2 = (f16[192,1152]{1,0:T(8,128)(2,1)S(1)}, f16[192,1152]{1,0:T(8,128)(2,1)}, u32[]{:S(2)}, u32[]{:S(2)}) collective-permute-start(f16[192,1152]{1,0:T(8,128)(2,1)S(1)} %fusion), channel_id=1, source_target_pairs={{0,2},{2,4},{4,6},{6,0},{1,3},{3,5},{5,7},{7,1},{8,10},{10,12},{12... | collective-permute-start | bytes 1327112 | tf_op jit(solution)/shard_map/ppermute | solution.py:56
  80.4 20.7 %collective-permute-start.1 = (f16[192,1152]{1,0:T(8,128)(2,1)S(1)}, f16[192,1152]{1,0:T(8,128)(2,1)}, u32[]{:S(2)}, u32[]{:S(2)}) collective-permute-start(f16[192,1152]{1,0:T(8,128)(2,1)S(1)} %fusion.1), channel_id=1, source_target_pairs={{0,4},{2,6},{4,0},{6,2},{1,5},{3,7},{5,1},{7,3},{8,12},{10,14},{12... | collective-permute-start | bytes 1327112 | tf_op jit(solution)/shard_map/ppermute | solution.py:56
  96.5 7.2 %all-to-all-start.3 = ((f32[4,1,128]{2,1,0:T(1,128)}), f32[4,1,128]{2,1,0:T(1,128)S(1)}, u32[]{:S(2)}, u32[]{:S(2)}) async-start(f32[4,1,128]{2,1,0:T(1,128)} %broadcast_in_dim.18), calls=%async_computation.3 | async-start | bytes 4096 | tf_op jit(solution)/shard_map/all_to_all | solution.py:51
  104.8 18.7 %all-to-all-start.4 = ((f16[8,24,1280]{2,1,0:T(8,128)(2,1)}), f16[8,24,1280]{2,1,0:T(8,128)(2,1)S(1)}, u32[]{:S(2)}, u32[]{:S(2)}) async-start(f16[8,24,1280]{2,1,0:T(8,128)(2,1)} %pad_maximum_fusion.2), calls=%async_computation.4 | async-start | bytes 983040 | tf_op jit(solution)/shard_map/all_to_all | solution.py:51

commit v13 on v12

--- a/solution.py
+++ b/solution.py
@@ -61,10 +61,10 @@
     return swap(jnp.broadcast_to(block[None], (count,) + block.shape), axis)
 
 
-def slopes_kernel(place, scalars, rows, cols, row_ids, col_ids, slopes, totals):
+def slopes_kernel(place, scalars, rows, cols, row_ids, col_ids, slopes, in_order, totals):
     parts = 4
     high = rows.shape[0] // parts
-    sums = [0.0, 0.0, 0.0]
+    sums = [0.0, 0.0, 0.0, 0.0]
     ones = jnp.ones((row_ids.shape[1], cols.shape[0]), jnp.bfloat16)
     for k in range(parts):
         part = pl.ds(pl.multiple_of(lax.rem(place[0] + k, parts) * high, high), high)
@@ -78,12 +78,20 @@
         match = spot == col_ids[...]
         against = jnp.where(match, -logits, logits)
         decay = jnp.exp(-jnp.abs(against))
-        objective = jnp.maximum(against, 0.0) + jnp.log1p(decay)
-        weight = jnp.where(against >= 0.0, 1.0, decay) / (1.0 + decay)
+        above = 1.0 + decay
+        below = 1.0 / above
+        weight = jnp.where(against >= 0.0, below, decay * below)
+        objective = jnp.maximum(against, 0.0) + (decay - (above - 1.0)) * below
+        product = above[:8]
+        for i in range(1, high // 8):
+            product = product * above[8 * i : 8 * (i + 1)]
+        sums[3] += jnp.sum(jnp.log(product), 0, keepdims=True)
         slope = jnp.where(match, -weight, weight)
         slopes[k * high : (k + 1) * high, :] = slope.astype(jnp.bfloat16)
+        in_order[part, :] = slope.astype(jnp.bfloat16)
         for i, term in enumerate((objective, slope * dots, slope)):
             sums[i] += jnp.sum(term, 0, keepdims=True)
+    sums[0] += sums.pop()
     lane = lax.broadcasted_iota(jnp.int32, totals.shape, 1)
     total = jnp.zeros(totals.shape, jnp.float32)
     for i in range(3):
@@ -92,18 +100,13 @@
 
 
 def text_kernel(side, place, rows, slopes, totals, out):
-    parts = 4
-    high = rows.shape[0] // parts
     half = slopes.shape[1] // 2
-    for k in range(parts):
-        part = pl.ds(pl.multiple_of(lax.rem(place[0] + k, parts) * high, high), high)
-        product = lax.dot_general(
-            slopes[k * high : (k + 1) * high, side * half : (side + 1) * half],
-            rows[part, :],
-            (((0,), (0,)), ((), ())),
-            preferred_element_type=jnp.float32,
-        )
-        out[:half, :] = product if k == 0 else out[:half, :] + product
+    out[:half, :] = lax.dot_general(
+        slopes[:, side * half : (side + 1) * half],
+        rows[...],
+        (((0,), (0,)), ((), ())),
+        preferred_element_type=jnp.float32,
+    )
     if side:
         out[half:, :] = totals[...]
 
@@ -113,8 +116,9 @@
     return pl.pallas_call(
         slopes_kernel,
         in_specs=[SMEM, SMEM, VMEM, VMEM, VMEM, VMEM],
-        out_specs=[VMEM, VMEM],
+        out_specs=[VMEM, VMEM, VMEM],
         out_shape=(
+            jax.ShapeDtypeStruct((rows.shape[0], wide), jnp.bfloat16),
             jax.ShapeDtypeStruct((rows.shape[0], wide), jnp.bfloat16),
             jax.ShapeDtypeStruct((8, width), jnp.float32),
         ),
@@ -135,6 +139,23 @@
         cost_estimate=pl.CostEstimate(flops=5 * 10**8, bytes_accessed=4 * 10**6, transcendentals=0),
         name="text_products_%d" % side,
     )(place, rows, slopes, totals)
+
+
+def copies_kernel(block, out):
+    for i in range(out.shape[0]):
+        out[i] = block[...]
+
+
+def copies_of(block, count):
+    return pl.pallas_call(
+        copies_kernel,
+        in_specs=[VMEM],
+        out_specs=VMEM,
+        out_shape=jax.ShapeDtypeStruct((count,) + block.shape, block.dtype),
+        compiler_params=pltpu.CompilerParams(vmem_limit_bytes=8 * 2**20),
+        cost_estimate=pl.CostEstimate(flops=0, bytes_accessed=2 * 10**6, transcendentals=0),
+        name="copies",
+    )(block)
 
 
 def finish_kernel(last, scale, unit, radius, accum, sums, grad, loss, scale_grad, bias_grad):
@@ -190,7 +211,7 @@
     own = swap(copies, "y").reshape(-1, width)
     cols = (uyb[0].astype(jnp.float32) * UNIT).astype(jnp.float16)
     own, cols = lax.optimization_barrier((own, cols))
-    rows = spread(own, "x").reshape(-1, width)
+    rows = swap(copies_of(own, lax.axis_size("x")), "x").reshape(-1, width)
     cols = lax.all_gather(cols, Z + ("core",), axis=0, tiled=True)
     cols = (cols.astype(jnp.float32) * (1 / UNIT)).astype(jnp.bfloat16)
     cols = cols.reshape(8, 2, txt_rows, width)
@@ -214,15 +235,15 @@
     half = cols.shape[0] // 2
     high = rows.shape[0] // 4
     place = x.reshape(1).astype(jnp.int32)
-    near, totals = slopes_of(place, jnp.stack([scale, bias[0]]), rows, cols, row_ids, col_ids)
+    near, whole, totals = slopes_of(place, jnp.stack([scale, bias[0]]), rows, cols, row_ids, col_ids)
 
     back = {}
     for k in (2, 1, 3, 0):
         drows = 64.0 * jnp.dot(near[k * high : (k + 1) * high], cols, preferred_element_type=jnp.float32)
         back[k] = drows.astype(jnp.float16) if k else drows
 
-    got = shifted(text_products(1, place, rows, near, totals), "core", 1)
-    mine = text_products(0, place, rows, near, totals)
+    got = shifted(text_products(1, place, rows, whole, totals), "core", 1)
+    mine = text_products(0, place, rows, whole, totals)
     dcols = ((got[:half] + mine) * 32.0).astype(jnp.float16).reshape(8, txt_rows, width)
     dcols, back[1], back[2], back[3] = lax.optimization_barrier((dcols, back[1], back[2], back[3]))
     dcols, stats = swap_sum(dcols, got[half : half + 1, :128] + totals[:1, :128], Z, 128.0)

time: 125 us -> 125 us (level)
    broadcast_in_dim x2 -> x1, local copies, waits for them, and re-layouts: 1.95 us -> 0.58 us  [spread(): return swap(jnp.broadcast_to(block[None], (count,) + block.shape), axis)]
    unnamed x8 -> x10, local copies, waits for them, and re-layouts: 1.7 us -> 2.92 us
where the time goes in v13:
time: 125 us; the launch traced here: 124 us
  starting transfers between devices  37.5 us (30%)
  waiting for transfers between devices  37.3 us (30%)
  blocking collectives  27.4 us (22%)
  Pallas kernels  6.61 us (5%)
  local copies, waits for them, and re-layouts  5.77 us (5%)
  other arithmetic  3.95 us (3%)
  matrix products  3.16 us (3%)
  between operations  2.27 us (2%)
    all_to_all x5, waiting for transfers between devices, swap(): return lax.all_to_all(value, axis, 0, 0, tiled=False)  35.4 us
    all_gather x1, blocking collectives, body(): cols = lax.all_gather(cols, Z + ('core',), axis=0, tiled=True)  27.4 us
    all_to_all x5, starting transfers between devices, swap(): return lax.all_to_all(value, axis, 0, 0, tiled=False)  27.1 us
    ppermute x4, starting transfers between devices, shifted(): lax.ppermute(value, axis, [(i, (i + steps) % count) for i in range(count)])  10.5 us
    pallas_call x1, Pallas kernels, slopes_of(): pl.pallas_call(slopes_kernel, in_specs=[SMEM, SMEM, VMEM, VMEM, VMEM, VME...  3.24 us
    dot_general x4, matrix products, body(): jnp.dot(near[k * high:(k + 1) * high], cols, preferred_element_type=jnp.f...  3.16 us
    unnamed x10, local copies, waits for them, and re-layouts  2.92 us
  transfers between devices with their start and end apart: 9, of which 6 were waited for; matrix products, arithmetic and copies ran while one was open for 6% of the time, Pallas kernels for 1%

profile of v13, /device:TPU:1, one launch (start us, length us, event | category | flops | bytes accessed | tf_op | source)
XLA Modules:
  0.0 124.0 jit_solution(9373893661277272197)
XLA Ops:
  0.6 0.8 copy-done.3
  1.4 0.9 normalize_8.1
  2.3 7.7 %all-to-all-start = ((bf16[8,24,1152]{2,1,0:T(8,128)(2,1)}), bf16[8,24,1152]{2,1,0:T(8,128)(2,1)S(1)}, u32[]{:S(2)}, u32[]{:S(2)}) async-start(bf16[8,24,1152]{2,1,0:T(8,128)(2,1)} %get-tuple-element.26), calls=%async_computation | async-start | bytes 884736 | tf_op jit(solution)/shard_map/all_to_all | solution.py:51
  11.3 0.9 copy-done.2
  12.3 1.2 reshape.181
  14.5 8.2 %all-to-all-done = bf16[8,24,1152]{2,1,0:T(8,128)(2,1)S(1)} async-done(((bf16[8,24,1152]{2,1,0:T(8,128)(2,1)}), bf16[8,24,1152]{2,1,0:T(8,128)(2,1)S(1)}, u32[]{:S(2)}, u32[]{:S(2)}) %all-to-all-start) | async-done | bytes 442400 | tf_op jit(solution)/shard_map/all_to_all | solution.py:51
  22.8 1.2 copy-done
  24.1 7.1 %all-to-all-start.1 = ((bf16[4,192,1152]{2,1,0:T(8,128)(2,1)}), bf16[4,192,1152]{2,1,0:T(8,128)(2,1)S(1)}, u32[]{:S(2)}, u32[]{:S(2)}) async-start(bf16[4,192,1152]{2,1,0:T(8,128)(2,1)} %copy-done), calls=%async_computation.1 | async-start | bytes 3538944 | tf_op jit(solution)/shard_map/all_to_all | solution.py:51
  31.2 27.4 %all-gather.1 = f16[512,1152]{1,0:T(8,128)(2,1)S(1)} all-gather(f16[32,1152]{1,0:T(8,128)(2,1)S(1)} %fusion.9), channel_id=1, replica_groups=mesh['y'=8,'zh'=2,'zl'=4,'x'=4,'core'=2] {'zh','zl','core'}, dimensions={0}, use_global_device_ids=true | all-gather | bytes 1253376 | tf_op jit(solution)/shard_map/all_gather | solution.py:215
  59.0 3.2 %slopes.1 = (bf16[768,512]{1,0:T(8,128)(2,1)S(1)}, bf16[768,512]{1,0:T(8,128)(2,1)S(1)}, f32[8,1152]{1,0:T(8,128)S(1)}) custom-call(s32[1]{0:T(128)} %bitcast.place, f32[2]{0:T(128)S(1)} %pad_maximum_fusion.3.scalars, bf16[768,1152]{1,0:T(8,128)(2,1)S(1)} %bitcast.43, bf16[512,1152]{1,0:T(8,128)(2,1)S(1)} %bitcast.38, ...), custom_call_target="tpu_custom_call" | custom-call | flops 1000000000 | bytes 4000000 | tf_op jit(solution)/shard_map/slopes/pallas_call | solution.py:116
  63.0 2.1 %collective-permute-start = (f32[264,1152]{1,0:T(8,128)S(1)}, f32[264,1152]{1,0:T(8,128)S(1)}, u32[]{:S(2)}, u32[]{:S(2)}) collective-permute-start(f32[264,1152]{1,0:T(8,128)S(1)} %text_products_1.1), channel_id=1, source_target_pairs={{0,1},{1,0},{2,3},{3,2},{4,5},{5,4},{6,7},{7,6},{8,9},{9,8},{10,11... | collective-permute-start | bytes 3649544 | tf_op jit(solution)/shard_map/ppermute | solution.py:56
  68.1 1.0 pad_maximum_fusion.1
  69.1 5.6 %all-to-all-start.2 = ((f16[8,32,1280]{2,1,0:T(8,128)(2,1)}), f16[8,32,1280]{2,1,0:T(8,128)(2,1)S(1)}, u32[]{:S(2)}, u32[]{:S(2)}) async-start(f16[8,32,1280]{2,1,0:T(8,128)(2,1)} %pad_maximum_fusion.1), calls=%async_computation.2 | async-start | bytes 1310720 | tf_op jit(solution)/shard_map/all_to_all | solution.py:51
  74.7 2.8 %collective-permute-start.3 = (f16[192,1152]{1,0:T(8,128)(2,1)S(1)}, f16[192,1152]{1,0:T(8,128)(2,1)}, u32[]{:S(2)}, u32[]{:S(2)}) collective-permute-start(f16[192,1152]{1,0:T(8,128)(2,1)S(1)} %fusion.2), channel_id=1, source_target_pairs={{0,6},{2,0},{4,2},{6,4},{1,7},{3,1},{5,3},{7,5},{8,14},{10,8},{12,... | collective-permute-start | bytes 1327112 | tf_op jit(solution)/shard_map/ppermute | solution.py:56
  77.6 2.4 %collective-permute-start.2 = (f16[192,1152]{1,0:T(8,128)(2,1)S(1)}, f16[192,1152]{1,0:T(8,128)(2,1)}, u32[]{:S(2)}, u32[]{:S(2)}) collective-permute-start(f16[192,1152]{1,0:T(8,128)(2,1)S(1)} %fusion), channel_id=1, source_target_pairs={{0,2},{2,4},{4,6},{6,0},{1,3},{3,5},{5,7},{7,1},{8,10},{10,12},{12... | collective-permute-start | bytes 1327112 | tf_op jit(solution)/shard_map/ppermute | solution.py:56
  80.0 3.1 %collective-permute-start.1 = (f16[192,1152]{1,0:T(8,128)(2,1)S(1)}, f16[192,1152]{1,0:T(8,128)(2,1)}, u32[]{:S(2)}, u32[]{:S(2)}) collective-permute-start(f16[192,1152]{1,0:T(8,128)(2,1)S(1)} %fusion.1), channel_id=1, source_target_pairs={{0,4},{2,6},{4,0},{6,2},{1,5},{3,7},{5,1},{7,3},{8,12},{10,14},{12... | collective-permute-start | bytes 1327112 | tf_op jit(solution)/shard_map/ppermute | solution.py:56
  83.3 12.2 %all-to-all-done.2 = f16[8,32,1280]{2,1,0:T(8,128)(2,1)S(1)} async-done(((f16[8,32,1280]{2,1,0:T(8,128)(2,1)}), f16[8,32,1280]{2,1,0:T(8,128)(2,1)S(1)}, u32[]{:S(2)}, u32[]{:S(2)}) %all-to-all-start.2) | async-done | bytes 655392 | tf_op jit(solution)/shard_map/all_to_all | solution.py:51
  96.1 3.2 %all-to-all-start.3 = ((f32[4,1,128]{2,1,0:T(1,128)}), f32[4,1,128]{2,1,0:T(1,128)S(1)}, u32[]{:S(2)}, u32[]{:S(2)}) async-start(f32[4,1,128]{2,1,0:T(1,128)} %broadcast_in_dim.15), calls=%async_computation.3 | async-start | bytes 4096 | tf_op jit(solution)/shard_map/all_to_all | solution.py:51
  99.4 1.3 %collective-permute-done.1 = f16[192,1152]{1,0:T(8,128)(2,1)} collective-permute-done((f16[192,1152]{1,0:T(8,128)(2,1)S(1)}, f16[192,1152]{1,0:T(8,128)(2,1)}, u32[]{:S(2)}, u32[]{:S(2)}) %collective-permute-start.1) | collective-permute-done | bytes 442400 | tf_op jit(solution)/shard_map/ppermute | solution.py:56
  100.7 1.9 %multiply_convert_fusion.1 = f16[192,1152]{1,0:T(8,128)(2,1)S(1)} fusion(f16[192,1152]{1,0:T(8,128)(2,1)} %collective-permute-done.3, f16[192,1152]{1,0:T(8,128)(2,1)} %collective-permute-done.2, f16[192,1152]{1,0:T(8,128)(2,1)} %collective-permute-done.1, bf16[512,1152]{1,0:T(8,128)(2,1)S(1)} %bitcast.42, bf16[768,512]{1,0:T(8,128)(2,1)} %copy-done.1), kind=kOutput, calls=%fused_computation.14 | convolution fusion | flops 228483072 | bytes 3145728 | tf_op jit(solution)/shard_map/dot_general | solution.py:242
  102.6 0.8 all-to-all-done.3
  103.5 0.9 pad_maximum_fusion.2
  104.4 3.5 %all-to-all-start.4 = ((f16[8,24,1280]{2,1,0:T(8,128)(2,1)}), f16[8,24,1280]{2,1,0:T(8,128)(2,1)S(1)}, u32[]{:S(2)}, u32[]{:S(2)}) async-start(f16[8,24,1280]{2,1,0:T(8,128)(2,1)} %pad_maximum_fusion.2), calls=%async_computation.4 | async-start | bytes 983040 | tf_op jit(solution)/shard_map/all_to_all | solution.py:51
  109.0 14.2 %all-to-all-done.4 = f16[8,24,1280]{2,1,0:T(8,128)(2,1)S(1)} async-done(((f16[8,24,1280]{2,1,0:T(8,128)(2,1)}), f16[8,24,1280]{2,1,0:T(8,128)(2,1)S(1)}, u32[]{:S(2)}, u32[]{:S(2)}) %all-to-all-start.4) | async-done | bytes 491552 | tf_op jit(solution)/shard_map/all_to_all | solution.py:51
  (58 shorter events, 8.0 us)
Async XLA Ops:
  0.6 0.8 copy-start.3
  1.4 12.4 %copy-start.4 = (s32[16384]{0:T(1024)S(1)}, s32[16384]{0:T(1024)}, u32[]{:S(2)}) copy-start(s32[16384]{0:T(1024)} %param.9) | copy-start | bytes 196612
  2.3 20.4 %all-to-all-start = ((bf16[8,24,1152]{2,1,0:T(8,128)(2,1)}), bf16[8,24,1152]{2,1,0:T(8,128)(2,1)S(1)}, u32[]{:S(2)}, u32[]{:S(2)}) async-start(bf16[8,24,1152]{2,1,0:T(8,128)(2,1)} %get-tuple-element.26), calls=%async_computation | async-start | bytes 884736 | tf_op jit(solution)/shard_map/all_to_all | solution.py:51
  11.3 0.9 copy-start.2
  22.8 1.2 copy-start
  24.1 35.0 %all-to-all-start.1 = ((bf16[4,192,1152]{2,1,0:T(8,128)(2,1)}), bf16[4,192,1152]{2,1,0:T(8,128)(2,1)S(1)}, u32[]{:S(2)}, u32[]{:S(2)}) async-start(bf16[4,192,1152]{2,1,0:T(8,128)(2,1)} %copy-done), calls=%async_computation.1 | async-start | bytes 3538944 | tf_op jit(solution)/shard_map/all_to_all | solution.py:51
  62.3 4.5 %copy-start.1 = (bf16[768,512]{1,0:T(8,128)(2,1)}, bf16[768,512]{1,0:T(8,128)(2,1)S(1)}, u32[]{:S(2)}) copy-start(bf16[768,512]{1,0:T(8,128)(2,1)S(1)} %get-tuple-element.32) | copy-start | bytes 2359300
  63.0 4.8 %collective-permute-start = (f32[264,1152]{1,0:T(8,128)S(1)}, f32[264,1152]{1,0:T(8,128)S(1)}, u32[]{:S(2)}, u32[]{:S(2)}) collective-permute-start(f32[264,1152]{1,0:T(8,128)S(1)} %text_products_1.1), channel_id=1, source_target_pairs={{0,1},{1,0},{2,3},{3,2},{4,5},{5,4},{6,7},{7,6},{8,9},{9,8},{10,11... | collective-permute-start | bytes 3649544 | tf_op jit(solution)/shard_map/ppermute | solution.py:56
  69.1 26.4 %all-to-all-start.2 = ((f16[8,32,1280]{2,1,0:T(8,128)(2,1)}), f16[8,32,1280]{2,1,0:T(8,128)(2,1)S(1)}, u32[]{:S(2)}, u32[]{:S(2)}) async-start(f16[8,32,1280]{2,1,0:T(8,128)(2,1)} %pad_maximum_fusion.1), calls=%async_computation.2 | async-start | bytes 1310720 | tf_op jit(solution)/shard_map/all_to_all | solution.py:51
  74.7 24.6 %collective-permute-start.3 = (f16[192,1152]{1,0:T(8,128)(2,1)S(1)}, f16[192,1152]{1,0:T(8,128)(2,1)}, u32[]{:S(2)}, u32[]{:S(2)}) collective-permute-start(f16[192,1152]{1,0:T(8,128)(2,1)S(1)} %fusion.2), channel_id=1, source_target_pairs={{0,6},{2,0},{4,2},{6,4},{1,7},{3,1},{5,3},{7,5},{8,14},{10,8},{12,... | collective-permute-start | bytes 1327112 | tf_op jit(solution)/shard_map/ppermute | solution.py:56
  77.6 21.8 %collective-permute-start.2 = (f16[192,1152]{1,0:T(8,128)(2,1)S(1)}, f16[192,1152]{1,0:T(8,128)(2,1)}, u32[]{:S(2)}, u32[]{:S(2)}) collective-permute-start(f16[192,1152]{1,0:T(8,128)(2,1)S(1)} %fusion), channel_id=1, source_target_pairs={{0,2},{2,4},{4,6},{6,0},{1,3},{3,5},{5,7},{7,1},{8,10},{10,12},{12... | collective-permute-start | bytes 1327112 | tf_op jit(solution)/shard_map/ppermute | solution.py:56
  80.0 20.7 %collective-permute-start.1 = (f16[192,1152]{1,0:T(8,128)(2,1)S(1)}, f16[192,1152]{1,0:T(8,128)(2,1)}, u32[]{:S(2)}, u32[]{:S(2)}) collective-permute-start(f16[192,1152]{1,0:T(8,128)(2,1)S(1)} %fusion.1), channel_id=1, source_target_pairs={{0,4},{2,6},{4,0},{6,2},{1,5},{3,7},{5,1},{7,3},{8,12},{10,14},{12... | collective-permute-start | bytes 1327112 | tf_op jit(solution)/shard_map/ppermute | solution.py:56
  96.1 7.2 %all-to-all-start.3 = ((f32[4,1,128]{2,1,0:T(1,128)}), f32[4,1,128]{2,1,0:T(1,128)S(1)}, u32[]{:S(2)}, u32[]{:S(2)}) async-start(f32[4,1,128]{2,1,0:T(1,128)} %broadcast_in_dim.15), calls=%async_computation.3 | async-start | bytes 4096 | tf_op jit(solution)/shard_map/all_to_all | solution.py:51
  104.4 18.7 %all-to-all-start.4 = ((f16[8,24,1280]{2,1,0:T(8,128)(2,1)}), f16[8,24,1280]{2,1,0:T(8,128)(2,1)S(1)}, u32[]{:S(2)}, u32[]{:S(2)}) async-start(f16[8,24,1280]{2,1,0:T(8,128)(2,1)} %pad_maximum_fusion.2), calls=%async_computation.4 | async-start | bytes 983040 | tf_op jit(solution)/shard_map/all_to_all | solution.py:51
